TPU v7x, 32 devices: a whole 2x2x4 slice. The times are simulated.
32 devices in a mesh: dev: 32 (over z, y, x, core).
Axes of the slice: x: 2, y: 2, z: 4, core: 2. Of those that a mesh axis runs over, the one named last changes fastest.
Arguments:
- tokens: bfloat16 [16384, 1024], P('dev'), may hold values from -6 to 6
- cotangent: bfloat16 [16384, 1024], P('dev'), may hold values from -6 to 6
- segment_ids: int32 [16384], P('dev'), may hold values from 0 to 14, never falling along the last dimension, each value on 1 to 1370 neighbouring positions
- validity: int32 [16384], P('dev'), may hold values 0 or 1
- first_gain: bfloat16 [1024], P('dev'), may hold values from 0.099609375 to 1.8984375
- first_bias: bfloat16 [1024], P('dev'), may hold values from -4 to 4
- query_weight: bfloat16 [1024, 1024], P('dev'), may hold values from -0.25 to 0.25
- query_bias: bfloat16 [1024], P('dev'), may hold values from -4 to 4
- key_weight: bfloat16 [1024, 1024], P('dev'), may hold values from -0.25 to 0.25
- value_weight: bfloat16 [1024, 1024], P('dev'), may hold values from -0.1875 to 0.1875
- value_bias: bfloat16 [1024], P('dev'), may hold values from -4 to 4
- output_weight: bfloat16 [1024, 1024], P('dev'), may hold values from -0.75 to 0.75
- output_bias: bfloat16 [1024], P('dev'), may hold values from -4 to 4
- attention_scale: bfloat16 [1024], P('dev'), may hold values from 0.5 to 2
- second_gain: bfloat16 [1024], P('dev'), may hold values from 0.099609375 to 1.8984375
- second_bias: bfloat16 [1024], P('dev'), may hold values from -4 to 4
- hidden_weight: bfloat16 [1024, 4096], P('dev'), may hold values from -0.1875 to 0.1875
- hidden_bias: bfloat16 [4096], P('dev'), may hold values from -4 to 4
- project_weight: bfloat16 [4096, 1024], P('dev'), may hold values from -0.09375 to 0.09375
- project_bias: bfloat16 [1024], P('dev'), may hold values from -4 to 4
- dense_scale: bfloat16 [1024], P('dev'), may hold values from 0.5 to 2
Outputs:
- layer_output: bfloat16 [16384, 1024], P('dev')
- input_gradient: float32 [16384, 1024], P('dev')
- first_gain_grad: float32 [1024], P('dev')
- first_bias_grad: float32 [1024], P('dev')
- query_weight_grad: float32 [1024, 1024], P('dev')
- query_bias_grad: float32 [1024], P('dev')
- key_weight_grad: float32 [1024, 1024], P('dev')
- value_weight_grad: float32 [1024, 1024], P('dev')
- value_bias_grad: float32 [1024], P('dev')
- output_weight_grad: float32 [1024, 1024], P('dev')
- output_bias_grad: float32 [1024], P('dev')
- attention_scale_grad: float32 [1024], P('dev')
- second_gain_grad: float32 [1024], P('dev')
- second_bias_grad: float32 [1024], P('dev')
- hidden_weight_grad: float32 [1024, 4096], P('dev')
- hidden_bias_grad: float32 [4096], P('dev')
- project_weight_grad: float32 [4096, 1024], P('dev')
- project_bias_grad: float32 [1024], P('dev')
- dense_scale_grad: float32 [1024], P('dev')
Inputs may be any that keep to these rules, and one draw needn't show every extreme that they name: `segment_ids`: never falls along the rows; each of the 15 images takes 1 to 1370 consecutive rows, and one takes exactly 1370.
All inputs are finite; a program needn't handle non-finite values. No bound on the sum of `validity` on one device may be relied on, other than what follows from the above.
Results may differ from a plain program's by a relative error of at most 0.013.
The roundings to bfloat16 on the way count: a program that leaves them out, or rounds other values in their place, can miss the bound.
Values may be sent and summed in bfloat16 or wider, within the bound.
No kernel may reach another device: no remote copies, remote signals or barrier semaphores. Data moves between devices by JAX's collectives and lax.ppermute only.
A program may use at most 192 MiB of HBM per device.

v0:
```python
import jax
import jax.numpy as jnp
from jax import lax
from jax.sharding import PartitionSpec as P

HEAD_DIM = 64
IMG = 1370


norm_eps = 1e-06


def passed_along(block, axis, distance):
    devices = range(lax.axis_size(axis))
    route = [(i - distance, i) for i in devices if i - distance in devices]
    return lax.ppermute(block, axis, route)


def layer_norm(row_values, gain_row, bias_row):
    center = row_values - jnp.mean(row_values, axis=-1, keepdims=True)
    spread = jnp.mean(center * center, axis=-1, keepdims=True)
    return center * lax.rsqrt(spread + norm_eps) * gain_row + bias_row


def gelu_exact(arguments):
    return jax.nn.gelu(arguments, approximate=False)


def product(left_rows, right_rows):
    return jnp.dot(left_rows, right_rows, preferred_element_type=jnp.float32)


def inner_rows(left_rows, right_rows):
    return lax.dot_general(
        left_rows, right_rows, (((0,), (0,)), ((), ())), preferred_element_type=jnp.float32
    )


def against(left_rows, right_rows):
    return lax.dot_general(
        left_rows, right_rows, (((1,), (1,)), ((), ())), preferred_element_type=jnp.float32
    )


def column_sums(matrix_rows):
    return jnp.sum(matrix_rows.astype(jnp.float32), axis=0)


def on_device(
    tokens,
    cotangent,
    segment_ids,
    validity,
    first_gain,
    first_bias,
    query_weight,
    query_bias,
    key_weight,
    value_weight,
    value_bias,
    output_weight,
    output_bias,
    attention_scale,
    second_gain,
    second_bias,
    hidden_weight,
    hidden_bias,
    project_weight,
    project_bias,
    dense_scale,
):
    row_count = tokens.shape[0]
    reach_count = (IMG + row_count - 2) // row_count
    window_width = (2 * reach_count + 1) * row_count
    pair_width = 2 * HEAD_DIM
    score_scale = HEAD_DIM ** (-0.5)
    attention_full = (
        lax.all_gather(first_gain, "dev", axis=0, tiled=True),
        lax.all_gather(first_bias, "dev", axis=0, tiled=True),
        lax.all_gather(query_weight, "dev", axis=0, tiled=True),
        lax.all_gather(query_bias, "dev", axis=0, tiled=True),
        lax.all_gather(key_weight, "dev", axis=0, tiled=True),
        lax.all_gather(value_weight, "dev", axis=0, tiled=True),
        lax.all_gather(value_bias, "dev", axis=0, tiled=True),
        lax.all_gather(output_weight, "dev", axis=0, tiled=True),
        lax.all_gather(output_bias, "dev", axis=0, tiled=True),
        lax.all_gather(attention_scale, "dev", axis=0, tiled=True),
    )
    (
        gain_first,
        bias_first,
        weight_query,
        bias_query,
        weight_key,
        weight_value,
        bias_value,
        weight_output,
        bias_output,
        scale_first,
    ) = attention_full
    inputs = tokens.astype(jnp.float32)
    normed, first_norm_back = jax.vjp(
        layer_norm, inputs, gain_first.astype(jnp.float32), bias_first.astype(jnp.float32)
    )
    normed_low = normed.astype(jnp.bfloat16)
    queries = (product(normed_low, weight_query) + bias_query.astype(jnp.float32)).astype(
        jnp.bfloat16
    )
    key_rows = product(normed_low, weight_key).astype(jnp.bfloat16)
    value_rows = (product(normed_low, weight_value) + bias_value.astype(jnp.float32)).astype(
        jnp.bfloat16
    )
    query_label = segment_ids + 1
    own_label = jnp.where(validity == 1, segment_ids + 1, 0)
    own_tags = jnp.stack([own_label, query_label])
    own_pairs = jnp.stack([key_rows, value_rows])
    below_pairs = []
    below_labels = []
    moving_pairs = own_pairs
    moving_labels = own_tags
    for offset in range(reach_count):
        moving_pairs = passed_along(moving_pairs, "dev", 1)
        moving_labels = passed_along(moving_labels, "dev", 1)
        below_pairs.insert(0, moving_pairs)
        below_labels.insert(0, moving_labels)
    above_pairs = []
    above_labels = []
    moving_pairs = own_pairs
    moving_labels = own_tags
    for offset in range(reach_count):
        moving_pairs = passed_along(moving_pairs, "dev", -1)
        moving_labels = passed_along(moving_labels, "dev", -1)
        above_pairs.append(moving_pairs)
        above_labels.append(moving_labels)
    window_pairs = jnp.concatenate(below_pairs + [own_pairs] + above_pairs, axis=1)
    window_tags = jnp.concatenate(below_labels + [own_tags] + above_labels, axis=1)
    window_label = window_tags[0]
    row_index = lax.broadcasted_iota(jnp.int32, (row_count, window_width), 0)
    col_index = lax.broadcasted_iota(jnp.int32, (row_count, window_width), 1)
    allowed = (query_label[:, None] == window_label[None, :]) | (
        col_index == row_index + reach_count * row_count
    )

    def pair_inputs(pair_index):
        column_start = pair_index * pair_width
        query_pair = lax.dynamic_slice_in_dim(queries, column_start, pair_width, 1).reshape(
            row_count, 2, HEAD_DIM
        )
        both_pairs = lax.dynamic_slice_in_dim(window_pairs, column_start, pair_width, 2)
        key_pair = both_pairs[0].reshape(window_width, 2, HEAD_DIM)
        value_pair = both_pairs[1].reshape(window_width, 2, HEAD_DIM)
        scores = (
            jnp.einsum("qhd,khd->hqk", query_pair, key_pair, preferred_element_type=jnp.float32)
            * score_scale
        )
        scores = jnp.where(allowed[None], scores, -1e30)
        return (column_start, query_pair, key_pair, value_pair, scores)

    def attend_pair(pair_index, carried):
        attended, log_totals = carried
        column_start, query_pair, key_pair, value_pair, scores = pair_inputs(pair_index)
        row_peak = jnp.max(scores, axis=-1, keepdims=True)
        exponent = jnp.exp(scores - row_peak)
        row_total = jnp.sum(exponent, axis=-1, keepdims=True)
        weights_low = (exponent / row_total).astype(jnp.bfloat16)
        outputs = jnp.einsum(
            "hqk,khd->qhd", weights_low, value_pair, preferred_element_type=jnp.float32
        ).reshape(row_count, pair_width)
        attended = lax.dynamic_update_slice_in_dim(attended, outputs, column_start, 1)
        log_totals = lax.dynamic_update_slice_in_dim(
            log_totals, (row_peak + jnp.log(row_total))[:, :, 0], pair_index * 2, 0
        )
        return (attended, log_totals)

    pair_count = queries.shape[1] // pair_width
    attended, log_totals = lax.fori_loop(
        0,
        pair_count,
        attend_pair,
        (
            jnp.zeros((row_count, queries.shape[1]), jnp.float32),
            jnp.zeros((2 * pair_count, row_count), jnp.float32),
        ),
    )
    attended_low = attended.astype(jnp.bfloat16)
    branch = product(attended_low, weight_output) + bias_output.astype(jnp.float32)
    middle = inputs + scale_first.astype(jnp.float32) * branch
    dense_full = (
        lax.all_gather(second_gain, "dev", axis=0, tiled=True),
        lax.all_gather(second_bias, "dev", axis=0, tiled=True),
        lax.all_gather(hidden_weight, "dev", axis=0, tiled=True),
        lax.all_gather(hidden_bias, "dev", axis=0, tiled=True),
        lax.all_gather(project_weight, "dev", axis=0, tiled=True),
        lax.all_gather(project_bias, "dev", axis=0, tiled=True),
        lax.all_gather(dense_scale, "dev", axis=0, tiled=True),
    )
    (
        gain_second,
        bias_second,
        weight_hidden,
        bias_hidden,
        weight_project,
        bias_project,
        scale_second,
    ) = dense_full
    normed_two, second_norm_back = jax.vjp(
        layer_norm, middle, gain_second.astype(jnp.float32), bias_second.astype(jnp.float32)
    )
    normed_two_low = normed_two.astype(jnp.bfloat16)
    hidden = product(normed_two_low, weight_hidden) + bias_hidden.astype(jnp.float32)
    active, gelu_back = jax.vjp(gelu_exact, hidden)
    active_low = active.astype(jnp.bfloat16)
    dense_out = product(active_low, weight_project) + bias_project.astype(jnp.float32)
    layer_output = (middle + scale_second.astype(jnp.float32) * dense_out).astype(jnp.bfloat16)
    attention_back = (
        lax.all_gather(first_gain, "dev", axis=0, tiled=True),
        lax.all_gather(first_bias, "dev", axis=0, tiled=True),
        lax.all_gather(query_weight, "dev", axis=0, tiled=True),
        lax.all_gather(query_bias, "dev", axis=0, tiled=True),
        lax.all_gather(key_weight, "dev", axis=0, tiled=True),
        lax.all_gather(value_weight, "dev", axis=0, tiled=True),
        lax.all_gather(value_bias, "dev", axis=0, tiled=True),
        lax.all_gather(output_weight, "dev", axis=0, tiled=True),
        lax.all_gather(output_bias, "dev", axis=0, tiled=True),
        lax.all_gather(attention_scale, "dev", axis=0, tiled=True),
    )
    dense_back = (
        lax.all_gather(second_gain, "dev", axis=0, tiled=True),
        lax.all_gather(second_bias, "dev", axis=0, tiled=True),
        lax.all_gather(hidden_weight, "dev", axis=0, tiled=True),
        lax.all_gather(hidden_bias, "dev", axis=0, tiled=True),
        lax.all_gather(project_weight, "dev", axis=0, tiled=True),
        lax.all_gather(project_bias, "dev", axis=0, tiled=True),
        lax.all_gather(dense_scale, "dev", axis=0, tiled=True),
    )
    back_query, back_key, back_value, back_output, back_scale_first = (
        attention_back[2],
        attention_back[4],
        attention_back[5],
        attention_back[7],
        attention_back[9],
    )
    back_hidden, back_project, back_scale_second = (dense_back[2], dense_back[4], dense_back[6])
    upstream = cotangent.astype(jnp.float32)
    dense_scale_grad = jnp.sum(upstream * dense_out, axis=0)
    grad_dense = (upstream * back_scale_second.astype(jnp.float32)).astype(jnp.bfloat16)
    project_weight_grad = inner_rows(active_low, grad_dense)
    project_bias_grad = column_sums(grad_dense)
    grad_active = against(grad_dense, back_project)
    grad_hidden = gelu_back(grad_active)[0].astype(jnp.bfloat16)
    hidden_weight_grad = inner_rows(normed_two_low, grad_hidden)
    hidden_bias_grad = column_sums(grad_hidden)
    grad_middle_norm, second_gain_grad, second_bias_grad = second_norm_back(
        against(grad_hidden, back_hidden)
    )
    grad_middle = upstream + grad_middle_norm
    dense_gradients = (
        lax.psum_scatter(second_gain_grad, "dev", scatter_dimension=0, tiled=True),
        lax.psum_scatter(second_bias_grad, "dev", scatter_dimension=0, tiled=True),
        lax.psum_scatter(hidden_weight_grad, "dev", scatter_dimension=0, tiled=True),
        lax.psum_scatter(hidden_bias_grad, "dev", scatter_dimension=0, tiled=True),
        lax.psum_scatter(project_weight_grad, "dev", scatter_dimension=0, tiled=True),
        lax.psum_scatter(project_bias_grad, "dev", scatter_dimension=0, tiled=True),
        lax.psum_scatter(dense_scale_grad, "dev", scatter_dimension=0, tiled=True),
    )
    attention_scale_grad = jnp.sum(grad_middle * branch, axis=0)
    grad_branch = (grad_middle * back_scale_first.astype(jnp.float32)).astype(jnp.bfloat16)
    output_weight_grad = inner_rows(attended_low, grad_branch)
    output_bias_grad = column_sums(grad_branch)
    grad_attended = against(grad_branch, back_output).astype(jnp.bfloat16)

    def pair_core(pair_index):
        column_start, query_pair, key_pair, value_pair, scores = pair_inputs(pair_index)
        log_pair = lax.dynamic_slice_in_dim(log_totals, pair_index * 2, 2, 0)
        weights = jnp.exp(scores - log_pair[:, :, None])
        grad_pair = lax.dynamic_slice_in_dim(grad_attended, column_start, pair_width, 1).reshape(
            row_count, 2, HEAD_DIM
        )
        grad_probs = jnp.einsum(
            "qhd,khd->hqk", grad_pair, value_pair, preferred_element_type=jnp.float32
        )
        inner_sum = jnp.sum(grad_probs * weights, axis=-1, keepdims=True)
        grad_scores = (weights * (grad_probs - inner_sum)).astype(jnp.bfloat16)
        grad_query_pair = (
            jnp.einsum("hqk,khd->qhd", grad_scores, key_pair, preferred_element_type=jnp.float32)
            * score_scale
        )
        return (
            column_start,
            query_pair,
            grad_pair,
            weights,
            grad_scores,
            grad_query_pair,
            inner_sum,
        )

    def pair_backward(pair_index, carried):
        grad_queries, grad_window = carried
        column_start, query_pair, grad_pair, weights, grad_scores, grad_query_pair, inner_sum = (
            pair_core(pair_index)
        )
        grad_key_pair = (
            jnp.einsum("hqk,qhd->khd", grad_scores, query_pair, preferred_element_type=jnp.float32)
            * score_scale
        )
        grad_value_pair = jnp.einsum(
            "hqk,qhd->khd",
            weights.astype(jnp.bfloat16),
            grad_pair,
            preferred_element_type=jnp.float32,
        )
        grad_queries = lax.dynamic_update_slice_in_dim(
            grad_queries, grad_query_pair.reshape(row_count, pair_width), column_start, 1
        )
        window_update = jnp.stack(
            [
                grad_key_pair.reshape(window_width, pair_width),
                grad_value_pair.reshape(window_width, pair_width),
            ]
        )
        grad_window = lax.dynamic_update_slice_in_dim(grad_window, window_update, column_start, 2)
        return (grad_queries, grad_window)

    grad_queries, grad_window = lax.fori_loop(
        0,
        pair_count,
        pair_backward,
        (
            jnp.zeros((row_count, queries.shape[1]), jnp.float32),
            jnp.zeros((2, window_width, queries.shape[1]), jnp.float32),
        ),
    )

    def window_block(block_index):
        return grad_window[:, block_index * row_count : (block_index + 1) * row_count]

    falling = window_block(0)
    for offset in range(reach_count - 1, -1, -1):
        falling = passed_along(falling.astype(jnp.bfloat16), "dev", -1).astype(
            falling.dtype
        ) + window_block(reach_count - offset)
    rising = window_block(2 * reach_count)
    for offset in range(reach_count - 1, -1, -1):
        rising = passed_along(rising.astype(jnp.bfloat16), "dev", 1).astype(rising.dtype)
        if offset > 0:
            rising = rising + window_block(reach_count + offset)
    grad_own = falling + rising
    grad_keys_low = grad_own[0].astype(jnp.bfloat16)
    grad_values_low = grad_own[1].astype(jnp.bfloat16)
    grad_queries_low = grad_queries.astype(jnp.bfloat16)
    query_weight_grad = inner_rows(normed_low, grad_queries_low)
    query_bias_grad = column_sums(grad_queries_low)
    key_weight_grad = inner_rows(normed_low, grad_keys_low)
    value_weight_grad = inner_rows(normed_low, grad_values_low)
    value_bias_grad = column_sums(grad_values_low)
    grad_normed = (
        against(grad_queries_low, back_query)
        + against(grad_keys_low, back_key)
        + against(grad_values_low, back_value)
    )
    grad_input_norm, first_gain_grad, first_bias_grad = first_norm_back(grad_normed)
    input_gradient = grad_middle + grad_input_norm
    attention_gradients = (
        lax.psum_scatter(first_gain_grad, "dev", scatter_dimension=0, tiled=True),
        lax.psum_scatter(first_bias_grad, "dev", scatter_dimension=0, tiled=True),
        lax.psum_scatter(query_weight_grad, "dev", scatter_dimension=0, tiled=True),
        lax.psum_scatter(query_bias_grad, "dev", scatter_dimension=0, tiled=True),
        lax.psum_scatter(key_weight_grad, "dev", scatter_dimension=0, tiled=True),
        lax.psum_scatter(value_weight_grad, "dev", scatter_dimension=0, tiled=True),
        lax.psum_scatter(value_bias_grad, "dev", scatter_dimension=0, tiled=True),
        lax.psum_scatter(output_weight_grad, "dev", scatter_dimension=0, tiled=True),
        lax.psum_scatter(output_bias_grad, "dev", scatter_dimension=0, tiled=True),
        lax.psum_scatter(attention_scale_grad, "dev", scatter_dimension=0, tiled=True),
    )
    return (
        layer_output,
        input_gradient,
        attention_gradients[0],
        attention_gradients[1],
        attention_gradients[2],
        attention_gradients[3],
        attention_gradients[4],
        attention_gradients[5],
        attention_gradients[6],
        attention_gradients[7],
        attention_gradients[8],
        attention_gradients[9],
        dense_gradients[0],
        dense_gradients[1],
        dense_gradients[2],
        dense_gradients[3],
        dense_gradients[4],
        dense_gradients[5],
        dense_gradients[6],
    )


def solution(mesh):
    placed = (
        P("dev", None),
        P("dev", None),
        P("dev"),
        P("dev"),
        P("dev"),
        P("dev"),
        P("dev", None),
        P("dev"),
        P("dev", None),
        P("dev", None),
        P("dev"),
        P("dev", None),
        P("dev"),
        P("dev"),
        P("dev"),
        P("dev"),
        P("dev", None),
        P("dev"),
        P("dev", None),
        P("dev"),
        P("dev"),
    )
    return jax.shard_map(
        on_device,
        mesh=mesh,
        in_specs=placed,
        out_specs=(
            P("dev", None),
            P("dev", None),
            P("dev"),
            P("dev"),
            P("dev", None),
            P("dev"),
            P("dev", None),
            P("dev", None),
            P("dev"),
            P("dev", None),
            P("dev"),
            P("dev"),
            P("dev"),
            P("dev"),
            P("dev", None),
            P("dev"),
            P("dev", None),
            P("dev"),
            P("dev"),
        ),
        check_vma=False,
    )
```

profile of v0, /device:TPU:0, one launch (start us, length us, event | category | flops | bytes accessed | tf_op | source)
XLA Modules:
  0.0 1734.1 jit_solution(4417000328175401871)
XLA Ops:
  19.0 42.8 %all-reduce.22 = (bf16[1024]{0:T(1024)(128)(2,1)S(1)}, bf16[1024]{0:T(1024)(128)(2,1)S(1)}, bf16[1024]{0:T(1024)(128)(2,1)S(1)}, bf16[1024]{0:T(1024)(128)(2,1)S...) all-reduce(bf16[1024]{0:T(1024)(128)(2,1)S(1)} %dynamic-update-slic, ...), channel_id=1, replica_groups=mesh['dev'=32] {'dev'}, use_global_device_ids=true, to_apply=%add.3 | all-reduce | flops 10240 | bytes 40960
  63.8 6.7 all-gather.8.cloned.1.call-done
  73.4 55.2 %all-gather.10.cloned.1.call-done = bf16[1024,1024]{1,0:T(8,128)(2,1)} async-done(((bf16[32,1024]{1,0:T(8,128)(2,1)}), bf16[1024,1024]{1,0:T(8,128)(2,1)}) %all-gather.10.cloned.1.call-update) | async-done | bytes 2097168 | tf_op jit(solution)/shard_map/all_gather | solution.py:83
  139.7 52.2 %collective-permute-start.1 = (bf16[2,512,1024]{2,1,0:T(8,128)(2,1)S(1)}, bf16[2,512,1024]{2,1,0:T(8,128)(2,1)}, u32[]{:S(2)}, u32[]{:S(2)}) collective-permute-start(bf16[2,512,1024]{2,1,0:T(8,128)(2,1)S(1)} %collective-permute-done), channel_id=1, source_target_pairs={{0,1},{1,2},{2,3},{3,4},{4,5},{5,6},{6,7},{7,8},{8,9},{9,10},{10,1... | collective-permute-start | bytes 6291464 | tf_op jit(solution)/shard_map/ppermute | solution.py:16
  194.5 49.6 %collective-permute-start.2 = (bf16[2,512,1024]{2,1,0:T(8,128)(2,1)}, bf16[2,512,1024]{2,1,0:T(8,128)(2,1)}, u32[]{:S(2)}, u32[]{:S(2)}) collective-permute-start(bf16[2,512,1024]{2,1,0:T(8,128)(2,1)} %collective-permute-done.1), channel_id=1, source_target_pairs={{0,1},{1,2},{2,3},{3,4},{4,5},{5,6},{6,7},{7,8},{8,9},{9,10},{10,1... | collective-permute-start | bytes 6291464 | tf_op jit(solution)/shard_map/ppermute | solution.py:16
  248.7 25.5 %collective-permute-start.7 = (s32[2,512]{1,0:T(2,128)S(1)}, s32[2,512]{1,0:T(2,128)S(1)}, u32[]{:S(2)}, u32[]{:S(2)}) collective-permute-start(s32[2,512]{1,0:T(2,128)S(1)} %collective-permute-done.6), channel_id=1, source_target_pairs={{0,1},{1,2},{2,3},{3,4},{4,5},{5,6},{6,7},{7,8},{8,9},{9,10},{10,1... | collective-permute-start | bytes 12296 | tf_op jit(solution)/shard_map/ppermute | solution.py:16
  278.5 5.0 collective-permute-start.8
  283.5 37.9 %all-gather = bf16[32,1,128]{2,1,0:T(2,128)(2,1)S(1)} all-gather(bf16[1,1,128]{2,1,0:T(2,128)(2,1)S(1)} %bitcast.139), channel_id=1, replica_groups=mesh['dev'=32] {'dev'}, dimensions={0}, use_global_device_ids=true | all-gather | bytes 8448 | tf_op jit(solution)/shard_map/all_gather | solution.py:192
  349.4 18.8 %copy.45 = bf16[2,3584,1024]{1,2,0:T(8,128)(2,1)} copy(bf16[2,3584,1024]{2,1,0:T(8,128)(2,1)} %constant_dynamic-update-slice_fusion.2) | data formatting | bytes 29360128
  368.4 116.9 %while.32 = (s32[]{:T(128)}, bf16[512,1024]{0,1:T(8,128)(2,1)S(1)}, f32[16,512]{1,0:T(8,128)S(1)}, bf16[2,3584,1024]{1,2,0:T(8,128)(2,1)}, bf16[512,1024]{0,1:T(...) while((s32[]{:T(128)}, bf16[512,1024]{0,1:T(8,128)(2,1)S(1)}, ...), condition=%wide.region_5.6_spmd.clone, body=%wide.region_2.5_spmd.clone.sunk | while | flops 989068288 | bytes 57723148 | solution.py:176
  393.6 4.0 fusion.128
  437.4 4.0 fusion.128
  486.6 4.6 fusion.65
  492.0 39.5 %multiply_convert_fusion.1 = (bf16[512,4096]{1,0:T(8,128)(2,1)}, f32[512,4096]{1,0:T(8,128)}, f32[512,4096]{1,0:T(8,128)}) fusion(f32[4096]{0:T(1024)S(1)} %bitcast.137, bf16[1024,4096]{1,0:T(8,128)(2,1)} %all-gather.16.cloned.1.call-done, f32[512,1024]{1,0:T(8,128)S(1)} %get-tuple-element.429, f32[1024]{0:T(1024)S(1)} %copy-done.52, ...), kind=kOutput, calls=%fused_computation.37 | convolution fusion | flops 4436000768 | bytes 31485952 | tf_op jit(solution)/shard_map/dot_general | solution.py:30
  531.5 15.5 convert_reduce_fusion
  547.0 7.6 multiply_reduce_fusion.1
  564.5 13.4 broadcast_in_dim.106
  578.0 247.1 %while.33 = (s32[]{:T(128)}, bf16[512,1024]{0,1:T(8,128)(2,1)}, f32[2,3584,1024]{1,2,0:T(8,128)}, bf16[2,3584,1024]{1,2,0:T(8,128)(2,1)}, bf16[512,1024]{0,1:T(8...) while((s32[]{:T(128)}, bf16[512,1024]{0,1:T(8,128)(2,1)}, ...), condition=%wide.region_12.13_spmd.clone, body=%wide.region_10.12_spmd.clone.sunk | while | flops 2388851712 | bytes 142383504 | solution.py:325
  588.3 7.3 multiply_reduce_fusion.6
  595.6 7.0 multiply_convert_fusion.5
  619.2 7.3 multiply_reduce_fusion.6
  626.4 7.1 multiply_convert_fusion.5
  650.0 7.3 multiply_reduce_fusion.6
  657.3 7.1 multiply_convert_fusion.5
  680.8 7.3 multiply_reduce_fusion.6
  688.1 7.0 multiply_convert_fusion.5
  711.7 7.3 multiply_reduce_fusion.6
  718.9 7.1 multiply_convert_fusion.5
  742.5 7.3 multiply_reduce_fusion.6
  749.7 7.0 multiply_convert_fusion.5
  773.3 7.3 multiply_reduce_fusion.6
  780.6 7.0 multiply_convert_fusion.5
  804.2 7.3 multiply_reduce_fusion.6
  811.4 7.0 multiply_convert_fusion.5
  825.1 10.6 convert.8
  838.7 15.4 collective-permute-start.15
  862.7 48.6 %collective-permute-done.13 = bf16[2,512,1024]{1,2,0:T(8,128)(2,1)S(1)} collective-permute-done((bf16[2,512,1024]{1,2,0:T(8,128)(2,1)S(1)}, bf16[2,512,1024]{1,2,0:T(8,128)(2,1)S(1)}, u32[]{:S(2)}, u32[]{:S(2)}) %collective-permute-start.13) | collective-permute-done | bytes 2097184 | tf_op jit(solution)/shard_map/ppermute | solution.py:16
  911.2 5.6 add_convert_fusion.4
  916.8 31.1 %collective-permute-start.16 = (bf16[2,512,1024]{1,2,0:T(8,128)(2,1)S(1)}, bf16[2,512,1024]{1,2,0:T(8,128)(2,1)S(1)}, u32[]{:S(2)}, u32[]{:S(2)}) collective-permute-start(bf16[2,512,1024]{1,2,0:T(8,128)(2,1)S(1)} %get-tuple-element.439), channel_id=1, source_target_pairs={{0,1},{1,2},{2,3},{3,4},{4,5},{5,6},{6,7},{7,8},{8,9},{9,10},{10,1... | collective-permute-start | bytes 6291464 | tf_op jit(solution)/shard_map/ppermute | solution.py:16
  954.6 53.5 %collective-permute-start.17 = (bf16[2,512,1024]{1,2,0:T(8,128)(2,1)S(1)}, bf16[2,512,1024]{1,2,0:T(8,128)(2,1)S(1)}, u32[]{:S(2)}, u32[]{:S(2)}) collective-permute-start(bf16[2,512,1024]{1,2,0:T(8,128)(2,1)S(1)} %add_convert_fusion.2), channel_id=1, source_target_pairs={{0,1},{1,2},{2,3},{3,4},{4,5},{5,6},{6,7},{7,8},{8,9},{9,10},{10,1... | collective-permute-start | bytes 6291464 | tf_op jit(solution)/shard_map/ppermute | solution.py:16
  1023.7 10.6 fusion.54
  1034.9 12.8 fusion.37
  1060.5 7.5 fusion.31
  1068.0 100.7 %all-reduce.21 = (f32[1024]{0:T(1024)S(1)}, f32[1024]{0:T(1024)S(1)}, f32[1024]{0:T(1024)S(1)}, f32[1024]{0:T(1024)S(1)}, f32[1024]{0:T(1024)S(1)}, /*index=5*/f...) all-reduce(f32[1024]{0:T(1024)S(1)} %get-tuple-element.357, ...), channel_id=2, replica_groups=mesh['dev'=32] {'dev'}, use_global_device_ids=true, to_apply=%region_16.17.clone | all-reduce | flops 14336 | bytes 114688
  1175.1 43.1 %reduce-scatter.11.cloned.1.call-done = f32[32,1024]{1,0:T(8,128)} async-done(((f32[1024,1024]{1,0:T(8,128)}), f32[32,1024]{1,0:T(8,128)}) %reduce-scatter.11.cloned.1.call-update) | async-done | bytes 131088 | tf_op jit(solution)/shard_map/reduce_scatter | solution.py:370
  1218.2 139.6 %reduce-scatter.9.cloned.1.call-done = f32[32,1024]{1,0:T(8,128)} async-done(((f32[1024,1024]{1,0:T(8,128)}), f32[32,1024]{1,0:T(8,128)}) %reduce-scatter.9.cloned.1.call-update) | async-done | bytes 131088 | tf_op jit(solution)/shard_map/reduce_scatter | solution.py:369
  1357.8 181.6 %reduce-scatter.15.cloned.1.call-done = f32[32,4096]{1,0:T(8,128)} async-done(((f32[1024,4096]{1,0:T(8,128)}), f32[32,4096]{1,0:T(8,128)}) %reduce-scatter.15.cloned.1.call-update) | async-done | bytes 524304 | tf_op jit(solution)/shard_map/reduce_scatter | solution.py:260
  1539.4 187.4 %reduce-scatter.17.cloned.1.call-done = f32[128,1024]{1,0:T(8,128)} async-done(((f32[4096,1024]{1,0:T(8,128)}), f32[128,1024]{1,0:T(8,128)}) %reduce-scatter.17.cloned.1.call-update) | async-done | bytes 524304 | tf_op jit(solution)/shard_map/reduce_scatter | solution.py:262
  (497 shorter events, 371.7 us)
Async XLA Ops:
  7.2 56.1 %copy-start.2 = (bf16[512,1024]{1,0:T(8,128)(2,1)S(1)}, bf16[512,1024]{1,0:T(8,128)(2,1)}, u32[]{:S(2)}) copy-start(bf16[512,1024]{1,0:T(8,128)(2,1)} %param.25) | copy-start | bytes 3145732
  7.2 63.3 %all-gather.8.cloned.1.call-start = ((), (), s32[]{:S(2)}) async-start(), calls=%async_computation.6 | async-start | bytes 2162688 | tf_op jit(solution)/shard_map/all_gather | solution.py:82
  7.9 120.7 %all-gather.10.cloned.1.call-start = ((), (), s32[]{:S(2)}) async-start(), calls=%async_computation.7 | async-start | bytes 2162688 | tf_op jit(solution)/shard_map/all_gather | solution.py:83
  8.7 316.5 %all-gather.12.cloned.1.call-start = ((), (), s32[]{:S(2)}) async-start(), calls=%async_computation.8 | async-start | bytes 2162688 | tf_op jit(solution)/shard_map/all_gather | solution.py:80
  9.4 475.9 %all-gather.14.cloned.1.call-start = ((), (), s32[]{:S(2)}) async-start(), calls=%async_computation.9 | async-start | bytes 2162688 | tf_op jit(solution)/shard_map/all_gather | solution.py:85
  10.0 481.6 %all-gather.16.cloned.1.call-start = ((), (), s32[]{:S(2)}) async-start(), calls=%async_computation.10 | async-start | bytes 8650752 | tf_op jit(solution)/shard_map/all_gather | solution.py:191
  10.6 520.9 %all-gather.18.cloned.1.call-start = ((), (), s32[]{:S(2)}) async-start(), calls=%async_computation.11 | async-start | bytes 8650752 | tf_op jit(solution)/shard_map/all_gather | solution.py:193
  61.8 263.4 %copy-start.24 = (f32[1024]{0:T(1024)}, f32[1024]{0:T(1024)S(1)}, u32[]{:S(2)}) copy-start(f32[1024]{0:T(1024)S(1)} %convert_element_type.158) | copy-start | bytes 12292
  61.8 263.4 %copy-start.50 = (f32[1024]{0:T(1024)}, f32[1024]{0:T(1024)S(1)}, u32[]{:S(2)}) copy-start(f32[1024]{0:T(1024)S(1)} %convert_element_type.159) | copy-start | bytes 12292
  63.3 261.9 %copy-start.26 = (f32[512]{0:T(512)}, f32[512]{0:T(512)S(1)}, u32[]{:S(2)}) copy-start(f32[512]{0:T(512)S(1)} %broadcast_multiply_fusion.1) | copy-start | bytes 6148
  63.8 261.5 %copy-start.38 = (f32[512]{0:T(512)}, f32[512]{0:T(512)S(1)}, u32[]{:S(2)}) copy-start(f32[512]{0:T(512)S(1)} %fusion.47) | copy-start | bytes 6148
  131.5 112.6 %copy-start.55 = (s32[512]{0:T(512)S(1)}, s32[512]{0:T(512)}, u32[]{:S(2)}) copy-start(s32[512]{0:T(512)} %param.28) | copy-start | bytes 6148
  131.5 112.5 %copy-start.56 = (s32[512]{0:T(512)S(1)}, s32[512]{0:T(512)}, u32[]{:S(2)}) copy-start(s32[512]{0:T(512)} %param.27) | copy-start | bytes 6148
  131.6 152.0 %copy-start.57 = (bf16[128]{0:T(256)(128)(2,1)S(1)}, bf16[128]{0:T(256)(128)(2,1)}, u32[]{:S(2)}) copy-start(bf16[128]{0:T(256)(128)(2,1)} %param.42) | copy-start | bytes 772
  132.5 5.9 collective-permute-start
  134.8 57.2 %collective-permute-start.3 = (bf16[2,512,1024]{2,1,0:T(8,128)(2,1)S(1)}, bf16[2,512,1024]{2,1,0:T(8,128)(2,1)}, u32[]{:S(2)}, u32[]{:S(2)}) collective-permute-start(bf16[2,512,1024]{2,1,0:T(8,128)(2,1)S(1)} %pad_maximum_fusion), channel_id=1, source_target_pairs={{1,0},{2,1},{3,2},{4,3},{5,4},{6,5},{7,6},{8,7},{9,8},{10,9},{11,1... | collective-permute-start | bytes 6291464 | tf_op jit(solution)/shard_map/ppermute | solution.py:16
  139.7 54.8 %collective-permute-start.1 = (bf16[2,512,1024]{2,1,0:T(8,128)(2,1)S(1)}, bf16[2,512,1024]{2,1,0:T(8,128)(2,1)}, u32[]{:S(2)}, u32[]{:S(2)}) collective-permute-start(bf16[2,512,1024]{2,1,0:T(8,128)(2,1)S(1)} %collective-permute-done), channel_id=1, source_target_pairs={{0,1},{1,2},{2,3},{3,4},{4,5},{5,6},{6,7},{7,8},{8,9},{9,10},{10,1... | collective-permute-start | bytes 6291464 | tf_op jit(solution)/shard_map/ppermute | solution.py:16
  192.0 131.5 %collective-permute-start.4 = (bf16[2,512,1024]{2,1,0:T(8,128)(2,1)}, bf16[2,512,1024]{2,1,0:T(8,128)(2,1)}, u32[]{:S(2)}, u32[]{:S(2)}) collective-permute-start(bf16[2,512,1024]{2,1,0:T(8,128)(2,1)} %collective-permute-done.3), channel_id=1, source_target_pairs={{1,0},{2,1},{3,2},{4,3},{5,4},{6,5},{7,6},{8,7},{9,8},{10,9},{11,1... | collective-permute-start | bytes 6291464 | tf_op jit(solution)/shard_map/ppermute | solution.py:16
  194.5 136.2 %collective-permute-start.2 = (bf16[2,512,1024]{2,1,0:T(8,128)(2,1)}, bf16[2,512,1024]{2,1,0:T(8,128)(2,1)}, u32[]{:S(2)}, u32[]{:S(2)}) collective-permute-start(bf16[2,512,1024]{2,1,0:T(8,128)(2,1)} %collective-permute-done.1), channel_id=1, source_target_pairs={{0,1},{1,2},{2,3},{3,4},{4,5},{5,6},{6,7},{7,8},{8,9},{9,10},{10,1... | collective-permute-start | bytes 6291464 | tf_op jit(solution)/shard_map/ppermute | solution.py:16
  244.1 4.6 collective-permute-start.6
  247.3 29.9 %collective-permute-start.9 = (s32[2,512]{1,0:T(2,128)S(1)}, s32[2,512]{1,0:T(2,128)S(1)}, u32[]{:S(2)}, u32[]{:S(2)}) collective-permute-start(s32[2,512]{1,0:T(2,128)S(1)} %pad_add_fusion), channel_id=1, source_target_pairs={{1,0},{2,1},{3,2},{4,3},{5,4},{6,5},{7,6},{8,7},{9,8},{10,9},{11,1... | collective-permute-start | bytes 12296 | tf_op jit(solution)/shard_map/ppermute | solution.py:16
  248.7 926.5 %reduce-scatter.13.cloned.1.call-start = ((), (), s32[]{:S(2)}) async-start(), calls=%async_computation.15 | async-start | bytes 4325376 | tf_op jit(solution)/shard_map/reduce_scatter | solution.py:372
  248.7 29.8 %collective-permute-start.7 = (s32[2,512]{1,0:T(2,128)S(1)}, s32[2,512]{1,0:T(2,128)S(1)}, u32[]{:S(2)}, u32[]{:S(2)}) collective-permute-start(s32[2,512]{1,0:T(2,128)S(1)} %collective-permute-done.6), channel_id=1, source_target_pairs={{0,1},{1,2},{2,3},{3,4},{4,5},{5,6},{6,7},{7,8},{8,9},{9,10},{10,1... | collective-permute-start | bytes 12296 | tf_op jit(solution)/shard_map/ppermute | solution.py:16
  277.2 44.9 %collective-permute-start.10 = (s32[2,512]{1,0:T(2,128)S(1)}, s32[2,512]{1,0:T(2,128)S(1)}, u32[]{:S(2)}, u32[]{:S(2)}) collective-permute-start(s32[2,512]{1,0:T(2,128)S(1)} %collective-permute-done.9), channel_id=1, source_target_pairs={{1,0},{2,1},{3,2},{4,3},{5,4},{6,5},{7,6},{8,7},{9,8},{10,9},{11,1... | collective-permute-start | bytes 12296 | tf_op jit(solution)/shard_map/ppermute | solution.py:16
  278.5 44.9 %collective-permute-start.8 = (s32[2,512]{1,0:T(2,128)S(1)}, s32[2,512]{1,0:T(2,128)S(1)}, u32[]{:S(2)}, u32[]{:S(2)}) collective-permute-start(s32[2,512]{1,0:T(2,128)S(1)} %collective-permute-done.7), channel_id=1, source_target_pairs={{0,1},{1,2},{2,3},{3,4},{4,5},{5,6},{6,7},{7,8},{8,9},{9,10},{10,1... | collective-permute-start | bytes 12296 | tf_op jit(solution)/shard_map/ppermute | solution.py:16
  322.1 3.0 collective-permute-start.11
  323.4 22.9 %collective-permute-start.5 = (bf16[2,512,1024]{2,1,0:T(8,128)(2,1)}, bf16[2,512,1024]{2,1,0:T(8,128)(2,1)}, u32[]{:S(2)}, u32[]{:S(2)}) collective-permute-start(bf16[2,512,1024]{2,1,0:T(8,128)(2,1)} %collective-permute-done.4), channel_id=1, source_target_pairs={{1,0},{2,1},{3,2},{4,3},{5,4},{6,5},{7,6},{8,7},{9,8},{10,9},{11,1... | collective-permute-start | bytes 6291464 | tf_op jit(solution)/shard_map/ppermute | solution.py:16
  368.3 118.2 %copy-start.3 = (bf16[512,1024]{1,0:T(8,128)(2,1)S(1)}, bf16[512,1024]{1,0:T(8,128)(2,1)}, u32[]{:S(2)}) copy-start(bf16[512,1024]{1,0:T(8,128)(2,1)} %param.25) | copy-start | bytes 3145732
  368.3 118.2 %copy-start.37 = (f32[1024]{0:T(1024)S(1)}, f32[1024]{0:T(1024)}, u32[]{:S(2)}) copy-start(f32[1024]{0:T(1024)} %convert_element_type.157) | copy-start | bytes 12292
  368.4 118.2 %copy-start.48 = (f32[1024]{0:T(1024)S(1)}, f32[1024]{0:T(1024)}, u32[]{:S(2)}) copy-start(f32[1024]{0:T(1024)} %convert_element_type.167) | copy-start | bytes 12292
  491.2 63.4 %copy-start.5 = (f32[512,1024]{1,0:T(8,128)}, f32[512,1024]{1,0:T(8,128)S(1)}, u32[]{:S(2)}) copy-start(f32[512,1024]{1,0:T(8,128)S(1)} %get-tuple-element.429) | copy-start | bytes 6291460
  491.2 63.4 %copy-start.30 = (f32[512]{0:T(512)}, f32[512]{0:T(512)S(1)}, u32[]{:S(2)}) copy-start(f32[512]{0:T(512)S(1)} %broadcast_multiply_fusion) | copy-start | bytes 6148
  491.6 63.0 %copy-start.42 = (f32[512]{0:T(512)}, f32[512]{0:T(512)S(1)}, u32[]{:S(2)}) copy-start(f32[512]{0:T(512)S(1)} %fusion.48) | copy-start | bytes 6148
  492.0 39.5 %copy-start.20 = (bf16[512,1024]{1,0:T(8,128)(2,1)S(1)}, bf16[512,1024]{1,0:T(8,128)(2,1)}, u32[]{:S(2)}) copy-start(bf16[512,1024]{1,0:T(8,128)(2,1)} %param.26) | copy-start | bytes 3145732
  492.0 39.5 %copy-start.46 = (f32[1024]{0:T(1024)S(1)}, f32[1024]{0:T(1024)}, u32[]{:S(2)}) copy-start(f32[1024]{0:T(1024)} %convert_element_type.168) | copy-start | bytes 12292
  560.6 614.6 %reduce-scatter.7.cloned.1.call-start = ((), (), s32[]{:S(2)}) async-start(), calls=%async_computation.12 | async-start | bytes 4325376 | tf_op jit(solution)/shard_map/reduce_scatter | solution.py:367
  835.7 18.3 %copy-start.4 = (bf16[512,1024]{1,0:T(8,128)(2,1)S(1)}, bf16[512,1024]{1,0:T(8,128)(2,1)}, u32[]{:S(2)}) copy-start(bf16[512,1024]{1,0:T(8,128)(2,1)} %param.25) | copy-start | bytes 3145732
  835.7 18.3 %copy-start.12 = (bf16[512,1024]{0,1:T(8,128)(2,1)S(1)}, bf16[512,1024]{0,1:T(8,128)(2,1)}, u32[]{:S(2)}) copy-start(bf16[512,1024]{0,1:T(8,128)(2,1)} %get-tuple-element.271) | copy-start | bytes 3145732
  837.4 20.4 %collective-permute-start.12 = (bf16[2,512,1024]{1,2,0:T(8,128)(2,1)}, bf16[2,512,1024]{1,2,0:T(8,128)(2,1)}, u32[]{:S(2)}, u32[]{:S(2)}) collective-permute-start(bf16[2,512,1024]{1,2,0:T(8,128)(2,1)} %get-tuple-element.440), channel_id=1, source_target_pairs={{1,0},{2,1},{3,2},{4,3},{5,4},{6,5},{7,6},{8,7},{9,8},{10,9},{11,1... | collective-permute-start | bytes 6291464 | tf_op jit(solution)/shard_map/ppermute | solution.py:16
  838.7 24.0 %collective-permute-start.15 = (bf16[2,512,1024]{1,2,0:T(8,128)(2,1)S(1)}, bf16[2,512,1024]{1,2,0:T(8,128)(2,1)}, u32[]{:S(2)}, u32[]{:S(2)}) collective-permute-start(bf16[2,512,1024]{1,2,0:T(8,128)(2,1)S(1)} %get-tuple-element.441), channel_id=1, source_target_pairs={{0,1},{1,2},{2,3},{3,4},{4,5},{5,6},{6,7},{7,8},{8,9},{9,10},{10,1... | collective-permute-start | bytes 6291464 | tf_op jit(solution)/shard_map/ppermute | solution.py:16
  857.7 360.5 %reduce-scatter.11.cloned.1.call-start = ((), (), s32[]{:S(2)}) async-start(), calls=%async_computation.14 | async-start | bytes 4325376 | tf_op jit(solution)/shard_map/reduce_scatter | solution.py:370
  861.4 49.9 %collective-permute-start.13 = (bf16[2,512,1024]{1,2,0:T(8,128)(2,1)S(1)}, bf16[2,512,1024]{1,2,0:T(8,128)(2,1)S(1)}, u32[]{:S(2)}, u32[]{:S(2)}) collective-permute-start(bf16[2,512,1024]{1,2,0:T(8,128)(2,1)S(1)} %add_convert_fusion.5), channel_id=1, source_target_pairs={{1,0},{2,1},{3,2},{4,3},{5,4},{6,5},{7,6},{8,7},{9,8},{10,9},{11,1... | collective-permute-start | bytes 6291464 | tf_op jit(solution)/shard_map/ppermute | solution.py:16
  916.8 34.8 %collective-permute-start.16 = (bf16[2,512,1024]{1,2,0:T(8,128)(2,1)S(1)}, bf16[2,512,1024]{1,2,0:T(8,128)(2,1)S(1)}, u32[]{:S(2)}, u32[]{:S(2)}) collective-permute-start(bf16[2,512,1024]{1,2,0:T(8,128)(2,1)S(1)} %get-tuple-element.439), channel_id=1, source_target_pairs={{0,1},{1,2},{2,3},{3,4},{4,5},{5,6},{6,7},{7,8},{8,9},{9,10},{10,1... | collective-permute-start | bytes 6291464 | tf_op jit(solution)/shard_map/ppermute | solution.py:16
  947.9 60.2 %collective-permute-start.14 = (bf16[2,512,1024]{1,2,0:T(8,128)(2,1)S(1)}, bf16[2,512,1024]{1,2,0:T(8,128)(2,1)S(1)}, u32[]{:S(2)}, u32[]{:S(2)}) collective-permute-start(bf16[2,512,1024]{1,2,0:T(8,128)(2,1)S(1)} %get-tuple-element.438), channel_id=1, source_target_pairs={{1,0},{2,1},{3,2},{4,3},{5,4},{6,5},{7,6},{8,7},{9,8},{10,9},{11,1... | collective-permute-start | bytes 6291464 | tf_op jit(solution)/shard_map/ppermute | solution.py:16
  954.6 57.2 %collective-permute-start.17 = (bf16[2,512,1024]{1,2,0:T(8,128)(2,1)S(1)}, bf16[2,512,1024]{1,2,0:T(8,128)(2,1)S(1)}, u32[]{:S(2)}, u32[]{:S(2)}) collective-permute-start(bf16[2,512,1024]{1,2,0:T(8,128)(2,1)S(1)} %add_convert_fusion.2), channel_id=1, source_target_pairs={{0,1},{1,2},{2,3},{3,4},{4,5},{5,6},{6,7},{7,8},{8,9},{9,10},{10,1... | collective-permute-start | bytes 6291464 | tf_op jit(solution)/shard_map/ppermute | solution.py:16
  1018.5 339.4 %reduce-scatter.9.cloned.1.call-start = ((), (), s32[]{:S(2)}) async-start(), calls=%async_computation.13 | async-start | bytes 4325376 | tf_op jit(solution)/shard_map/reduce_scatter | solution.py:369
  1022.1 517.3 %reduce-scatter.15.cloned.1.call-start = ((), (), s32[]{:S(2)}) async-start(), calls=%async_computation.16 | async-start | bytes 17301504 | tf_op jit(solution)/shard_map/reduce_scatter | solution.py:260
  1034.2 692.5 %reduce-scatter.17.cloned.1.call-start = ((), (), s32[]{:S(2)}) async-start(), calls=%async_computation.17 | async-start | bytes 17301504 | tf_op jit(solution)/shard_map/reduce_scatter | solution.py:262
  (74 other events, 283.4 us)
Sparse Core Ops, SparseCore 0:
  10.9 59.5 all-gather.7
  73.3 55.2 all-gather.9
  131.5 65.7 all-gather.11
  200.0 69.3 all-gather.13
  272.1 85.0 all-gather.15
  359.9 77.0 all-gather.17
  560.7 159.8 reduce-scatter.12
  857.8 202.5 reduce-scatter.6
  1063.3 154.9 reduce-scatter.10
  1220.9 136.8 reduce-scatter.8
  1360.7 178.6 reduce-scatter.14
  1542.1 184.6 reduce-scatter.16
where the time goes:
time: 1740 us; the launch traced here: 1730 us
  waiting for transfers between devices  675 us (39%)
  matrix products  319 us (18%)
  starting transfers between devices  250 us (14%)
  blocking collectives  181 us (10%)
  other arithmetic  171 us (10%)
  local copies, waits for them, and re-layouts  120 us (7%)
    ppermute x18, starting transfers between devices, passed_along(): return lax.ppermute(block, axis, route)  250 us
    reduce_scatter x1, waiting for transfers between devices, on_device(): lax.psum_scatter(project_weight_grad, 'dev', scatter_dimension=0, tiled=T...  187 us
    reduce_scatter x1, waiting for transfers between devices, on_device(): lax.psum_scatter(hidden_weight_grad, 'dev', scatter_dimension=0, tiled=True)  182 us
    unnamed x2, blocking collectives  144 us
    reduce_scatter x1, waiting for transfers between devices, on_device(): lax.psum_scatter(key_weight_grad, 'dev', scatter_dimension=0, tiled=True)  140 us
    dot_general x6, matrix products, product(): return jnp.dot(left_rows, right_rows, preferred_element_type=jnp.float32)  61.2 us
    unnamed x163, local copies, waits for them, and re-layouts  59.5 us
    ppermute x18, waiting for transfers between devices, passed_along(): return lax.ppermute(block, axis, route)  58.2 us
  transfers between devices with their start and end apart: 30, of which 12 were waited for; matrix products, arithmetic and copies ran while one was open for 33% of the time, Pallas kernels for 0%

commit v1 on v0

v1 whole, which is shorter than its diff:
```python
from functools import partial
import jax
import jax.numpy as jnp
from jax import lax
from jax.experimental import pallas as pl
from jax.experimental.pallas import tpu as pltpu
from jax.sharding import PartitionSpec as P

HEAD_DIM = 64
PAIR = 2 * HEAD_DIM
IMG = 1370
BLK = 256
norm_eps = 1e-06
bf16 = jnp.bfloat16
f32 = jnp.float32
NEG = -1e30


def layer_norm(row_values, gain_row, bias_row):
    center = row_values - jnp.mean(row_values, axis=-1, keepdims=True)
    spread = jnp.mean(center * center, axis=-1, keepdims=True)
    return center * lax.rsqrt(spread + norm_eps) * gain_row + bias_row


def gelu_exact(arguments):
    return jax.nn.gelu(arguments, approximate=False)


def product(a, b):
    return jnp.dot(a, b, preferred_element_type=f32)


def inner_rows(a, b):
    return lax.dot_general(a, b, (((0,), (0,)), ((), ())), preferred_element_type=f32)


def against(a, b):
    return lax.dot_general(a, b, (((1,), (1,)), ((), ())), preferred_element_type=f32)


def column_sums(rows):
    return jnp.sum(rows.astype(f32), axis=0)


def head_lanes(h):
    lane = lax.broadcasted_iota(jnp.int32, (1, PAIR), 1)
    return (lane >= h * HEAD_DIM) & (lane < (h + 1) * HEAD_DIM)


def own_head(block, h):
    return jnp.where(head_lanes(h), block, jnp.zeros_like(block))


def offsets():
    shape = (BLK, BLK)
    return lax.broadcasted_iota(jnp.int32, shape, 1) - lax.broadcasted_iota(jnp.int32, shape, 0)


def attend_kernel(first, lo, hi, q_ref, k_ref, v_ref, ql_ref, kl_ref, o_ref, lse_ref, s_ref, m_ref, l_ref, a_ref):
    block = pl.program_id(1)
    start, stop = lo[block], hi[block]
    apart = offsets()
    ql = ql_ref[...]
    heads = [own_head(q_ref[...], h) for h in range(2)]
    m_ref[...] = jnp.full(m_ref.shape, NEG, f32)
    l_ref[...] = jnp.zeros(l_ref.shape, f32)
    a_ref[...] = jnp.zeros(a_ref.shape, f32)

    def scores(kb, _):
        rows = pl.ds(pl.multiple_of(kb * BLK, BLK), BLK)
        k = k_ref[rows, :]
        seen = (ql == kl_ref[:, rows]) | (apart == (first + block - kb) * BLK)
        for h in range(2):
            s = jnp.where(seen, against(heads[h], k), NEG)
            s_ref[h, kb] = s
            m_ref[h] = jnp.maximum(m_ref[h], jnp.maximum(s[:, :128], s[:, 128:]))
        return 0

    lax.fori_loop(start, stop, scores, 0)
    peaks = [jnp.max(m_ref[h], axis=1, keepdims=True) for h in range(2)]

    def values(kb, _):
        rows = pl.ds(pl.multiple_of(kb * BLK, BLK), BLK)
        v = v_ref[rows, :]
        for h in range(2):
            p = jnp.exp(s_ref[h, kb] - peaks[h])
            l_ref[h] = l_ref[h] + (p[:, :128] + p[:, 128:])
            a_ref[h] = a_ref[h] + product(p.astype(bf16), v)
        return 0

    lax.fori_loop(start, stop, values, 0)
    totals = [jnp.sum(l_ref[h], axis=1, keepdims=True) for h in range(2)]
    first_head = head_lanes(0)
    o_ref[...] = jnp.where(first_head, a_ref[0] / totals[0], a_ref[1] / totals[1])
    lse_ref[...] = jnp.where(first_head, peaks[0] + jnp.log(totals[0]), peaks[1] + jnp.log(totals[1]))


def query_kernel(first, lo, hi, q_ref, k_ref, v_ref, ql_ref, kl_ref, do_ref, lse_ref, dl_ref, dq_ref, a_ref):
    block = pl.program_id(1)
    apart = offsets()
    ql = ql_ref[...]
    q = [own_head(q_ref[...], h) for h in range(2)]
    do = [own_head(do_ref[...], h) for h in range(2)]
    lse = [lse_ref[:, h * HEAD_DIM : h * HEAD_DIM + 1] for h in range(2)]
    delta = [dl_ref[:, h * HEAD_DIM : h * HEAD_DIM + 1] for h in range(2)]
    a_ref[...] = jnp.zeros(a_ref.shape, f32)

    def step(kb, _):
        rows = pl.ds(pl.multiple_of(kb * BLK, BLK), BLK)
        k = k_ref[rows, :]
        v = v_ref[rows, :]
        seen = (ql == kl_ref[:, rows]) | (apart == (first + block - kb) * BLK)
        for h in range(2):
            p = jnp.exp(jnp.where(seen, against(q[h], k), NEG) - lse[h])
            ds = (p * (against(do[h], v) - delta[h])).astype(bf16)
            a_ref[h] = a_ref[h] + product(ds, k)
        return 0

    lax.fori_loop(lo[block], hi[block], step, 0)
    dq_ref[...] = (jnp.where(head_lanes(0), a_ref[0], a_ref[1]) * (HEAD_DIM**-0.5)).astype(bf16)


def key_kernel(first, lo, hi, q_ref, k_ref, v_ref, ql_ref, kl_ref, do_ref, st_ref, dk_ref, dv_ref, a_ref, b_ref):
    block = pl.program_id(1)
    pair = pl.program_id(0)
    apart = offsets()
    kl = kl_ref[...]
    k = [own_head(k_ref[...], h) for h in range(2)]
    v = [own_head(v_ref[...], h) for h in range(2)]
    a_ref[...] = jnp.zeros(a_ref.shape, f32)
    b_ref[...] = jnp.zeros(b_ref.shape, f32)

    def step(qb, _):
        rows = pl.ds(pl.multiple_of(qb * BLK, BLK), BLK)
        q = q_ref[rows, :]
        do = do_ref[rows, :]
        seen = (kl == ql_ref[:, rows]) | (apart == (first + block - qb) * BLK)
        for h in range(2):
            lse = st_ref[0, h : h + 1, rows]
            delta = st_ref[0, 2 + h : 3 + h, rows]
            p = jnp.exp(jnp.where(seen, against(k[h], q), NEG) - lse)
            ds = (p * (against(v[h], do) - delta)).astype(bf16)
            a_ref[h] = a_ref[h] + product(ds, q)
            b_ref[h] = b_ref[h] + product(p.astype(bf16), do)
        return 0

    lax.fori_loop(lo[block], hi[block], step, 0)
    dk_ref[...] = jnp.where(head_lanes(0), a_ref[0], a_ref[1]).astype(bf16)
    dv_ref[...] = jnp.where(head_lanes(0), b_ref[0], b_ref[1]).astype(bf16)


def attention_call(kernel, grid, in_specs, out_specs, out_shape, scratch, flops):
    return pl.pallas_call(
        kernel,
        grid_spec=pltpu.PrefetchScalarGridSpec(
            num_scalar_prefetch=2,
            grid=grid,
            in_specs=in_specs,
            out_specs=out_specs,
            scratch_shapes=scratch,
        ),
        out_shape=out_shape,
        compiler_params=pltpu.CompilerParams(vmem_limit_bytes=48 * 1024 * 1024),
        cost_estimate=pl.CostEstimate(flops=flops, bytes_accessed=20_000_000, transcendentals=12_000_000),
    )


def own_bit(bit):
    return (lax.axis_index("dev") >> bit) & 1


def swap(block, bit):
    count = lax.axis_size("dev")
    return lax.ppermute(block, "dev", [(i, i ^ (1 << bit)) for i in range(count)])


def shifted(block, distance):
    count = lax.axis_size("dev")
    return lax.ppermute(block, "dev", [(i, i + distance) for i in range(count) if 0 <= i + distance < count])


def pick(block, axis, index):
    return lax.dynamic_index_in_dim(block, index, axis, keepdims=False)


def scatter_sum(block, bits, order, kind=bf16):
    bits = list(bits)
    for bit in order:
        axis = bits.index(bit)
        mine = own_bit(bit)
        sent = pick(block, axis, 1 - mine).astype(kind)
        kept = pick(block, axis, mine)
        block = kept.astype(f32) + swap(sent, bit).astype(f32)
        if kind == bf16:
            block = block.astype(bf16)
        bits.remove(bit)
    return block


def bit_view(block, count, lead):
    depth = count.bit_length() - 1
    return block.reshape((2,) * depth + (lead,) + block.shape[1:])


def on_device(
    tokens,
    cotangent,
    segment_ids,
    validity,
    first_gain,
    first_bias,
    query_weight,
    query_bias,
    key_weight,
    value_weight,
    value_bias,
    output_weight,
    output_bias,
    attention_scale,
    second_gain,
    second_bias,
    hidden_weight,
    hidden_bias,
    project_weight,
    project_bias,
    dense_scale,
):
    count = lax.axis_size("dev")
    depth = count.bit_length() - 1
    rows, width = tokens.shape
    half = width // 2
    window = 8 * rows
    assert 1 << depth == count and 2 * rows + rows >= IMG - 1 and rows % BLK == 0
    core = own_bit(0)
    shard = query_weight.shape[0]
    ff = hidden_weight.shape[1]
    parts = ff // width

    vectors = jnp.concatenate(
        [
            v.reshape(-1, shard).T
            for v in (
                first_gain,
                first_bias,
                query_bias,
                value_bias,
                output_bias,
                attention_scale,
                second_gain,
                second_bias,
                project_bias,
                dense_scale,
                hidden_bias,
            )
        ],
        axis=1,
    )
    vectors = jnp.pad(vectors, ((0, 0), (0, 128 - vectors.shape[1])))
    attention_pack = jnp.concatenate(
        [w[:, c * half : (c + 1) * half] for c in range(2) for w in (query_weight, key_weight, value_weight)]
        + [output_weight, vectors],
        axis=1,
    )
    dense_pack = jnp.concatenate(
        [hidden_weight[:, j * width : (j + 1) * width] for j in range(parts)] + [project_weight], axis=0
    )
    attention_full = lax.all_gather(attention_pack, "dev", axis=0, tiled=True)
    dense_full = lax.all_gather(dense_pack, "dev", axis=0, tiled=True).reshape(count, -1, width)

    labels = segment_ids + 1
    tag_rows = jnp.stack(
        [jnp.concatenate([labels % 256, labels // 256]), jnp.concatenate([validity, jnp.zeros_like(validity)])]
    ).astype(bf16)
    tag_rows = jnp.pad(tag_rows, ((0, 14), (0, 0)))
    own = jnp.concatenate([tokens, tag_rows])
    below = shifted(own, 2)
    above = shifted(own, -2)
    far = lax.ppermute(
        own,
        "dev",
        [(i, i - 4) for i in range(4, count, 2)] + [(i, i + 4) for i in range(1, count - 4, 2)],
    )
    mine = jnp.stack([below, own, above, far])
    theirs = swap(mine, 0)
    zero, one = jnp.where(core == 0, mine, theirs), jnp.where(core == 0, theirs, mine)
    blocks = [one[3], zero[0], one[0], zero[1], one[1], zero[2], one[2], zero[3]]
    window_tokens = jnp.concatenate([b[:rows] for b in blocks])
    tags = jnp.stack([b[rows : rows + 2] for b in blocks]).astype(jnp.int32)
    window_labels = (tags[:, 0, :rows] + 256 * tags[:, 0, rows:]).reshape(window)
    window_valid = tags[:, 1, :rows].reshape(window)
    key_label = jnp.where(window_valid == 1, window_labels, 0)
    query_label = jnp.where(window_labels == 0, -1, window_labels)
    first_row, last_row = 3 * rows, 5 * rows
    own_blocks = 2 * rows // BLK
    index = lax.broadcasted_iota(jnp.int32, (own_blocks, window), 1)
    block_labels = window_labels[first_row:last_row].reshape(own_blocks, BLK)
    lo = jnp.min(jnp.where(window_labels[None] == block_labels[:, :1], index, window), axis=1) // BLK
    hi = jnp.max(jnp.where(window_labels[None] == block_labels[:, -1:], index, -1), axis=1) // BLK + 1

    columns = attention_full[:, 4 * width :].T.astype(f32)
    (
        gain_first,
        bias_first,
        bias_query,
        bias_value,
        bias_output,
        scale_first,
        gain_second,
        bias_second,
        bias_project,
        scale_second,
    ) = [columns[i] for i in range(10)]
    bias_hidden = columns[10 : 10 + parts].reshape(parts, count, shard).transpose(1, 0, 2).reshape(ff)
    weight_qkv = lax.dynamic_slice_in_dim(attention_full, core * 3 * half, 3 * half, 1)
    weight_output = attention_full[:, 3 * width : 4 * width]

    normed_window = layer_norm(window_tokens.astype(f32), gain_first, bias_first).astype(bf16)
    start = core * half
    bias_qkv = jnp.concatenate(
        [
            lax.dynamic_slice_in_dim(bias_query, start, half),
            jnp.zeros((half,), f32),
            lax.dynamic_slice_in_dim(bias_value, start, half),
        ]
    )
    scale_qkv = jnp.concatenate([jnp.full((half,), HEAD_DIM**-0.5, f32), jnp.ones((2 * half,), f32)])
    projected = ((product(normed_window, weight_qkv) + bias_qkv) * scale_qkv).astype(bf16)

    pairs = half // PAIR
    grid = (pairs, own_blocks)
    first = first_row // BLK
    q_own = pl.BlockSpec((BLK, PAIR), lambda h, b, lo, hi: (first + b, h))
    k_own = pl.BlockSpec((BLK, PAIR), lambda h, b, lo, hi: (first + b, pairs + h))
    v_own = pl.BlockSpec((BLK, PAIR), lambda h, b, lo, hi: (first + b, 2 * pairs + h))
    q_all = pl.BlockSpec((window, PAIR), lambda h, b, lo, hi: (0, h))
    k_all = pl.BlockSpec((window, PAIR), lambda h, b, lo, hi: (0, pairs + h))
    v_all = pl.BlockSpec((window, PAIR), lambda h, b, lo, hi: (0, 2 * pairs + h))
    row_block = pl.BlockSpec((BLK, PAIR), lambda h, b, lo, hi: (b, h))
    label_rows = pl.BlockSpec((BLK, 1), lambda h, b, lo, hi: (first + b, 0))
    label_all = pl.BlockSpec((1, window), lambda h, b, lo, hi: (0, 0))
    share = 2 * rows * 1400 * half * 2
    attended_f, lse = attention_call(
        partial(attend_kernel, first),
        grid,
        [q_own, k_all, v_all, label_rows, label_all],
        [row_block, row_block],
        [jax.ShapeDtypeStruct((2 * rows, half), f32)] * 2,
        [
            pltpu.VMEM((2, window // BLK, BLK, BLK), f32),
            pltpu.VMEM((2, BLK, 128), f32),
            pltpu.VMEM((2, BLK, 128), f32),
            pltpu.VMEM((2, BLK, PAIR), f32),
        ],
        2 * share,
    )(lo, hi, projected, projected, projected, query_label[:, None], key_label[None])

    def columns_of(c, mine, theirs):
        return jnp.where(c == 0, jnp.concatenate([mine, theirs], 1), jnp.concatenate([theirs, mine], 1))

    attended_half = attended_f.astype(bf16)
    attended_low = columns_of(
        core,
        lax.dynamic_slice_in_dim(attended_half, core * rows, rows, 0),
        swap(lax.dynamic_slice_in_dim(attended_half, (1 - core) * rows, rows, 0), 0),
    )
    inputs = tokens.astype(f32)
    branch = product(attended_low, weight_output) + bias_output
    middle = inputs + scale_first * branch

    weight_hidden = (
        dense_full[:, : parts * shard]
        .reshape(count, parts, shard, width)
        .transpose(0, 2, 1, 3)
        .reshape(width, ff)
    )
    weight_project = dense_full[:, parts * shard :].reshape(ff, width)
    normed_two, second_norm_back = jax.vjp(layer_norm, middle, gain_second, bias_second)
    normed_two_low = normed_two.astype(bf16)
    hidden = product(normed_two_low, weight_hidden) + bias_hidden
    active, gelu_back = jax.vjp(gelu_exact, hidden)
    active_low = active.astype(bf16)
    dense_out = product(active_low, weight_project) + bias_project
    layer_output = (middle + scale_second * dense_out).astype(bf16)
    upstream = cotangent.astype(f32)
    dense_scale_grad = jnp.sum(upstream * dense_out, axis=0)
    grad_dense = (upstream * scale_second).astype(bf16)
    project_weight_grad = inner_rows(active_low, grad_dense).astype(bf16)
    project_bias_grad = column_sums(grad_dense)
    grad_hidden = gelu_back(against(grad_dense, weight_project))[0].astype(bf16)
    hidden_weight_grad = inner_rows(normed_two_low, grad_hidden).astype(bf16)
    hidden_bias_grad = column_sums(grad_hidden)
    grad_middle_norm, second_gain_grad, second_bias_grad = second_norm_back(against(grad_hidden, weight_hidden))
    grad_middle = upstream + grad_middle_norm
    attention_scale_grad = jnp.sum(grad_middle * branch, axis=0)
    grad_branch = (grad_middle * scale_first).astype(bf16)
    output_weight_grad = inner_rows(attended_low, grad_branch).astype(bf16)
    output_bias_grad = column_sums(grad_branch)
    grad_attended = against(grad_branch, weight_output).astype(bf16)

    bits = list(range(depth - 1, -1, -1))
    project_rows = project_weight_grad.shape[0] // count
    cut = 3 * width // 4
    part_a = bit_view(project_weight_grad[:, :cut], count, project_rows)
    part_b = bit_view(hidden_weight_grad[:, :3 * width], count, shard)
    rest = project_weight_grad[:, cut:].reshape(count, parts, shard, width - cut)
    part_c = jnp.concatenate(
        [rest[:, j] for j in range(parts)]
        + [
            hidden_weight_grad[:, 3 * width :].reshape(count, shard, -1),
            output_weight_grad.reshape(count, shard, width),
        ],
        axis=2,
    )
    part_c = part_c.reshape((2,) * depth + part_c.shape[1:])

    def order_of(turn, low):
        chips = list(range(1, depth))
        axes, last = chips[:3], chips[3:]
        return low + axes[turn:] + axes[:turn] + last

    sum_a = scatter_sum(part_a, bits, order_of(0, [0]))
    sum_b = scatter_sum(part_b, bits, order_of(1, [0]))
    sum_c = scatter_sum(part_c, bits, order_of(2, [0]))

    grad_half = jnp.where(core == 0, grad_attended[:, :half], grad_attended[:, half:])
    grad_other = swap(jnp.where(core == 0, grad_attended[:, half:], grad_attended[:, :half]), 0)
    grad_pair = jnp.where(
        core == 0, jnp.concatenate([grad_half, grad_other]), jnp.concatenate([grad_other, grad_half])
    )
    delta = jnp.sum((grad_pair.astype(f32) * attended_f).reshape(2 * rows, 2 * pairs, HEAD_DIM), axis=2)
    stats = jnp.concatenate([lse.reshape(2 * rows, 2 * pairs, HEAD_DIM)[:, :, 0].T, delta.T])
    top = lax.reduce_precision(stats, 8, 7)
    mid = lax.reduce_precision(stats - top, 8, 7)
    pieces = jnp.concatenate([top, mid, stats - top - mid]).astype(bf16)
    stat_count = pieces.shape[0]
    packed = [jnp.concatenate([grad_pair[c * rows : (c + 1) * rows], pieces[:, c * rows : (c + 1) * rows]]) for c in range(2)]
    both = jnp.concatenate(packed)
    from_below = shifted(both, 2)
    from_above = shifted(both, -2)
    far_below = shifted(packed[1], 4)
    far_above = shifted(packed[0], -4)
    unit = rows + stat_count
    arrived = [far_below, from_below[:unit], from_below[unit:], packed[0], packed[1], from_above[:unit], from_above[unit:], far_above]
    grad_window = jnp.concatenate([b[:rows] for b in arrived])
    stat_window = jnp.concatenate([b[rows:] for b in arrived], axis=1).astype(f32)
    stat_window = stat_window.reshape(3, 2, pairs, 2, window)
    stat_window = (stat_window[0] + stat_window[1] + stat_window[2]).transpose(1, 0, 2, 3).reshape(pairs, 4, window)
    delta_wide = jnp.repeat(delta, HEAD_DIM, axis=1)
    (grad_queries,) = attention_call(
        partial(query_kernel, first),
        grid,
        [q_own, k_all, v_all, label_rows, label_all, row_block, row_block, row_block],
        [row_block],
        [jax.ShapeDtypeStruct((2 * rows, half), bf16)],
        [pltpu.VMEM((2, BLK, PAIR), f32)],
        3 * share,
    )(lo, hi, projected, projected, projected, query_label[:, None], key_label[None], grad_pair, lse, delta_wide)
    stat_spec = pl.BlockSpec((1, 4, window), lambda h, b, lo, hi: (h, 0, 0))
    do_all = pl.BlockSpec((window, PAIR), lambda h, b, lo, hi: (0, h))
    grad_keys, grad_values = attention_call(
        partial(key_kernel, first),
        grid,
        [q_all, k_own, v_own, label_all, label_rows, do_all, stat_spec],
        [row_block, row_block],
        [jax.ShapeDtypeStruct((2 * rows, half), bf16)] * 2,
        [pltpu.VMEM((2, BLK, PAIR), f32)] * 2,
        4 * share,
    )(lo, hi, projected, projected, projected, query_label[None], key_label[:, None], grad_window, stat_window)

    normed_pair = normed_window[first_row:last_row]
    chip_bits = bits[:-1]
    sums = [
        scatter_sum(inner_rows(normed_pair, g).astype(bf16).reshape((2,) * (depth - 1) + (2 * shard, half)), chip_bits, order_of(turn, []))
        for turn, g in enumerate((grad_queries, grad_keys, grad_values))
    ]
    chip_rows = jnp.concatenate(sums, axis=1)
    kept = lax.dynamic_slice_in_dim(chip_rows, core * shard, shard, 0)
    other = swap(lax.dynamic_slice_in_dim(chip_rows, (1 - core) * shard, shard, 0), 0)
    query_out, key_out, value_out = [
        columns_of(core, kept[:, i * half : (i + 1) * half], other[:, i * half : (i + 1) * half]).astype(f32)
        for i in range(3)
    ]

    grad_all = jnp.concatenate([grad_queries, grad_keys, grad_values], axis=1)
    grad_normed_pair = against(grad_all, weight_qkv)
    grad_normed = lax.dynamic_slice_in_dim(grad_normed_pair, core * rows, rows, 0) + swap(
        lax.dynamic_slice_in_dim(grad_normed_pair, (1 - core) * rows, rows, 0), 0
    )
    _, first_norm_back = jax.vjp(layer_norm, inputs, gain_first, bias_first)
    grad_input_norm, first_gain_grad, first_bias_grad = first_norm_back(grad_normed)
    input_gradient = grad_middle + grad_input_norm

    def placed_half(values):
        spread = jnp.zeros((width,), f32)
        return lax.dynamic_update_slice_in_dim(spread, values, core * half, 0)

    grads = [
        first_gain_grad,
        first_bias_grad,
        placed_half(column_sums(grad_queries)),
        placed_half(column_sums(grad_values)),
        output_bias_grad,
        attention_scale_grad,
        second_gain_grad,
        second_bias_grad,
        project_bias_grad,
        dense_scale_grad,
        hidden_bias_grad,
    ]
    vector_rows = jnp.concatenate([g.reshape(count, -1) for g in grads], axis=1)
    vector_rows = jnp.pad(vector_rows, ((0, 0), (0, -vector_rows.shape[1] % 128)))
    vector_sum = scatter_sum(vector_rows.reshape((2,) * depth + (1, -1)), bits, bits, f32)[0]
    out = [vector_sum[i * shard : (i + 1) * shard] for i in range(10)]
    hidden_bias_out = vector_sum[10 * shard : (10 + parts) * shard]
    c_rows = sum_c.astype(f32)
    rest_width = width - cut
    project_out = jnp.concatenate(
        [sum_a.astype(f32), jnp.concatenate([c_rows[:, j * rest_width : (j + 1) * rest_width] for j in range(parts)])], axis=1
    )
    hidden_out = jnp.concatenate([sum_b.astype(f32), c_rows[:, width : 2 * width]], axis=1)
    output_out = c_rows[:, 2 * width :]
    return (
        layer_output,
        input_gradient,
        out[0],
        out[1],
        query_out,
        out[2],
        key_out,
        value_out,
        out[3],
        output_out,
        out[4],
        out[5],
        out[6],
        out[7],
        hidden_out,
        hidden_bias_out,
        project_out,
        out[8],
        out[9],
    )


def solution(mesh):
    placed = (
        P("dev", None),
        P("dev", None),
        P("dev"),
        P("dev"),
        P("dev"),
        P("dev"),
        P("dev", None),
        P("dev"),
        P("dev", None),
        P("dev", None),
        P("dev"),
        P("dev", None),
        P("dev"),
        P("dev"),
        P("dev"),
        P("dev"),
        P("dev", None),
        P("dev"),
        P("dev", None),
        P("dev"),
        P("dev"),
    )
    return jax.shard_map(
        on_device,
        mesh=mesh,
        in_specs=placed,
        out_specs=(
            P("dev", None),
            P("dev", None),
            P("dev"),
            P("dev"),
            P("dev", None),
            P("dev"),
            P("dev", None),
            P("dev", None),
            P("dev"),
            P("dev", None),
            P("dev"),
            P("dev"),
            P("dev"),
            P("dev"),
            P("dev", None),
            P("dev"),
            P("dev", None),
            P("dev"),
            P("dev"),
        ),
        check_vma=False,
    )
```

time: 1740 us -> 896 us (0.51)
  waiting for transfers between devices: 675 us -> 292 us
  matrix products: 319 us -> 119 us
  blocking collectives: 181 us -> 0 us
  Pallas kernels: 0 us -> 179 us
  starting transfers between devices: 250 us -> 106 us
  other arithmetic: 171 us -> 48.4 us
    reduce_scatter x6 -> x0, waiting for transfers between devices: 552 us -> none  [the longest x1 187 us: on_device(): lax.psum_scatter(project_weight_grad, 'dev', scatter_dimension=0, tiled=T...]
    dot_general x74 -> x14, matrix products: 319 us -> 119 us  [the longest x4 62 us: product(): return jnp.dot(a, b, preferred_element_type=f32)]
    ppermute x18 -> x44, waiting for transfers between devices: 58.2 us -> 246 us  [the longest x37 161 us: swap(): return lax.ppermute(block, 'dev', [(i, i ^ 1 << bit) for i in range(count)])]
    pallas_call x0 -> x3, Pallas kernels: none -> 179 us  [the longest x1 63.1 us: on_device(): attention_call(partial(key_kernel, first), grid, [q_all, k_own, v_own, la...]
    unnamed x2 -> x0, blocking collectives: 144 us -> none
    ppermute x18 -> x44, starting transfers between devices: 250 us -> 106 us  [the longest x37 87.9 us: swap(): return lax.ppermute(block, 'dev', [(i, i ^ 1 << bit) for i in range(count)])]
    convert_element_type x22 -> x35, other arithmetic: 72.3 us -> 22.7 us  [the longest x24 13.5 us: scatter_sum(): block = block.astype(bf16)]
    all_gather x1 -> x0, blocking collectives: 37.9 us -> none  [on_device(): lax.all_gather(hidden_bias, 'dev', axis=0, tiled=True)]
  transfers between devices with their start and end apart: 30 -> 46, of which waited for: 12 -> 32; matrix products, arithmetic and copies ran while one was open for 33% -> 17% of each run, Pallas kernels for 0% -> 20%
where the time goes in v1:
time: 896 us; the launch traced here: 879 us
  waiting for transfers between devices  292 us (33%)
  Pallas kernels  179 us (20%)
  local copies, waits for them, and re-layouts  119 us (13%)
  matrix products  119 us (13%)
  starting transfers between devices  106 us (12%)
  other arithmetic  48.4 us (5%)
  between operations  16 us (2%)
    ppermute x37, waiting for transfers between devices, swap(): return lax.ppermute(block, 'dev', [(i, i ^ 1 << bit) for i in range(count)])  161 us
    ppermute x37, starting transfers between devices, swap(): return lax.ppermute(block, 'dev', [(i, i ^ 1 << bit) for i in range(count)])  87.9 us
    ppermute x6, waiting for transfers between devices, shifted(): lax.ppermute(block, 'dev', [(i, i + distance) for i in range(count) if 0...  73.2 us
    pallas_call x1, Pallas kernels, on_device(): attention_call(partial(key_kernel, first), grid, [q_all, k_own, v_own, la...  63.1 us
    dot_general x4, matrix products, product(): return jnp.dot(a, b, preferred_element_type=f32)  62 us
    pallas_call x1, Pallas kernels, on_device(): attention_call(partial(query_kernel, first), grid, [q_own, k_all, v_all,...  60.8 us
    unnamed x167, local copies, waits for them, and re-layouts  56.8 us
    pallas_call x1, Pallas kernels, on_device(): attention_call(partial(attend_kernel, first), grid, [q_own, k_all, v_all,...  54.6 us
  transfers between devices with their start and end apart: 46, of which 32 were waited for; matrix products, arithmetic and copies ran while one was open for 17% of the time, Pallas kernels for 20%

profile of v1, /device:TPU:0, one launch (start us, length us, event | category | flops | bytes accessed | tf_op | source)
XLA Modules:
  0.0 879.0 jit_solution(4460950649374383244)
XLA Ops:
  25.2 5.5 collective-permute-start
  30.8 11.8 %collective-permute-done.2 = bf16[528,1024]{1,0:T(8,128)(2,1)S(1)} collective-permute-done((bf16[528,1024]{1,0:T(8,128)(2,1)S(1)}, bf16[528,1024]{1,0:T(8,128)(2,1)S(1)}, u32[]{:S(2)}, u32[]{:S(2)}) %collective-permute-start.2) | collective-permute-done | bytes 1081376 | tf_op jit(solution)/shard_map/ppermute | solution.py:278
  42.6 12.0 %collective-permute-done.1 = bf16[528,1024]{1,0:T(8,128)(2,1)S(1)} collective-permute-done((bf16[528,1024]{1,0:T(8,128)(2,1)S(1)}, bf16[528,1024]{1,0:T(8,128)(2,1)S(1)}, u32[]{:S(2)}, u32[]{:S(2)}) %collective-permute-start.1) | collective-permute-done | bytes 1081376 | tf_op jit(solution)/shard_map/ppermute | solution.py:179
  54.6 22.7 %collective-permute-done = bf16[528,1024]{1,0:T(8,128)(2,1)S(1)} collective-permute-done((bf16[528,1024]{1,0:T(8,128)(2,1)S(1)}, bf16[528,1024]{1,0:T(8,128)(2,1)S(1)}, u32[]{:S(2)}, u32[]{:S(2)}) %collective-permute-start) | collective-permute-done | bytes 1081376 | tf_op jit(solution)/shard_map/ppermute | solution.py:179
  80.7 7.3 collective-permute-done.3
  112.2 26.9 %all-gather.3.cloned.1.call-done = bf16[1024,4224]{1,0:T(8,128)(2,1)} async-done(((bf16[32,4224]{1,0:T(8,128)(2,1)}), bf16[1024,4224]{1,0:T(8,128)(2,1)}) %all-gather.3.cloned.1.call-update) | async-done | bytes 8650768 | tf_op jit(solution)/shard_map/all_gather | solution.py:267
  142.8 5.9 fusion.5
  148.7 19.8 %multiply_convert_fusion.q_ref.k_ref.v_ref = bf16[4096,1536]{1,0:T(8,128)(2,1)} fusion(bf16[4096,1024]{1,0:T(8,128)(2,1)S(1)} %fusion.5, f32[1536]{0:T(1024)S(1)} %copy-done.55, f32[1536]{0:T(1024)S(1)} %pad_maximum_fusion.9, bf16[1024,4224]{1,0:T(8,128)(2,1)} %all-gather.3.cloned.1.call-done, s32[]{:T(128)S(6)} %select_n.262), kind=kOutput, calls=%fused_computation | convolution fusion | flops 12903776256 | bytes 24129540 | tf_op jit(solution)/shard_map/dot_general | solution.py:30
  168.5 54.6 %shard_map.348 = (f32[1024,512]{1,0:T(8,128)S(1)}, f32[1024,512]{1,0:T(8,128)S(1)}) custom-call(s32[4]{0:T(128)S(1)} %get-tuple-element.136.lo, s32[4]{0:T(128)S(1)} %get-tuple-element.137.hi, bf16[4096,1536]{1,0:T(8,128)(2,1)} %multiply_convert_fusion.q_ref.k_ref.v_ref, bf16[4096,1536]{1,0:T(8,128)(2,1)} %multiply_convert_fusion.q_ref.k_ref.v_ref, ...), custom_call_target="tpu_custom_call" | custom-call | flops 2936012800 | bytes 20000000 | tf_op jit(solution)/shard_map/pallas_call | solution.py:342
  230.3 4.9 fusion.132
  236.5 19.5 %all-gather.5.cloned.1.call-done = bf16[8192,1024]{1,0:T(8,128)(2,1)} async-done(((bf16[256,1024]{1,0:T(8,128)(2,1)}), bf16[8192,1024]{1,0:T(8,128)(2,1)}) %all-gather.5.cloned.1.call-update) | async-done | bytes 16777232 | tf_op jit(solution)/shard_map/all_gather | solution.py:268
  256.1 9.6 %fusion.133 = (bf16[32,128,1024]{2,1,0:T(8,128)(2,1)}, bf16[32,128,1024]{2,1,0:T(8,128)(2,1)S(1)}) fusion(bf16[32,256,1024]{2,1,0:T(8,128)(2,1)} %bitcast.324), kind=kLoop, calls=%fused_computation.384 | loop fusion | bytes 33554432 | tf_op jit(solution)/shard_map/slice | solution.py:376
  265.7 7.6 copy.129
  273.3 12.1 %copy.174 = bf16[128,8,4,1024]{3,1,2,0:T(8,128)(2,1)} copy(bf16[128,8,4,1024]{3,2,1,0:T(4,128)(2,1)} %bitcast.318) | data formatting | bytes 16777216
  285.4 27.9 %multiply_convert_fusion.1 = (bf16[512,4096]{1,0:T(8,128)(2,1)}, f32[512,4096]{1,0:T(8,128)}, f32[512,4096]{1,0:T(8,128)}) fusion(f32[4096]{0:T(1024)S(1)} %add.435, bf16[1024,4096]{1,0:T(8,128)(2,1)} %bitcast.325, f32[512,1024]{1,0:T(8,128)S(1)} %get-tuple-element.58, f32[1024]{0:T(1024)S(1)} %get-tuple-element.40, f32[1024]{0:T(1024)S(1)} %get-tuple-element.41, ...), kind=kOutput, calls=%fused_computation.13 | convolution fusion | flops 4436000768 | bytes 31485952 | tf_op jit(solution)/shard_map/dot_general | solution.py:30
  313.3 15.7 %convert_reduce_fusion.1 = (f32[4096]{0:T(1024)}, bf16[512,4096]{1,0:T(8,128)(2,1)}) fusion(f32[512,4096]{1,0:T(8,128)} %get-tuple-element.56, bf16[4096,1024]{1,0:T(8,128)(2,1)} %bitcast.328, bf16[512,1024]{1,0:T(8,128)(2,1)S(1)} %copy-done.39, f32[1024]{0:T(1024)S(1)} %get-tuple-element.38, f32[512,4096]{1,0:T(8,128)} %get-tuple-element.130, ...), kind=kOutput, calls=%fused_computation.11 | convolution fusion | flops 4332187648 | bytes 30445568 | tf_op jit(solution)/shard_map/dot_general | solution.py:38
  329.0 8.3 multiply_reduce_fusion
  337.3 7.2 convolution_convert_fusion
  344.6 4.2 copy-done.17
  349.8 5.3 convolution_convert_fusion.1
  355.1 3.5 copy-done.16
  398.5 60.8 %shard_map.349 = bf16[1024,512]{1,0:T(8,128)(2,1)S(1)} custom-call(s32[4]{0:T(128)S(1)} %copy-done.10, s32[4]{0:T(128)S(1)} %copy-done.12, bf16[4096,1536]{1,0:T(8,128)(2,1)} %multiply_convert_fusion.q_ref.k_ref.v_ref, bf16[4096,1536]{1,0:T(8,128)(2,1)} %multiply_convert_fusion.q_ref.k_ref.v_ref, bf16[4096,1536]{1,0:T(8,128)(2,1)} %multiply_convert_fusion.q_ref.k_ref.v_ref, ...), custom_call_target="tpu_custom_call" | custom-call | flops 4404019200 | bytes 20000000 | tf_op jit(solution)/shard_map/pallas_call | solution.py:449
  459.3 3.3 fusion.49
  463.5 5.9 collective-permute-start.16
  470.4 5.0 collective-permute-start.6
  476.6 5.5 collective-permute-done.16
  486.6 7.0 collective-permute-done.17
  498.2 3.4 collective-permute-done.18
  508.2 11.4 %collective-permute-done.7 = bf16[1120,512]{1,0:T(8,128)(2,1)S(1)} collective-permute-done((bf16[1120,512]{1,0:T(8,128)(2,1)S(1)}, bf16[1120,512]{1,0:T(8,128)(2,1)S(1)}, u32[]{:S(2)}, u32[]{:S(2)}) %collective-permute-start.7) | collective-permute-done | bytes 1146912 | tf_op jit(solution)/shard_map/ppermute | solution.py:179
  521.0 27.2 %collective-permute-done.8 = bf16[1120,512]{1,0:T(8,128)(2,1)S(1)} collective-permute-done((bf16[1120,512]{1,0:T(8,128)(2,1)S(1)}, bf16[1120,512]{1,0:T(8,128)(2,1)S(1)}, u32[]{:S(2)}, u32[]{:S(2)}) %collective-permute-start.8) | collective-permute-done | bytes 1146912 | tf_op jit(solution)/shard_map/ppermute | solution.py:179
  555.6 63.1 %shard_map.350 = (bf16[1024,512]{1,0:T(8,128)(2,1)S(1)}, bf16[1024,512]{1,0:T(8,128)(2,1)S(1)}) custom-call(s32[4]{0:T(128)S(1)} %copy-done.10, s32[4]{0:T(128)S(1)} %copy-done.12, bf16[4096,1536]{1,0:T(8,128)(2,1)} %multiply_convert_fusion.q_ref.k_ref.v_ref, bf16[4096,1536]{1,0:T(8,128)(2,1)} %multiply_convert_fusion.q_ref.k_ref.v_ref, ...), custom_call_target="tpu_custom_call" | custom-call | flops 5872025600 | bytes 20000000 | tf_op jit(solution)/shard_map/pallas_call | solution.py:460
  622.6 39.5 %collective-permute-start.24 = (bf16[2,2,2,64,512]{4,3,0,1,2:T(8,128)(2,1)S(1)}, bf16[2,2,2,64,512]{4,3,0,1,2:T(8,128)(2,1)S(1)}, u32[]{:S(2)}, u32[]{:S(2)}) collective-permute-start(bf16[2,2,2,64,512]{4,3,0,1,2:T(8,128)(2,1)S(1)} %bitcast.349), channel_id=1, source_target_pairs={{0,8},{1,9},{2,10},{3,11},{4,12},{5,13},{6,14},{7,15},{8,0},{9,1},... | collective-permute-start | bytes 1572872 | tf_op jit(solution)/shard_map/ppermute | solution.py:174
  666.2 5.3 fusion.15
  672.1 3.3 collective-permute-done.20
  675.6 6.2 collective-permute-done.25
  682.7 5.5 collective-permute-done.21
  688.5 4.6 collective-permute-done.26
  693.2 4.9 collective-permute-done.22
  698.1 4.4 collective-permute-start.27
  713.5 3.2 fusion.14
  719.9 9.5 %fusion.35 = (f32[1024]{0:T(1024)S(1)}, f32[1024]{0:T(1024)S(1)}, f32[1024]{0:T(1024)S(1)}, f32[512,1024]{1,0:T(8,128)}, bf16[512,1024]{1,0:T(8,128)(2,1)}) fusion(bf16[512,1024]{1,0:T(8,128)(2,1)S(1)} %copy-done.40, f32[1024]{0:T(1024)S(1)} %copy-done.52, f32[512,1024]{1,0:T(8,128)S(1)} %copy-done.56, f32[1024]{0:T(1024)S(1)} %copy-done.54, ...), kind=kOutput, calls=%fused_computation.76 | convolution fusion | flops 4308071424 | bytes 26253312 | tf_op jit(solution)/shard_map/dot_general | solution.py:30
  740.5 29.6 %collective-permute-done.12 = f32[2,2,2,1,512]{4,2,1,0,3:T(2,128)S(1)} collective-permute-done((f32[2,2,2,1,512]{4,2,1,0,3:T(2,128)S(1)}, f32[2,2,2,1,512]{4,2,1,0,3:T(2,128)S(1)}, u32[]{:S(2)}, u32[]{:S(2)}) %collective-permute-start.12) | collective-permute-done | bytes 16416 | tf_op jit(solution)/shard_map/ppermute | solution.py:174
  782.1 25.4 %collective-permute-done.35 = bf16[2,2,2,32,3072]{4,3,0,2,1:T(8,128)(2,1)S(1)} collective-permute-done((bf16[2,2,2,32,3072]{4,3,0,2,1:T(8,128)(2,1)S(1)}, bf16[2,2,2,32,3072]{4,3,0,2,1:T(8,128)(2,1)S(1)}, u32[]{:S(2)}, u32[]{:S(2)}) %collective-permute-start.35) | collective-permute-done | bytes 1572896 | tf_op jit(solution)/shard_map/ppermute | solution.py:174
  809.7 5.4 collective-permute-done.40
  817.5 14.1 %collective-permute-done.31 = bf16[2,2,32,3072]{3,2,0,1:T(8,128)(2,1)S(1)} collective-permute-done((bf16[2,2,32,3072]{3,2,0,1:T(8,128)(2,1)S(1)}, bf16[2,2,32,3072]{3,2,0,1:T(8,128)(2,1)S(1)}, u32[]{:S(2)}, u32[]{:S(2)}) %collective-permute-start.31) | collective-permute-done | bytes 786464 | tf_op jit(solution)/shard_map/ppermute | solution.py:174
  837.4 5.5 collective-permute-done.32
  847.7 16.2 %collective-permute-done.33 = bf16[32,3072]{1,0:T(8,128)(2,1)S(1)} collective-permute-done((bf16[32,3072]{1,0:T(8,128)(2,1)S(1)}, bf16[32,3072]{1,0:T(8,128)(2,1)S(1)}, u32[]{:S(2)}, u32[]{:S(2)}) %collective-permute-start.33) | collective-permute-done | bytes 196640 | tf_op jit(solution)/shard_map/ppermute | solution.py:174
  864.7 3.5 collective-permute-done.38
  (423 shorter events, 192.0 us)
Async XLA Ops:
  7.2 131.9 %all-gather.3.cloned.1.call-start = ((), (), s32[]{:S(2)}) async-start(), calls=%async_computation | async-start | bytes 8921088 | tf_op jit(solution)/shard_map/all_gather | solution.py:267
  15.8 240.3 %all-gather.5.cloned.1.call-start = ((), (), s32[]{:S(2)}) async-start(), calls=%async_computation.1 | async-start | bytes 17301504 | tf_op jit(solution)/shard_map/all_gather | solution.py:268
  22.6 19.9 %collective-permute-start.2 = (bf16[528,1024]{1,0:T(8,128)(2,1)S(1)}, bf16[528,1024]{1,0:T(8,128)(2,1)S(1)}, u32[]{:S(2)}, u32[]{:S(2)}) collective-permute-start(bf16[528,1024]{1,0:T(8,128)(2,1)S(1)} %get-tuple-element.78), channel_id=1, source_target_pairs={{4,0},{6,2},{8,4},{10,6},{12,8},{14,10},{16,12},{18,14},{20,16},{2... | collective-permute-start | bytes 3244040 | tf_op jit(solution)/shard_map/ppermute | solution.py:278
  23.9 30.6 %collective-permute-start.1 = (bf16[528,1024]{1,0:T(8,128)(2,1)S(1)}, bf16[528,1024]{1,0:T(8,128)(2,1)S(1)}, u32[]{:S(2)}, u32[]{:S(2)}) collective-permute-start(bf16[528,1024]{1,0:T(8,128)(2,1)S(1)} %get-tuple-element.78), channel_id=1, source_target_pairs={{2,0},{3,1},{4,2},{5,3},{6,4},{7,5},{8,6},{9,7},{10,8},{11,9},{12,... | collective-permute-start | bytes 3244040 | tf_op jit(solution)/shard_map/ppermute | solution.py:179
  25.2 52.0 %collective-permute-start = (bf16[528,1024]{1,0:T(8,128)(2,1)S(1)}, bf16[528,1024]{1,0:T(8,128)(2,1)S(1)}, u32[]{:S(2)}, u32[]{:S(2)}) collective-permute-start(bf16[528,1024]{1,0:T(8,128)(2,1)S(1)} %get-tuple-element.78), channel_id=1, source_target_pairs={{0,2},{1,3},{2,4},{3,5},{4,6},{5,7},{6,8},{7,9},{8,10},{9,11},{10,... | collective-permute-start | bytes 3244040 | tf_op jit(solution)/shard_map/ppermute | solution.py:179
  79.7 8.3 collective-permute-start.3
  142.5 87.8 %copy-start.53 = (f32[1024]{0:T(1024)}, f32[1024]{0:T(1024)S(1)}, u32[]{:S(2)}) copy-start(f32[1024]{0:T(1024)S(1)} %get-tuple-element.42) | copy-start | bytes 12292
  225.8 4.5 collective-permute-start.4
  235.1 123.5 %copy-start.27 = (f32[512,1024]{1,0:T(8,128)}, f32[512,1024]{1,0:T(8,128)S(1)}, u32[]{:S(2)}) copy-start(f32[512,1024]{1,0:T(8,128)S(1)} %get-tuple-element.58) | copy-start | bytes 6291460
  364.1 22.5 %collective-permute-start.5 = (bf16[512,512]{1,0:T(8,128)(2,1)}, bf16[512,512]{1,0:T(8,128)(2,1)}, u32[]{:S(2)}, u32[]{:S(2)}) collective-permute-start(bf16[512,512]{1,0:T(8,128)(2,1)} %get-tuple-element.87), channel_id=1, source_target_pairs={{0,1},{1,0},{2,3},{3,2},{4,5},{5,4},{6,7},{7,6},{8,9},{9,8},{10,11... | collective-permute-start | bytes 1572872 | tf_op jit(solution)/shard_map/ppermute | solution.py:174
  374.1 339.4 %collective-permute-start.29 = (bf16[2,2,2,2,32,3072]{5,4,0,2,3,1:T(8,128)(2,1)}, bf16[2,2,2,2,32,3072]{5,4,0,2,3,1:T(8,128)(2,1)}, u32[]{:S(2)}, u32[]{:S(2)}) collective-permute-start(bf16[2,2,2,2,32,3072]{5,4,0,2,3,1:T(8,128)(2,1)} %bitcast.310), channel_id=1, source_target_pairs={{0,1},{1,0},{2,3},{3,2},{4,5},{5,4},{6,7},{7,6},{8,9},{9,8},{10,11... | collective-permute-start | bytes 9437192 | tf_op jit(solution)/shard_map/ppermute | solution.py:174
  380.4 357.1 %collective-permute-start.34 = (bf16[2,2,2,2,32,3072]{5,4,0,3,1,2:T(8,128)(2,1)}, bf16[2,2,2,2,32,3072]{5,4,0,3,1,2:T(8,128)(2,1)}, u32[]{:S(2)}, u32[]{:S(2)}) collective-permute-start(bf16[2,2,2,2,32,3072]{5,4,0,3,1,2:T(8,128)(2,1)} %bitcast.312), channel_id=1, source_target_pairs={{0,1},{1,0},{2,3},{3,2},{4,5},{5,4},{6,7},{7,6},{8,9},{9,8},{10,11... | collective-permute-start | bytes 9437192 | tf_op jit(solution)/shard_map/ppermute | solution.py:174
  386.3 387.7 %collective-permute-start.39 = (bf16[2,2,2,2,128,768]{5,4,0,1,2,3:T(8,128)(2,1)}, bf16[2,2,2,2,128,768]{5,4,0,1,2,3:T(8,128)(2,1)}, u32[]{:S(2)}, u32[]{:S(2)}) collective-permute-start(bf16[2,2,2,2,128,768]{5,4,0,1,2,3:T(8,128)(2,1)} %bitcast.311), channel_id=1, source_target_pairs={{0,1},{1,0},{2,3},{3,2},{4,5},{5,4},{6,7},{7,6},{8,9},{9,8},{10,11... | collective-permute-start | bytes 9437192 | tf_op jit(solution)/shard_map/ppermute | solution.py:174
  463.5 18.6 %collective-permute-start.16 = (bf16[2,2,2,64,512]{4,3,0,1,2:T(8,128)(2,1)}, bf16[2,2,2,64,512]{4,3,0,1,2:T(8,128)(2,1)}, u32[]{:S(2)}, u32[]{:S(2)}) collective-permute-start(bf16[2,2,2,64,512]{4,3,0,1,2:T(8,128)(2,1)} %bitcast.315), channel_id=1, source_target_pairs={{0,2},{1,3},{2,0},{3,1},{4,6},{5,7},{6,4},{7,5},{8,10},{9,11},{10,... | collective-permute-start | bytes 1572872 | tf_op jit(solution)/shard_map/ppermute | solution.py:174
  470.4 25.8 %collective-permute-start.6 = (bf16[560,512]{1,0:T(8,128)(2,1)}, bf16[560,512]{1,0:T(8,128)(2,1)S(1)}, u32[]{:S(2)}, u32[]{:S(2)}) collective-permute-start(bf16[560,512]{1,0:T(8,128)(2,1)} %pad_maximum_fusion.3), channel_id=1, source_target_pairs={{0,4},{1,5},{2,6},{3,7},{4,8},{5,9},{6,10},{7,11},{8,12},{9,13},{1... | collective-permute-start | bytes 1720328 | tf_op jit(solution)/shard_map/ppermute | solution.py:179
  483.3 10.2 %collective-permute-start.17 = (bf16[2,2,64,512]{3,2,0,1:T(8,128)(2,1)S(1)}, bf16[2,2,64,512]{3,2,0,1:T(8,128)(2,1)S(1)}, u32[]{:S(2)}, u32[]{:S(2)}) collective-permute-start(bf16[2,2,64,512]{3,2,0,1:T(8,128)(2,1)S(1)} %dynamic-slice_bitcast_fusion.11), channel_id=1, source_target_pairs={{0,4},{1,5},{2,6},{3,7},{4,0},{5,1},{6,2},{7,3},{8,12},{9,13},{10,... | collective-permute-start | bytes 786440 | tf_op jit(solution)/shard_map/ppermute | solution.py:174
  493.5 26.0 %collective-permute-start.7 = (bf16[1120,512]{1,0:T(8,128)(2,1)S(1)}, bf16[1120,512]{1,0:T(8,128)(2,1)S(1)}, u32[]{:S(2)}, u32[]{:S(2)}) collective-permute-start(bf16[1120,512]{1,0:T(8,128)(2,1)S(1)} %pad_maximum_fusion.1), channel_id=1, source_target_pairs={{0,2},{1,3},{2,4},{3,5},{4,6},{5,7},{6,8},{7,9},{8,10},{9,11},{10,... | collective-permute-start | bytes 3440648 | tf_op jit(solution)/shard_map/ppermute | solution.py:179
  496.2 5.3 collective-permute-start.18
  501.6 5.2 collective-permute-start.19
  506.8 41.4 %collective-permute-start.8 = (bf16[1120,512]{1,0:T(8,128)(2,1)S(1)}, bf16[1120,512]{1,0:T(8,128)(2,1)S(1)}, u32[]{:S(2)}, u32[]{:S(2)}) collective-permute-start(bf16[1120,512]{1,0:T(8,128)(2,1)S(1)} %pad_maximum_fusion.1), channel_id=1, source_target_pairs={{2,0},{3,1},{4,2},{5,3},{6,4},{7,5},{8,6},{9,7},{10,8},{11,9},{12,... | collective-permute-start | bytes 3440648 | tf_op jit(solution)/shard_map/ppermute | solution.py:179
  519.5 28.7 %collective-permute-start.9 = (bf16[560,512]{1,0:T(8,128)(2,1)S(1)}, bf16[560,512]{1,0:T(8,128)(2,1)S(1)}, u32[]{:S(2)}, u32[]{:S(2)}) collective-permute-start(bf16[560,512]{1,0:T(8,128)(2,1)S(1)} %pad_maximum_fusion.4), channel_id=1, source_target_pairs={{4,0},{5,1},{6,2},{7,3},{8,4},{9,5},{10,6},{11,7},{12,8},{13,9},{1... | collective-permute-start | bytes 1720328 | tf_op jit(solution)/shard_map/ppermute | solution.py:179
  622.6 49.2 %collective-permute-start.24 = (bf16[2,2,2,64,512]{4,3,0,1,2:T(8,128)(2,1)S(1)}, bf16[2,2,2,64,512]{4,3,0,1,2:T(8,128)(2,1)S(1)}, u32[]{:S(2)}, u32[]{:S(2)}) collective-permute-start(bf16[2,2,2,64,512]{4,3,0,1,2:T(8,128)(2,1)S(1)} %bitcast.349), channel_id=1, source_target_pairs={{0,8},{1,9},{2,10},{3,11},{4,12},{5,13},{6,14},{7,15},{8,0},{9,1},... | collective-permute-start | bytes 1572872 | tf_op jit(solution)/shard_map/ppermute | solution.py:174
  665.2 10.2 %collective-permute-start.20 = (bf16[2,2,2,64,512]{4,3,0,2,1:T(8,128)(2,1)S(1)}, bf16[2,2,2,64,512]{4,3,0,2,1:T(8,128)(2,1)S(1)}, u32[]{:S(2)}, u32[]{:S(2)}) collective-permute-start(bf16[2,2,2,64,512]{4,3,0,2,1:T(8,128)(2,1)S(1)} %bitcast.350), channel_id=1, source_target_pairs={{0,4},{1,5},{2,6},{3,7},{4,0},{5,1},{6,2},{7,3},{8,12},{9,13},{10,... | collective-permute-start | bytes 1572872 | tf_op jit(solution)/shard_map/ppermute | solution.py:174
  671.8 44.8 %collective-permute-start.10 = (f32[512,1024]{1,0:T(8,128)S(1)}, f32[512,1024]{1,0:T(8,128)S(1)}, u32[]{:S(2)}, u32[]{:S(2)}) collective-permute-start(f32[512,1024]{1,0:T(8,128)S(1)} %constant_dynamic-slice_fusion.22), channel_id=1, source_target_pairs={{0,1},{1,0},{2,3},{3,2},{4,5},{5,4},{6,7},{7,6},{8,9},{9,8},{10,11... | collective-permute-start | bytes 6291464 | tf_op jit(solution)/shard_map/ppermute | solution.py:174
  675.4 6.4 collective-permute-start.25
  681.8 6.4 collective-permute-start.21
  688.1 5.0 collective-permute-start.26
  693.1 5.0 collective-permute-start.22
  698.1 6.6 collective-permute-start.27
  704.7 5.3 collective-permute-start.23
  710.0 1.4 collective-permute-start.28
  730.0 5.3 collective-permute-start.11
  733.1 47.3 %collective-permute-start.30 = (bf16[2,2,2,32,3072]{4,3,0,1,2:T(8,128)(2,1)S(1)}, bf16[2,2,2,32,3072]{4,3,0,1,2:T(8,128)(2,1)S(1)}, u32[]{:S(2)}, u32[]{:S(2)}) collective-permute-start(bf16[2,2,2,32,3072]{4,3,0,1,2:T(8,128)(2,1)S(1)} %dynamic-slice_bitcast_fusion.2), channel_id=1, source_target_pairs={{0,8},{1,9},{2,10},{3,11},{4,12},{5,13},{6,14},{7,15},{8,0},{9,1},... | collective-permute-start | bytes 4718600 | tf_op jit(solution)/shard_map/ppermute | solution.py:174
  735.4 34.7 %collective-permute-start.12 = (f32[2,2,2,1,512]{4,2,1,0,3:T(2,128)S(1)}, f32[2,2,2,1,512]{4,2,1,0,3:T(2,128)S(1)}, u32[]{:S(2)}, u32[]{:S(2)}) collective-permute-start(f32[2,2,2,1,512]{4,2,1,0,3:T(2,128)S(1)} %fusion.106), channel_id=1, source_target_pairs={{0,8},{1,9},{2,10},{3,11},{4,12},{5,13},{6,14},{7,15},{8,0},{9,1},... | collective-permute-start | bytes 49160 | tf_op jit(solution)/shard_map/ppermute | solution.py:174
  770.1 3.8 collective-permute-start.13
  772.0 35.5 %collective-permute-start.35 = (bf16[2,2,2,32,3072]{4,3,0,2,1:T(8,128)(2,1)S(1)}, bf16[2,2,2,32,3072]{4,3,0,2,1:T(8,128)(2,1)S(1)}, u32[]{:S(2)}, u32[]{:S(2)}) collective-permute-start(bf16[2,2,2,32,3072]{4,3,0,2,1:T(8,128)(2,1)S(1)} %dynamic-slice_bitcast_fusion.1), channel_id=1, source_target_pairs={{0,4},{1,5},{2,6},{3,7},{4,0},{5,1},{6,2},{7,3},{8,12},{9,13},{10,... | collective-permute-start | bytes 4718600 | tf_op jit(solution)/shard_map/ppermute | solution.py:174
  773.9 3.7 collective-permute-start.14
  777.6 1.6 collective-permute-start.15
  777.8 37.3 %collective-permute-start.40 = (bf16[2,2,2,128,768]{4,3,0,1,2:T(8,128)(2,1)S(1)}, bf16[2,2,2,128,768]{4,3,0,1,2:T(8,128)(2,1)S(1)}, u32[]{:S(2)}, u32[]{:S(2)}) collective-permute-start(bf16[2,2,2,128,768]{4,3,0,1,2:T(8,128)(2,1)S(1)} %dynamic-slice_bitcast_fusion), channel_id=1, source_target_pairs={{0,2},{1,3},{2,0},{3,1},{4,6},{5,7},{6,4},{7,5},{8,10},{9,11},{10,... | collective-permute-start | bytes 4718600 | tf_op jit(solution)/shard_map/ppermute | solution.py:174
  781.1 50.4 %collective-permute-start.31 = (bf16[2,2,32,3072]{3,2,0,1:T(8,128)(2,1)S(1)}, bf16[2,2,32,3072]{3,2,0,1:T(8,128)(2,1)S(1)}, u32[]{:S(2)}, u32[]{:S(2)}) collective-permute-start(bf16[2,2,32,3072]{3,2,0,1:T(8,128)(2,1)S(1)} %dynamic-slice_bitcast_fusion.5), channel_id=1, source_target_pairs={{0,2},{1,3},{2,0},{3,1},{4,6},{5,7},{6,4},{7,5},{8,10},{9,11},{10,... | collective-permute-start | bytes 2359304 | tf_op jit(solution)/shard_map/ppermute | solution.py:174
  808.2 25.4 %collective-permute-start.36 = (bf16[2,2,32,3072]{3,2,0,1:T(8,128)(2,1)S(1)}, bf16[2,2,32,3072]{3,2,0,1:T(8,128)(2,1)S(1)}, u32[]{:S(2)}, u32[]{:S(2)}) collective-permute-start(bf16[2,2,32,3072]{3,2,0,1:T(8,128)(2,1)S(1)} %dynamic-slice_bitcast_fusion.4), channel_id=1, source_target_pairs={{0,8},{1,9},{2,10},{3,11},{4,12},{5,13},{6,14},{7,15},{8,0},{9,1},... | collective-permute-start | bytes 2359304 | tf_op jit(solution)/shard_map/ppermute | solution.py:174
  815.6 19.7 %collective-permute-start.41 = (bf16[2,2,128,768]{3,2,0,1:T(8,128)(2,1)S(1)}, bf16[2,2,128,768]{3,2,0,1:T(8,128)(2,1)S(1)}, u32[]{:S(2)}, u32[]{:S(2)}) collective-permute-start(bf16[2,2,128,768]{3,2,0,1:T(8,128)(2,1)S(1)} %dynamic-slice_bitcast_fusion.3), channel_id=1, source_target_pairs={{0,4},{1,5},{2,6},{3,7},{4,0},{5,1},{6,2},{7,3},{8,12},{9,13},{10,... | collective-permute-start | bytes 2359304 | tf_op jit(solution)/shard_map/ppermute | solution.py:174
  831.8 11.1 %collective-permute-start.32 = (bf16[2,32,3072]{2,1,0:T(8,128)(2,1)S(1)}, bf16[2,32,3072]{2,1,0:T(8,128)(2,1)S(1)}, u32[]{:S(2)}, u32[]{:S(2)}) collective-permute-start(bf16[2,32,3072]{2,1,0:T(8,128)(2,1)S(1)} %dynamic-slice_bitcast_fusion.8), channel_id=1, source_target_pairs={{0,4},{1,5},{2,6},{3,7},{4,0},{5,1},{6,2},{7,3},{8,12},{9,13},{10,... | collective-permute-start | bytes 1179656 | tf_op jit(solution)/shard_map/ppermute | solution.py:174
  833.9 10.5 %collective-permute-start.37 = (bf16[2,32,3072]{2,1,0:T(8,128)(2,1)S(1)}, bf16[2,32,3072]{2,1,0:T(8,128)(2,1)S(1)}, u32[]{:S(2)}, u32[]{:S(2)}) collective-permute-start(bf16[2,32,3072]{2,1,0:T(8,128)(2,1)S(1)} %dynamic-slice_bitcast_fusion.7), channel_id=1, source_target_pairs={{0,2},{1,3},{2,0},{3,1},{4,6},{5,7},{6,4},{7,5},{8,10},{9,11},{10,... | collective-permute-start | bytes 1179656 | tf_op jit(solution)/shard_map/ppermute | solution.py:174
  835.6 11.3 %collective-permute-start.42 = (bf16[2,128,768]{2,1,0:T(8,128)(2,1)S(1)}, bf16[2,128,768]{2,1,0:T(8,128)(2,1)S(1)}, u32[]{:S(2)}, u32[]{:S(2)}) collective-permute-start(bf16[2,128,768]{2,1,0:T(8,128)(2,1)S(1)} %dynamic-slice_bitcast_fusion.6), channel_id=1, source_target_pairs={{0,8},{1,9},{2,10},{3,11},{4,12},{5,13},{6,14},{7,15},{8,0},{9,1},... | collective-permute-start | bytes 1179656 | tf_op jit(solution)/shard_map/ppermute | solution.py:174
  843.0 20.9 %collective-permute-start.33 = (bf16[32,3072]{1,0:T(8,128)(2,1)S(1)}, bf16[32,3072]{1,0:T(8,128)(2,1)S(1)}, u32[]{:S(2)}, u32[]{:S(2)}) collective-permute-start(bf16[32,3072]{1,0:T(8,128)(2,1)S(1)} %dynamic-slice_bitcast_fusion.14), channel_id=1, source_target_pairs={{0,16},{1,17},{2,18},{3,19},{4,20},{5,21},{6,22},{7,23},{8,24},{9,... | collective-permute-start | bytes 589832 | tf_op jit(solution)/shard_map/ppermute | solution.py:174
  844.5 23.6 %collective-permute-start.38 = (bf16[32,3072]{1,0:T(8,128)(2,1)S(1)}, bf16[32,3072]{1,0:T(8,128)(2,1)S(1)}, u32[]{:S(2)}, u32[]{:S(2)}) collective-permute-start(bf16[32,3072]{1,0:T(8,128)(2,1)S(1)} %dynamic-slice_bitcast_fusion.13), channel_id=1, source_target_pairs={{0,16},{1,17},{2,18},{3,19},{4,20},{5,21},{6,22},{7,23},{8,24},{9,... | collective-permute-start | bytes 589832 | tf_op jit(solution)/shard_map/ppermute | solution.py:174
  847.0 24.0 %collective-permute-start.43 = (bf16[128,768]{1,0:T(8,128)(2,1)S(1)}, bf16[128,768]{1,0:T(8,128)(2,1)S(1)}, u32[]{:S(2)}, u32[]{:S(2)}) collective-permute-start(bf16[128,768]{1,0:T(8,128)(2,1)S(1)} %dynamic-slice_bitcast_fusion.12), channel_id=1, source_target_pairs={{0,16},{1,17},{2,18},{3,19},{4,20},{5,21},{6,22},{7,23},{8,24},{9,... | collective-permute-start | bytes 589832 | tf_op jit(solution)/shard_map/ppermute | solution.py:174
  (62 other events, 670.2 us)
Sparse Core Ops, SparseCore 0:
  15.9 123.0 all-gather.2
  142.5 113.5 all-gather.4

commit v2 on v1

--- a/solution.py
+++ b/solution.py
@@ -10,6 +10,7 @@
 PAIR = 2 * HEAD_DIM
 IMG = 1370
 BLK = 256
+STEP = 512
 norm_eps = 1e-06
 bf16 = jnp.bfloat16
 f32 = jnp.float32
@@ -22,10 +23,6 @@
     return center * lax.rsqrt(spread + norm_eps) * gain_row + bias_row
 
 
-def gelu_exact(arguments):
-    return jax.nn.gelu(arguments, approximate=False)
-
-
 def product(a, b):
     return jnp.dot(a, b, preferred_element_type=f32)
 
@@ -51,44 +48,62 @@
     return jnp.where(head_lanes(h), block, jnp.zeros_like(block))
 
 
-def offsets():
-    shape = (BLK, BLK)
+def steps_of(lo, hi, block, window):
+    per = STEP // BLK
+    steps = (hi[block] - lo[block] + per - 1) // per
+    return jnp.minimum(lo[block], window // BLK - per * steps), steps
+
+
+def apart_of():
+    shape = (BLK, STEP)
     return lax.broadcasted_iota(jnp.int32, shape, 1) - lax.broadcasted_iota(jnp.int32, shape, 0)
+
+
+def step_rows(start, step):
+    block = start + step * (STEP // BLK)
+    return block, pl.ds(pl.multiple_of(block * BLK, BLK), STEP)
+
+
+def folded(combine, block):
+    parts = [block[:, i : i + 128] for i in range(0, block.shape[1], 128)]
+    while len(parts) > 1:
+        parts = [combine(parts[i], parts[i + 1]) for i in range(0, len(parts), 2)]
+    return parts[0]
 
 
 def attend_kernel(first, lo, hi, q_ref, k_ref, v_ref, ql_ref, kl_ref, o_ref, lse_ref, s_ref, m_ref, l_ref, a_ref):
     block = pl.program_id(1)
-    start, stop = lo[block], hi[block]
-    apart = offsets()
+    start, steps = steps_of(lo, hi, block, k_ref.shape[0])
+    apart = apart_of()
     ql = ql_ref[...]
     heads = [own_head(q_ref[...], h) for h in range(2)]
     m_ref[...] = jnp.full(m_ref.shape, NEG, f32)
     l_ref[...] = jnp.zeros(l_ref.shape, f32)
     a_ref[...] = jnp.zeros(a_ref.shape, f32)
 
-    def scores(kb, _):
-        rows = pl.ds(pl.multiple_of(kb * BLK, BLK), BLK)
+    def scores(step, _):
+        kb, rows = step_rows(start, step)
         k = k_ref[rows, :]
         seen = (ql == kl_ref[:, rows]) | (apart == (first + block - kb) * BLK)
         for h in range(2):
             s = jnp.where(seen, against(heads[h], k), NEG)
-            s_ref[h, kb] = s
-            m_ref[h] = jnp.maximum(m_ref[h], jnp.maximum(s[:, :128], s[:, 128:]))
+            s_ref[h, step] = s
+            m_ref[h] = jnp.maximum(m_ref[h], folded(jnp.maximum, s))
         return 0
 
-    lax.fori_loop(start, stop, scores, 0)
+    lax.fori_loop(0, steps, scores, 0)
     peaks = [jnp.max(m_ref[h], axis=1, keepdims=True) for h in range(2)]
 
-    def values(kb, _):
-        rows = pl.ds(pl.multiple_of(kb * BLK, BLK), BLK)
+    def values(step, _):
+        _, rows = step_rows(start, step)
         v = v_ref[rows, :]
         for h in range(2):
-            p = jnp.exp(s_ref[h, kb] - peaks[h])
-            l_ref[h] = l_ref[h] + (p[:, :128] + p[:, 128:])
+            p = jnp.exp(s_ref[h, step] - peaks[h])
+            l_ref[h] = l_ref[h] + folded(jnp.add, p)
             a_ref[h] = a_ref[h] + product(p.astype(bf16), v)
         return 0
 
-    lax.fori_loop(start, stop, values, 0)
+    lax.fori_loop(0, steps, values, 0)
     totals = [jnp.sum(l_ref[h], axis=1, keepdims=True) for h in range(2)]
     first_head = head_lanes(0)
     o_ref[...] = jnp.where(first_head, a_ref[0] / totals[0], a_ref[1] / totals[1])
@@ -97,7 +112,8 @@
 
 def query_kernel(first, lo, hi, q_ref, k_ref, v_ref, ql_ref, kl_ref, do_ref, lse_ref, dl_ref, dq_ref, a_ref):
     block = pl.program_id(1)
-    apart = offsets()
+    start, steps = steps_of(lo, hi, block, k_ref.shape[0])
+    apart = apart_of()
     ql = ql_ref[...]
     q = [own_head(q_ref[...], h) for h in range(2)]
     do = [own_head(do_ref[...], h) for h in range(2)]
@@ -105,8 +121,8 @@
     delta = [dl_ref[:, h * HEAD_DIM : h * HEAD_DIM + 1] for h in range(2)]
     a_ref[...] = jnp.zeros(a_ref.shape, f32)
 
-    def step(kb, _):
-        rows = pl.ds(pl.multiple_of(kb * BLK, BLK), BLK)
+    def take(step, _):
+        kb, rows = step_rows(start, step)
         k = k_ref[rows, :]
         v = v_ref[rows, :]
         seen = (ql == kl_ref[:, rows]) | (apart == (first + block - kb) * BLK)
@@ -116,22 +132,22 @@
             a_ref[h] = a_ref[h] + product(ds, k)
         return 0
 
-    lax.fori_loop(lo[block], hi[block], step, 0)
+    lax.fori_loop(0, steps, take, 0)
     dq_ref[...] = (jnp.where(head_lanes(0), a_ref[0], a_ref[1]) * (HEAD_DIM**-0.5)).astype(bf16)
 
 
 def key_kernel(first, lo, hi, q_ref, k_ref, v_ref, ql_ref, kl_ref, do_ref, st_ref, dk_ref, dv_ref, a_ref, b_ref):
     block = pl.program_id(1)
-    pair = pl.program_id(0)
-    apart = offsets()
+    start, steps = steps_of(lo, hi, block, q_ref.shape[0])
+    apart = apart_of()
     kl = kl_ref[...]
     k = [own_head(k_ref[...], h) for h in range(2)]
     v = [own_head(v_ref[...], h) for h in range(2)]
     a_ref[...] = jnp.zeros(a_ref.shape, f32)
     b_ref[...] = jnp.zeros(b_ref.shape, f32)
 
-    def step(qb, _):
-        rows = pl.ds(pl.multiple_of(qb * BLK, BLK), BLK)
+    def take(step, _):
+        qb, rows = step_rows(start, step)
         q = q_ref[rows, :]
         do = do_ref[rows, :]
         seen = (kl == ql_ref[:, rows]) | (apart == (first + block - qb) * BLK)
@@ -144,9 +160,59 @@
             b_ref[h] = b_ref[h] + product(p.astype(bf16), do)
         return 0
 
-    lax.fori_loop(lo[block], hi[block], step, 0)
+    lax.fori_loop(0, steps, take, 0)
     dk_ref[...] = jnp.where(head_lanes(0), a_ref[0], a_ref[1]).astype(bf16)
     dv_ref[...] = jnp.where(head_lanes(0), b_ref[0], b_ref[1]).astype(bf16)
+
+
+def dense_kernel(
+    n_ref, gd_ref, wh_ref, wp_ref, bh_ref, out_ref, gn_ref, dw_ref, dbh_ref, act_ref, gh_ref
+):
+    @pl.when(pl.program_id(0) == 0)
+    def _():
+        out_ref[...] = jnp.zeros(out_ref.shape, f32)
+        gn_ref[...] = jnp.zeros(gn_ref.shape, f32)
+
+    n = n_ref[...]
+    gd = gd_ref[...]
+    for u in range(0, wh_ref.shape[2], BLK):
+        units = slice(u, u + BLK)
+        hidden = product(n, wh_ref[0, :, units]) + bh_ref[0, :, units]
+        grad = against(gd, wp_ref[0, units, :])
+        below = 0.5 + 0.5 * lax.erf(hidden * 0.7071067811865476)
+        act_ref[:, units] = (hidden * below).astype(bf16)
+        gh = grad * (below + hidden * (jnp.exp(-0.5 * hidden * hidden) * 0.3989422804014327))
+        gh_low = gh.astype(bf16)
+        gh_ref[:, units] = gh_low
+        dbh_ref[0, :, units] = jnp.sum(gh_low.astype(f32), axis=0, keepdims=True)
+        dw_ref[1, 0, units, :] = inner_rows(act_ref[:, units], gd).astype(bf16)
+        dw_ref[0, 0, :, units] = inner_rows(n, gh_low).astype(bf16)
+    out_ref[...] += product(act_ref[...], wp_ref[0])
+    gn_ref[...] += against(gh_ref[...], wh_ref[0])
+
+
+def dense_call(n, gd, weights, bias):
+    rows, width = n.shape
+    parts = weights.shape[0] // 2
+    whole = pl.BlockSpec((rows, width), lambda j: (0, 0))
+    chunk = pl.BlockSpec((1, width, width), lambda j: (j, 0, 0))
+    second = pl.BlockSpec((1, width, width), lambda j: (parts + j, 0, 0))
+    row = pl.BlockSpec((1, 1, width), lambda j: (j, 0, 0))
+    return pl.pallas_call(
+        dense_kernel,
+        grid=(parts,),
+        in_specs=[whole, whole, chunk, second, row],
+        out_specs=[whole, whole, pl.BlockSpec((2, 1, width, width), lambda j: (0, j, 0, 0)), row],
+        out_shape=[
+            jax.ShapeDtypeStruct((rows, width), f32),
+            jax.ShapeDtypeStruct((rows, width), f32),
+            jax.ShapeDtypeStruct((2, parts, width, width), bf16),
+            jax.ShapeDtypeStruct((parts, 1, width), f32),
+        ],
+        scratch_shapes=[pltpu.VMEM((rows, width), bf16)] * 2,
+        compiler_params=pltpu.CompilerParams(vmem_limit_bytes=56 * 1024 * 1024),
+        cost_estimate=pl.CostEstimate(flops=50_000_000_000, bytes_accessed=40_000_000, transcendentals=4_000_000),
+    )(n, gd, weights, weights, bias)
 
 
 def attention_call(kernel, grid, in_specs, out_specs, out_shape, scratch, flops):
@@ -161,7 +227,7 @@
         ),
         out_shape=out_shape,
         compiler_params=pltpu.CompilerParams(vmem_limit_bytes=48 * 1024 * 1024),
-        cost_estimate=pl.CostEstimate(flops=flops, bytes_accessed=20_000_000, transcendentals=12_000_000),
+        cost_estimate=pl.CostEstimate(flops=flops, bytes_accessed=8_000_000, transcendentals=0),
     )
 
 
@@ -183,23 +249,17 @@
     return lax.dynamic_index_in_dim(block, index, axis, keepdims=False)
 
 
-def scatter_sum(block, bits, order, kind=bf16):
+def scatter_sum(blocks, bits, order, kind=bf16):
     bits = list(bits)
     for bit in order:
         axis = bits.index(bit)
         mine = own_bit(bit)
-        sent = pick(block, axis, 1 - mine).astype(kind)
-        kept = pick(block, axis, mine)
+        sent = jnp.concatenate([pick(b, axis, 1 - mine) for b in blocks], axis=-2).astype(kind)
+        kept = jnp.concatenate([pick(b, axis, mine) for b in blocks], axis=-2)
         block = kept.astype(f32) + swap(sent, bit).astype(f32)
-        if kind == bf16:
-            block = block.astype(bf16)
+        blocks = [block.astype(kind)]
         bits.remove(bit)
-    return block
-
-
-def bit_view(block, count, lead):
-    depth = count.bit_length() - 1
-    return block.reshape((2,) * depth + (lead,) + block.shape[1:])
+    return blocks[0]
 
 
 def on_device(
@@ -261,11 +321,10 @@
         + [output_weight, vectors],
         axis=1,
     )
-    dense_pack = jnp.concatenate(
-        [hidden_weight[:, j * width : (j + 1) * width] for j in range(parts)] + [project_weight], axis=0
-    )
+    hidden_local = hidden_weight.reshape(shard, count, parts, shard).transpose(2, 0, 1, 3).reshape(parts, shard, width)
+    dense_pack = jnp.concatenate([hidden_local, project_weight.reshape(parts, shard, width)])
     attention_full = lax.all_gather(attention_pack, "dev", axis=0, tiled=True)
-    dense_full = lax.all_gather(dense_pack, "dev", axis=0, tiled=True).reshape(count, -1, width)
+    dense_full = lax.all_gather(dense_pack, "dev", axis=1, tiled=True)
 
     labels = segment_ids + 1
     tag_rows = jnp.stack(
@@ -310,7 +369,7 @@
         bias_project,
         scale_second,
     ) = [columns[i] for i in range(10)]
-    bias_hidden = columns[10 : 10 + parts].reshape(parts, count, shard).transpose(1, 0, 2).reshape(ff)
+    bias_hidden = columns[10 : 10 + parts].reshape(parts, 1, width)
     weight_qkv = lax.dynamic_slice_in_dim(attention_full, core * 3 * half, 3 * half, 1)
     weight_output = attention_full[:, 3 * width : 4 * width]
 
@@ -327,31 +386,30 @@
     projected = ((product(normed_window, weight_qkv) + bias_qkv) * scale_qkv).astype(bf16)
 
     pairs = half // PAIR
-    grid = (pairs, own_blocks)
     first = first_row // BLK
-    q_own = pl.BlockSpec((BLK, PAIR), lambda h, b, lo, hi: (first + b, h))
-    k_own = pl.BlockSpec((BLK, PAIR), lambda h, b, lo, hi: (first + b, pairs + h))
-    v_own = pl.BlockSpec((BLK, PAIR), lambda h, b, lo, hi: (first + b, 2 * pairs + h))
-    q_all = pl.BlockSpec((window, PAIR), lambda h, b, lo, hi: (0, h))
-    k_all = pl.BlockSpec((window, PAIR), lambda h, b, lo, hi: (0, pairs + h))
-    v_all = pl.BlockSpec((window, PAIR), lambda h, b, lo, hi: (0, 2 * pairs + h))
+
+    def own_rows(group):
+        return pl.BlockSpec((BLK, PAIR), lambda h, b, lo, hi: (first + b, group * pairs + h))
+
+    def all_rows(group):
+        return pl.BlockSpec((window, PAIR), lambda h, b, lo, hi: (0, group * pairs + h))
+
     row_block = pl.BlockSpec((BLK, PAIR), lambda h, b, lo, hi: (b, h))
     label_rows = pl.BlockSpec((BLK, 1), lambda h, b, lo, hi: (first + b, 0))
     label_all = pl.BlockSpec((1, window), lambda h, b, lo, hi: (0, 0))
-    share = 2 * rows * 1400 * half * 2
     attended_f, lse = attention_call(
         partial(attend_kernel, first),
-        grid,
-        [q_own, k_all, v_all, label_rows, label_all],
+        (pairs, own_blocks),
+        [own_rows(0), all_rows(1), all_rows(2), label_rows, label_all],
         [row_block, row_block],
         [jax.ShapeDtypeStruct((2 * rows, half), f32)] * 2,
         [
-            pltpu.VMEM((2, window // BLK, BLK, BLK), f32),
+            pltpu.VMEM((2, window // STEP, BLK, STEP), f32),
             pltpu.VMEM((2, BLK, 128), f32),
             pltpu.VMEM((2, BLK, 128), f32),
             pltpu.VMEM((2, BLK, PAIR), f32),
         ],
-        2 * share,
+        60_000_000_000,
     )(lo, hi, projected, projected, projected, query_label[:, None], key_label[None])
 
     def columns_of(c, mine, theirs):
@@ -367,29 +425,17 @@
     branch = product(attended_low, weight_output) + bias_output
     middle = inputs + scale_first * branch
 
-    weight_hidden = (
-        dense_full[:, : parts * shard]
-        .reshape(count, parts, shard, width)
-        .transpose(0, 2, 1, 3)
-        .reshape(width, ff)
-    )
-    weight_project = dense_full[:, parts * shard :].reshape(ff, width)
     normed_two, second_norm_back = jax.vjp(layer_norm, middle, gain_second, bias_second)
-    normed_two_low = normed_two.astype(bf16)
-    hidden = product(normed_two_low, weight_hidden) + bias_hidden
-    active, gelu_back = jax.vjp(gelu_exact, hidden)
-    active_low = active.astype(bf16)
-    dense_out = product(active_low, weight_project) + bias_project
+    upstream = cotangent.astype(f32)
+    grad_dense = (upstream * scale_second).astype(bf16)
+    dense_sum, grad_normed_two, dense_weight_grads, hidden_bias_grad = dense_call(
+        normed_two.astype(bf16), grad_dense, dense_full, bias_hidden
+    )
+    dense_out = dense_sum + bias_project
     layer_output = (middle + scale_second * dense_out).astype(bf16)
-    upstream = cotangent.astype(f32)
     dense_scale_grad = jnp.sum(upstream * dense_out, axis=0)
-    grad_dense = (upstream * scale_second).astype(bf16)
-    project_weight_grad = inner_rows(active_low, grad_dense).astype(bf16)
     project_bias_grad = column_sums(grad_dense)
-    grad_hidden = gelu_back(against(grad_dense, weight_project))[0].astype(bf16)
-    hidden_weight_grad = inner_rows(normed_two_low, grad_hidden).astype(bf16)
-    hidden_bias_grad = column_sums(grad_hidden)
-    grad_middle_norm, second_gain_grad, second_bias_grad = second_norm_back(against(grad_hidden, weight_hidden))
+    grad_middle_norm, second_gain_grad, second_bias_grad = second_norm_back(grad_normed_two)
     grad_middle = upstream + grad_middle_norm
     attention_scale_grad = jnp.sum(grad_middle * branch, axis=0)
     grad_branch = (grad_middle * scale_first).astype(bf16)
@@ -397,30 +443,17 @@
     output_bias_grad = column_sums(grad_branch)
     grad_attended = against(grad_branch, weight_output).astype(bf16)
 
+    dense_sums = lax.psum_scatter(
+        dense_weight_grads.reshape(2 * parts, width, width), "dev", scatter_dimension=1, tiled=True
+    )
     bits = list(range(depth - 1, -1, -1))
-    project_rows = project_weight_grad.shape[0] // count
-    cut = 3 * width // 4
-    part_a = bit_view(project_weight_grad[:, :cut], count, project_rows)
-    part_b = bit_view(hidden_weight_grad[:, :3 * width], count, shard)
-    rest = project_weight_grad[:, cut:].reshape(count, parts, shard, width - cut)
-    part_c = jnp.concatenate(
-        [rest[:, j] for j in range(parts)]
-        + [
-            hidden_weight_grad[:, 3 * width :].reshape(count, shard, -1),
-            output_weight_grad.reshape(count, shard, width),
-        ],
-        axis=2,
-    )
-    part_c = part_c.reshape((2,) * depth + part_c.shape[1:])
 
     def order_of(turn, low):
         chips = list(range(1, depth))
         axes, last = chips[:3], chips[3:]
         return low + axes[turn:] + axes[:turn] + last
 
-    sum_a = scatter_sum(part_a, bits, order_of(0, [0]))
-    sum_b = scatter_sum(part_b, bits, order_of(1, [0]))
-    sum_c = scatter_sum(part_c, bits, order_of(2, [0]))
+    output_sum = scatter_sum([output_weight_grad.reshape((2,) * depth + (shard, width))], bits, order_of(2, [0]))
 
     grad_half = jnp.where(core == 0, grad_attended[:, :half], grad_attended[:, half:])
     grad_other = swap(jnp.where(core == 0, grad_attended[:, half:], grad_attended[:, :half]), 0)
@@ -439,38 +472,47 @@
     from_above = shifted(both, -2)
     far_below = shifted(packed[1], 4)
     far_above = shifted(packed[0], -4)
+    delta_wide = jnp.repeat(delta, HEAD_DIM, axis=1)
+    (grad_queries,) = attention_call(
+        partial(query_kernel, first),
+        (pairs, own_blocks),
+        [own_rows(0), all_rows(1), all_rows(2), label_rows, label_all, row_block, row_block, row_block],
+        [row_block],
+        [jax.ShapeDtypeStruct((2 * rows, half), bf16)],
+        [pltpu.VMEM((2, BLK, PAIR), f32)],
+        60_000_000_000,
+    )(lo, hi, projected, projected, projected, query_label[:, None], key_label[None], grad_pair, lse, delta_wide)
+    from_below, from_above, far_below, far_above, grad_queries = lax.optimization_barrier(
+        (from_below, from_above, far_below, far_above, grad_queries)
+    )
     unit = rows + stat_count
     arrived = [far_below, from_below[:unit], from_below[unit:], packed[0], packed[1], from_above[:unit], from_above[unit:], far_above]
     grad_window = jnp.concatenate([b[:rows] for b in arrived])
     stat_window = jnp.concatenate([b[rows:] for b in arrived], axis=1).astype(f32)
     stat_window = stat_window.reshape(3, 2, pairs, 2, window)
     stat_window = (stat_window[0] + stat_window[1] + stat_window[2]).transpose(1, 0, 2, 3).reshape(pairs, 4, window)
-    delta_wide = jnp.repeat(delta, HEAD_DIM, axis=1)
-    (grad_queries,) = attention_call(
-        partial(query_kernel, first),
-        grid,
-        [q_own, k_all, v_all, label_rows, label_all, row_block, row_block, row_block],
-        [row_block],
-        [jax.ShapeDtypeStruct((2 * rows, half), bf16)],
-        [pltpu.VMEM((2, BLK, PAIR), f32)],
-        3 * share,
-    )(lo, hi, projected, projected, projected, query_label[:, None], key_label[None], grad_pair, lse, delta_wide)
-    stat_spec = pl.BlockSpec((1, 4, window), lambda h, b, lo, hi: (h, 0, 0))
-    do_all = pl.BlockSpec((window, PAIR), lambda h, b, lo, hi: (0, h))
     grad_keys, grad_values = attention_call(
         partial(key_kernel, first),
-        grid,
-        [q_all, k_own, v_own, label_all, label_rows, do_all, stat_spec],
+        (pairs, own_blocks),
+        [
+            all_rows(0),
+            own_rows(1),
+            own_rows(2),
+            label_all,
+            label_rows,
+            pl.BlockSpec((window, PAIR), lambda h, b, lo, hi: (0, h)),
+            pl.BlockSpec((1, 4, window), lambda h, b, lo, hi: (h, 0, 0)),
+        ],
         [row_block, row_block],
         [jax.ShapeDtypeStruct((2 * rows, half), bf16)] * 2,
         [pltpu.VMEM((2, BLK, PAIR), f32)] * 2,
-        4 * share,
+        70_000_000_000,
     )(lo, hi, projected, projected, projected, query_label[None], key_label[:, None], grad_window, stat_window)
 
     normed_pair = normed_window[first_row:last_row]
     chip_bits = bits[:-1]
     sums = [
-        scatter_sum(inner_rows(normed_pair, g).astype(bf16).reshape((2,) * (depth - 1) + (2 * shard, half)), chip_bits, order_of(turn, []))
+        scatter_sum([inner_rows(normed_pair, g).astype(bf16).reshape((2,) * (depth - 1) + (2 * shard, half))], chip_bits, order_of(turn, []))
         for turn, g in enumerate((grad_queries, grad_keys, grad_values))
     ]
     chip_rows = jnp.concatenate(sums, axis=1)
@@ -505,20 +547,17 @@
         second_bias_grad,
         project_bias_grad,
         dense_scale_grad,
-        hidden_bias_grad,
+        hidden_bias_grad.reshape(parts, count, shard).transpose(1, 0, 2),
     ]
     vector_rows = jnp.concatenate([g.reshape(count, -1) for g in grads], axis=1)
     vector_rows = jnp.pad(vector_rows, ((0, 0), (0, -vector_rows.shape[1] % 128)))
-    vector_sum = scatter_sum(vector_rows.reshape((2,) * depth + (1, -1)), bits, bits, f32)[0]
+    vector_sum = scatter_sum([vector_rows.reshape((2,) * depth + (1, -1))], bits, bits, f32)[0]
     out = [vector_sum[i * shard : (i + 1) * shard] for i in range(10)]
     hidden_bias_out = vector_sum[10 * shard : (10 + parts) * shard]
-    c_rows = sum_c.astype(f32)
-    rest_width = width - cut
-    project_out = jnp.concatenate(
-        [sum_a.astype(f32), jnp.concatenate([c_rows[:, j * rest_width : (j + 1) * rest_width] for j in range(parts)])], axis=1
-    )
-    hidden_out = jnp.concatenate([sum_b.astype(f32), c_rows[:, width : 2 * width]], axis=1)
-    output_out = c_rows[:, 2 * width :]
+    dense_sums = dense_sums.astype(f32)
+    project_out = dense_sums[parts:].reshape(parts * shard, width)
+    hidden_out = dense_sums[:parts].reshape(parts, shard, count, shard).transpose(1, 2, 0, 3).reshape(shard, ff)
+    output_out = output_sum.astype(f32)
     return (
         layer_output,
         input_gradient,

time: 896 us -> 611 us (0.68); the launches traced: 879 us -> 606 us
  waiting for transfers between devices: 292 us -> 179 us
  matrix products: 119 us -> 44.4 us
  starting transfers between devices: 106 us -> 67 us
  local copies, waits for them, and re-layouts: 119 us -> 81.8 us
  Pallas kernels: 179 us -> 164 us
    ppermute x37 -> x27, waiting for transfers between devices: 161 us -> 77 us  [swap(): return lax.ppermute(block, 'dev', [(i, i ^ 1 << bit) for i in range(count)])]
    ppermute x37 -> x27, starting transfers between devices: 87.9 us -> 46.9 us  [swap(): return lax.ppermute(block, 'dev', [(i, i ^ 1 << bit) for i in range(count)])]
    dot_general x4 -> x2, matrix products: 62 us -> 24.8 us  [product(): return jnp.dot(a, b, preferred_element_type=f32)]
    ppermute x6, waiting for transfers between devices: 73.2 us -> 47.9 us  [shifted(): lax.ppermute(block, 'dev', [(i, i + distance) for i in range(count) if 0...]
    dot_general x4 -> x2, matrix products: 32.4 us -> 8.39 us  [against(): lax.dot_general(a, b, (((1,), (1,)), ((), ())), preferred_element_type=f32)]
    unnamed x167 -> x157, local copies, waits for them, and re-layouts: 56.8 us -> 35.8 us
    pallas_call x3 -> x4, Pallas kernels: 179 us -> 164 us  [the longest x1 46.9 us: on_device(): attention_call(partial(key_kernel, first), (pairs, own_blocks), [all_rows...]
    dot_general x6 -> x4, matrix products: 24.2 us -> 11.2 us  [inner_rows(): lax.dot_general(a, b, (((0,), (0,)), ((), ())), preferred_element_type=f32)]
  transfers between devices with their start and end apart: 46 -> 37, of which waited for: 32 -> 19; matrix products, arithmetic and copies ran while one was open for 17% -> 24% of each run, Pallas kernels for 20% -> 21%
where the time goes in v2:
time: 611 us; the launch traced here: 606 us
  waiting for transfers between devices  179 us (29%)
  Pallas kernels  164 us (27%)
  local copies, waits for them, and re-layouts  81.8 us (13%)
  starting transfers between devices  67 us (11%)
  other arithmetic  54.1 us (9%)
  matrix products  44.4 us (7%)
  between operations  15.6 us (3%)
    ppermute x27, waiting for transfers between devices, swap(): return lax.ppermute(block, 'dev', [(i, i ^ 1 << bit) for i in range(count)])  77 us
    ppermute x6, waiting for transfers between devices, shifted(): lax.ppermute(block, 'dev', [(i, i + distance) for i in range(count) if 0...  47.9 us
    ppermute x27, starting transfers between devices, swap(): return lax.ppermute(block, 'dev', [(i, i ^ 1 << bit) for i in range(count)])  46.9 us
    pallas_call x1, Pallas kernels, on_device(): attention_call(partial(key_kernel, first), (pairs, own_blocks), [all_rows...  46.9 us
    pallas_call x1, Pallas kernels, on_device(): attention_call(partial(query_kernel, first), (pairs, own_blocks), [own_ro...  41 us
    pallas_call x1, Pallas kernels, on_device(): attention_call(partial(attend_kernel, first), (pairs, own_blocks), [own_r...  38.4 us
    pallas_call x1, Pallas kernels, dense_call(): pl.pallas_call(dense_kernel, grid=(parts,), in_specs=[whole, whole, chunk...  37.5 us
    unnamed x157, local copies, waits for them, and re-layouts  35.8 us
  transfers between devices with their start and end apart: 37, of which 19 were waited for; matrix products, arithmetic and copies ran while one was open for 24% of the time, Pallas kernels for 21%

profile of v2, /device:TPU:0, one launch (start us, length us, event | category | flops | bytes accessed | tf_op | source)
XLA Modules:
  0.0 606.2 jit_solution(2767241464969495208)
XLA Ops:
  20.1 4.9 collective-permute-start
  27.9 45.2 %collective-permute-done = bf16[528,1024]{1,0:T(8,128)(2,1)S(1)} collective-permute-done((bf16[528,1024]{1,0:T(8,128)(2,1)S(1)}, bf16[528,1024]{1,0:T(8,128)(2,1)S(1)}, u32[]{:S(2)}, u32[]{:S(2)}) %collective-permute-start) | collective-permute-done | bytes 1081376 | tf_op jit(solution)/shard_map/ppermute | solution.py:245
  75.1 2.5 pad_maximum_fusion
  77.8 7.7 %collective-permute-done.3 = bf16[4,528,1024]{2,1,0:T(8,128)(2,1)} collective-permute-done((bf16[4,528,1024]{2,1,0:T(8,128)(2,1)}, bf16[4,528,1024]{2,1,0:T(8,128)(2,1)}, u32[]{:S(2)}, u32[]{:S(2)}) %collective-permute-start.3) | collective-permute-done | bytes 4325408 | tf_op jit(solution)/shard_map/ppermute | solution.py:240
  85.5 3.6 broadcast_select_fusion
  103.6 2.8 copy-done.3
  106.4 2.8 fusion.2
  109.2 2.3 broadcast_select_fusion.2
  111.6 23.1 %all-gather.3.cloned.1.call-done = bf16[1024,4224]{1,0:T(8,128)(2,1)} async-done(((bf16[32,4224]{1,0:T(8,128)(2,1)}), bf16[1024,4224]{1,0:T(8,128)(2,1)}) %all-gather.3.cloned.1.call-update) | async-done | bytes 8650768 | tf_op jit(solution)/shard_map/all_gather | solution.py:326
  136.6 5.9 fusion.5
  142.5 19.9 %multiply_convert_fusion.q_ref.k_ref.v_ref = bf16[4096,1536]{1,0:T(8,128)(2,1)} fusion(bf16[4096,1024]{1,0:T(8,128)(2,1)S(1)} %fusion.5, f32[1536]{0:T(1024)S(1)} %copy-done.59, f32[1536]{0:T(1024)S(1)} %pad_maximum_fusion.9, bf16[1024,4224]{1,0:T(8,128)(2,1)} %all-gather.3.cloned.1.call-done, s32[]{:T(128)S(6)} %select_n.235), kind=kOutput, calls=%fused_computation | convolution fusion | flops 12903776256 | bytes 24129540 | tf_op jit(solution)/shard_map/dot_general | solution.py:27
  162.3 38.4 %shard_map.348 = (f32[1024,512]{1,0:T(8,128)S(1)}, f32[1024,512]{1,0:T(8,128)S(1)}) custom-call(s32[4]{0:T(128)S(1)} %get-tuple-element.135.lo, s32[4]{0:T(128)S(1)} %get-tuple-element.136.hi, bf16[4096,1536]{1,0:T(8,128)(2,1)} %multiply_convert_fusion.q_ref.k_ref.v_ref, bf16[4096,1536]{1,0:T(8,128)(2,1)} %multiply_convert_fusion.q_ref.k_ref.v_ref, ...), custom_call_target="tpu_custom_call" | custom-call | flops 60000002048 | bytes 8000000 | tf_op jit(solution)/shard_map/pallas_call | solution.py:400
  204.0 3.4 copy.121
  208.4 2.6 convert_reduce_fusion.2
  211.6 5.0 fusion.105
  219.3 31.3 %all-gather.5.cloned.1.call-done.wh_ref.wp_ref = bf16[8,1024,1024]{2,1,0:T(8,128)(2,1)} async-done(((bf16[8,32,1024]{2,1,0:T(8,128)(2,1)}), bf16[8,1024,1024]{2,1,0:T(8,128)(2,1)}) %all-gather.5.cloned.1.call-update) | async-done | bytes 16777232 | tf_op jit(solution)/shard_map/all_gather | solution.py:327
  250.6 37.5 %shard_map.349 = (f32[512,1024]{1,0:T(8,128)}, f32[512,1024]{1,0:T(8,128)}, bf16[2,4,1024,1024]{3,2,1,0:T(8,128)(2,1)}, f32[4,1,1024]{2,1,0:T(1,128)}) custom-call(bf16[512,1024]{1,0:T(8,128)(2,1)} %add_convert_fusion.1.n_ref, bf16[512,1024]{1,0:T(8,128)(2,1)} %get-tuple-element.58.gd_ref, bf16[8,1024,1024]{2,1,0:T(8,128)(2,1)} %all-gather.5.cloned.1.call-done.wh_ref.wp_ref, ...), custom_call_target="tpu_custom_call" | custom-call | flops 49999998976 | bytes 40000000 | tf_op jit(solution)/shard_map/pallas_call | solution.py:201
  288.1 2.3 multiply_reduce_fusion
  290.5 3.0 fusion.104
  294.9 3.0 fusion.44
  299.0 2.5 convolution_convert_fusion
  307.8 3.4 convert_multiply_fusion.2
  314.7 4.4 collective-permute-start.6
  326.1 5.2 collective-permute-start.8
  333.1 2.2 collective-permute-start.30
  335.3 41.0 %shard_map.350 = bf16[1024,512]{1,0:T(8,128)(2,1)S(1)} custom-call(s32[4]{0:T(128)S(1)} %get-tuple-element.135.lo, s32[4]{0:T(128)S(1)} %get-tuple-element.136.hi, bf16[4096,1536]{1,0:T(8,128)(2,1)} %multiply_convert_fusion.q_ref.k_ref.v_ref, bf16[4096,1536]{1,0:T(8,128)(2,1)} %multiply_convert_fusion.q_ref.k_ref.v_ref, ...), custom_call_target="tpu_custom_call" | custom-call | flops 60000002048 | bytes 8000000 | tf_op jit(solution)/shard_map/pallas_call | solution.py:476
  376.3 20.4 %collective-permute-done.30 = bf16[2,2,2,32,1024]{4,3,0,1,2:T(8,128)(2,1)S(1)} collective-permute-done((bf16[2,2,2,32,1024]{4,3,0,1,2:T(8,128)(2,1)S(1)}, bf16[2,2,2,32,1024]{4,3,0,1,2:T(8,128)(2,1)S(1)}, u32[]{:S(2)}, u32[]{:S(2)}) %collective-permute-start.30) | collective-permute-done | bytes 524320 | tf_op jit(solution)/shard_map/ppermute | solution.py:240
  399.2 2.9 fusion.35
  403.9 17.5 %collective-permute-start.16 = (bf16[2,2,2,64,512]{4,3,0,1,2:T(8,128)(2,1)}, bf16[2,2,2,64,512]{4,3,0,1,2:T(8,128)(2,1)}, u32[]{:S(2)}, u32[]{:S(2)}) collective-permute-start(bf16[2,2,2,64,512]{4,3,0,1,2:T(8,128)(2,1)} %bitcast.245), channel_id=1, source_target_pairs={{0,2},{1,3},{2,0},{3,1},{4,6},{5,7},{6,4},{7,5},{8,10},{9,11},{10,... | collective-permute-start | bytes 1572872 | tf_op jit(solution)/shard_map/ppermute | solution.py:240
  432.8 46.9 %shard_map.351 = (bf16[1024,512]{1,0:T(8,128)(2,1)S(1)}, bf16[1024,512]{1,0:T(8,128)(2,1)S(1)}) custom-call(s32[4]{0:T(128)S(1)} %get-tuple-element.135.lo, s32[4]{0:T(128)S(1)} %get-tuple-element.136.hi, bf16[4096,1536]{1,0:T(8,128)(2,1)} %multiply_convert_fusion.q_ref.k_ref.v_ref, bf16[4096,1536]{1,0:T(8,128)(2,1)} %multiply_convert_fusion.q_ref.k_ref.v_ref, ...), custom_call_target="tpu_custom_call" | custom-call | flops 70000001024 | bytes 8000000 | tf_op jit(solution)/shard_map/pallas_call | solution.py:494
  479.7 2.9 fusion.38
  483.6 9.4 %collective-permute-start.20 = (bf16[2,2,2,64,512]{4,3,0,2,1:T(8,128)(2,1)}, bf16[2,2,2,64,512]{4,3,0,2,1:T(8,128)(2,1)}, u32[]{:S(2)}, u32[]{:S(2)}) collective-permute-start(bf16[2,2,2,64,512]{4,3,0,2,1:T(8,128)(2,1)} %bitcast.244), channel_id=1, source_target_pairs={{0,4},{1,5},{2,6},{3,7},{4,0},{5,1},{6,2},{7,3},{8,12},{9,13},{10,... | collective-permute-start | bytes 1572872 | tf_op jit(solution)/shard_map/ppermute | solution.py:240
  493.0 2.9 fusion.41
  497.6 5.4 fusion.6
  504.8 16.3 %collective-permute-done.32 = bf16[2,32,1024]{2,1,0:T(8,128)(2,1)S(1)} collective-permute-done((bf16[2,32,1024]{2,1,0:T(8,128)(2,1)S(1)}, bf16[2,32,1024]{2,1,0:T(8,128)(2,1)S(1)}, u32[]{:S(2)}, u32[]{:S(2)}) %collective-permute-start.32) | collective-permute-done | bytes 131104 | tf_op jit(solution)/shard_map/ppermute | solution.py:240
  521.2 5.9 collective-permute-start.33
  535.0 10.3 %collective-permute-done.17 = bf16[2,2,64,512]{3,2,0,1:T(8,128)(2,1)S(1)} collective-permute-done((bf16[2,2,64,512]{3,2,0,1:T(8,128)(2,1)S(1)}, bf16[2,2,64,512]{3,2,0,1:T(8,128)(2,1)S(1)}, u32[]{:S(2)}, u32[]{:S(2)}) %collective-permute-start.17) | collective-permute-done | bytes 262176 | tf_op jit(solution)/shard_map/ppermute | solution.py:240
  545.7 2.4 collective-permute-done.25
  550.8 3.2 collective-permute-start.19
  554.2 3.0 collective-permute-start.27
  557.2 2.3 collective-permute-done.19
  559.5 2.5 collective-permute-done.23
  566.9 3.0 fusion.23
  570.5 4.9 collective-permute-done.11
  575.6 3.7 collective-permute-done.12
  580.5 2.6 collective-permute-done.13
  591.8 3.2 copy.168
  595.0 4.4 reshape.440
  (368 shorter events, 108.9 us)
Async XLA Ops:
  7.2 127.5 %all-gather.3.cloned.1.call-start = ((), (), s32[]{:S(2)}) async-start(), calls=%async_computation.1 | async-start | bytes 8921088 | tf_op jit(solution)/shard_map/all_gather | solution.py:326
  15.7 234.9 %all-gather.5.cloned.1.call-start = ((), (), s32[]{:S(2)}) async-start(), calls=%async_computation.2 | async-start | bytes 17301504 | tf_op jit(solution)/shard_map/all_gather | solution.py:327
  19.8 569.4 %reduce-scatter.2.cloned.1.call-start = ((), (), s32[]{:S(2)}) async-start(), calls=%async_computation.3 | async-start | bytes 17301504 | tf_op jit(solution)/shard_map/reduce_scatter | solution.py:446
  20.1 53.1 %collective-permute-start = (bf16[528,1024]{1,0:T(8,128)(2,1)S(1)}, bf16[528,1024]{1,0:T(8,128)(2,1)S(1)}, u32[]{:S(2)}, u32[]{:S(2)}) collective-permute-start(bf16[528,1024]{1,0:T(8,128)(2,1)S(1)} %get-tuple-element.77), channel_id=1, source_target_pairs={{0,2},{1,3},{2,4},{3,5},{4,6},{5,7},{6,8},{7,9},{8,10},{9,11},{10,... | collective-permute-start | bytes 3244040 | tf_op jit(solution)/shard_map/ppermute | solution.py:245
  25.0 50.1 %collective-permute-start.1 = (bf16[528,1024]{1,0:T(8,128)(2,1)S(1)}, bf16[528,1024]{1,0:T(8,128)(2,1)S(1)}, u32[]{:S(2)}, u32[]{:S(2)}) collective-permute-start(bf16[528,1024]{1,0:T(8,128)(2,1)S(1)} %get-tuple-element.77), channel_id=1, source_target_pairs={{2,0},{3,1},{4,2},{5,3},{6,4},{7,5},{8,6},{9,7},{10,8},{11,9},{12,... | collective-permute-start | bytes 3244040 | tf_op jit(solution)/shard_map/ppermute | solution.py:245
  26.3 48.8 %collective-permute-start.2 = (bf16[528,1024]{1,0:T(8,128)(2,1)S(1)}, bf16[528,1024]{1,0:T(8,128)(2,1)S(1)}, u32[]{:S(2)}, u32[]{:S(2)}) collective-permute-start(bf16[528,1024]{1,0:T(8,128)(2,1)S(1)} %get-tuple-element.77), channel_id=1, source_target_pairs={{4,0},{6,2},{8,4},{10,6},{12,8},{14,10},{16,12},{18,14},{20,16},{2... | collective-permute-start | bytes 3244040 | tf_op jit(solution)/shard_map/ppermute | solution.py:337
  77.8 7.7 %collective-permute-start.3 = (bf16[4,528,1024]{2,1,0:T(8,128)(2,1)}, bf16[4,528,1024]{2,1,0:T(8,128)(2,1)}, u32[]{:S(2)}, u32[]{:S(2)}) collective-permute-start(bf16[4,528,1024]{2,1,0:T(8,128)(2,1)} %pad_maximum_fusion), channel_id=1, source_target_pairs={{0,1},{1,0},{2,3},{3,2},{4,5},{5,4},{6,7},{7,6},{8,9},{9,8},{10,11... | collective-permute-start | bytes 12976136 | tf_op jit(solution)/shard_map/ppermute | solution.py:240
  136.5 71.9 %copy-start.48 = (f32[1,1024]{1,0:T(1,128)}, f32[1,1024]{1,0:T(1,128)S(1)}, u32[]{:S(2)}) copy-start(f32[1,1024]{1,0:T(1,128)S(1)} %get-tuple-element.96) | copy-start | bytes 12292
  136.5 75.1 %copy-start.55 = (f32[1,1024]{1,0:T(1,128)}, f32[1,1024]{1,0:T(1,128)S(1)}, u32[]{:S(2)}) copy-start(f32[1,1024]{1,0:T(1,128)S(1)} %get-tuple-element.97) | copy-start | bytes 12292
  142.5 19.9 %copy-start.16 = (bf16[4096,1024]{1,0:T(8,128)(2,1)}, bf16[4096,1024]{1,0:T(8,128)(2,1)S(1)}, u32[]{:S(2)}) copy-start(bf16[4096,1024]{1,0:T(8,128)(2,1)S(1)} %fusion.5) | copy-start | bytes 25165828
  202.4 9.3 %collective-permute-start.4 = (bf16[512,512]{1,0:T(8,128)(2,1)}, bf16[512,512]{1,0:T(8,128)(2,1)}, u32[]{:S(2)}, u32[]{:S(2)}) collective-permute-start(bf16[512,512]{1,0:T(8,128)(2,1)} %get-tuple-element.90), channel_id=1, source_target_pairs={{0,1},{1,0},{2,3},{3,2},{4,5},{5,4},{6,7},{7,6},{8,9},{9,8},{10,11... | collective-permute-start | bytes 1572872 | tf_op jit(solution)/shard_map/ppermute | solution.py:240
  250.6 37.5 %copy-start.5 = (f32[512,1024]{1,0:T(8,128)S(1)}, f32[512,1024]{1,0:T(8,128)}, u32[]{:S(2)}) copy-start(f32[512,1024]{1,0:T(8,128)} %copy-done.4) | copy-start | bytes 6291460
  298.7 8.2 %collective-permute-start.5 = (bf16[512,512]{1,0:T(8,128)(2,1)S(1)}, bf16[512,512]{1,0:T(8,128)(2,1)S(1)}, u32[]{:S(2)}, u32[]{:S(2)}) collective-permute-start(bf16[512,512]{1,0:T(8,128)(2,1)S(1)} %get-tuple-element.86), channel_id=1, source_target_pairs={{0,1},{1,0},{2,3},{3,2},{4,5},{5,4},{6,7},{7,6},{8,9},{9,8},{10,11... | collective-permute-start | bytes 1572872 | tf_op jit(solution)/shard_map/ppermute | solution.py:240
  303.8 27.5 %collective-permute-start.29 = (bf16[2,2,2,2,32,1024]{5,4,0,2,3,1:T(8,128)(2,1)}, bf16[2,2,2,2,32,1024]{5,4,0,2,3,1:T(8,128)(2,1)}, u32[]{:S(2)}, u32[]{:S(2)}) collective-permute-start(bf16[2,2,2,2,32,1024]{5,4,0,2,3,1:T(8,128)(2,1)} %bitcast.241), channel_id=1, source_target_pairs={{0,1},{1,0},{2,3},{3,2},{4,5},{5,4},{6,7},{7,6},{8,9},{9,8},{10,11... | collective-permute-start | bytes 3145736 | tf_op jit(solution)/shard_map/ppermute | solution.py:240
  314.7 83.8 %collective-permute-start.6 = (bf16[1120,512]{1,0:T(8,128)(2,1)}, bf16[1120,512]{1,0:T(8,128)(2,1)}, u32[]{:S(2)}, u32[]{:S(2)}) collective-permute-start(bf16[1120,512]{1,0:T(8,128)(2,1)} %pad_maximum_fusion.1), channel_id=1, source_target_pairs={{0,2},{1,3},{2,4},{3,5},{4,6},{5,7},{6,8},{7,9},{8,10},{9,11},{10,... | collective-permute-start | bytes 3440648 | tf_op jit(solution)/shard_map/ppermute | solution.py:245
  319.1 80.1 %collective-permute-start.7 = (bf16[1120,512]{1,0:T(8,128)(2,1)}, bf16[1120,512]{1,0:T(8,128)(2,1)}, u32[]{:S(2)}, u32[]{:S(2)}) collective-permute-start(bf16[1120,512]{1,0:T(8,128)(2,1)} %pad_maximum_fusion.1), channel_id=1, source_target_pairs={{2,0},{3,1},{4,2},{5,3},{6,4},{7,5},{8,6},{9,7},{10,8},{11,9},{12,... | collective-permute-start | bytes 3440648 | tf_op jit(solution)/shard_map/ppermute | solution.py:245
  323.7 74.8 %collective-permute-start.9 = (bf16[560,512]{1,0:T(8,128)(2,1)S(1)}, bf16[560,512]{1,0:T(8,128)(2,1)S(1)}, u32[]{:S(2)}, u32[]{:S(2)}) collective-permute-start(bf16[560,512]{1,0:T(8,128)(2,1)S(1)} %pad_maximum_fusion.4), channel_id=1, source_target_pairs={{4,0},{5,1},{6,2},{7,3},{8,4},{9,5},{10,6},{11,7},{12,8},{13,9},{1... | collective-permute-start | bytes 1720328 | tf_op jit(solution)/shard_map/ppermute | solution.py:245
  326.1 72.4 %collective-permute-start.8 = (bf16[560,512]{1,0:T(8,128)(2,1)S(1)}, bf16[560,512]{1,0:T(8,128)(2,1)S(1)}, u32[]{:S(2)}, u32[]{:S(2)}) collective-permute-start(bf16[560,512]{1,0:T(8,128)(2,1)S(1)} %pad_maximum_fusion.3), channel_id=1, source_target_pairs={{0,4},{1,5},{2,6},{3,7},{4,8},{5,9},{6,10},{7,11},{8,12},{9,13},{1... | collective-permute-start | bytes 1720328 | tf_op jit(solution)/shard_map/ppermute | solution.py:245
  333.1 63.6 %collective-permute-start.30 = (bf16[2,2,2,32,1024]{4,3,0,1,2:T(8,128)(2,1)S(1)}, bf16[2,2,2,32,1024]{4,3,0,1,2:T(8,128)(2,1)S(1)}, u32[]{:S(2)}, u32[]{:S(2)}) collective-permute-start(bf16[2,2,2,32,1024]{4,3,0,1,2:T(8,128)(2,1)S(1)} %dynamic-slice_bitcast_fusion), channel_id=1, source_target_pairs={{0,8},{1,9},{2,10},{3,11},{4,12},{5,13},{6,14},{7,15},{8,0},{9,1},... | collective-permute-start | bytes 1572872 | tf_op jit(solution)/shard_map/ppermute | solution.py:240
  398.4 104.8 %collective-permute-start.31 = (bf16[2,2,32,1024]{3,2,0,1:T(8,128)(2,1)}, bf16[2,2,32,1024]{3,2,0,1:T(8,128)(2,1)}, u32[]{:S(2)}, u32[]{:S(2)}) collective-permute-start(bf16[2,2,32,1024]{3,2,0,1:T(8,128)(2,1)} %dynamic-slice_bitcast_fusion.1), channel_id=1, source_target_pairs={{0,2},{1,3},{2,0},{3,1},{4,6},{5,7},{6,4},{7,5},{8,10},{9,11},{10,... | collective-permute-start | bytes 786440 | tf_op jit(solution)/shard_map/ppermute | solution.py:240
  398.5 26.1 %copy-start.33 = (bf16[560,512]{1,0:T(8,128)(2,1)}, bf16[560,512]{1,0:T(8,128)(2,1)S(1)}, u32[]{:S(2)}) copy-start(bf16[560,512]{1,0:T(8,128)(2,1)S(1)} %collective-permute-done.9) | copy-start | bytes 1720324
  398.5 22.9 %copy-start.35 = (bf16[560,512]{1,0:T(8,128)(2,1)}, bf16[560,512]{1,0:T(8,128)(2,1)S(1)}, u32[]{:S(2)}) copy-start(bf16[560,512]{1,0:T(8,128)(2,1)S(1)} %collective-permute-done.8) | copy-start | bytes 1720324
  403.9 126.3 %collective-permute-start.16 = (bf16[2,2,2,64,512]{4,3,0,1,2:T(8,128)(2,1)}, bf16[2,2,2,64,512]{4,3,0,1,2:T(8,128)(2,1)}, u32[]{:S(2)}, u32[]{:S(2)}) collective-permute-start(bf16[2,2,2,64,512]{4,3,0,1,2:T(8,128)(2,1)} %bitcast.245), channel_id=1, source_target_pairs={{0,2},{1,3},{2,0},{3,1},{4,6},{5,7},{6,4},{7,5},{8,10},{9,11},{10,... | collective-permute-start | bytes 1572872 | tf_op jit(solution)/shard_map/ppermute | solution.py:240
  483.6 48.8 %collective-permute-start.20 = (bf16[2,2,2,64,512]{4,3,0,2,1:T(8,128)(2,1)}, bf16[2,2,2,64,512]{4,3,0,2,1:T(8,128)(2,1)}, u32[]{:S(2)}, u32[]{:S(2)}) collective-permute-start(bf16[2,2,2,64,512]{4,3,0,2,1:T(8,128)(2,1)} %bitcast.244), channel_id=1, source_target_pairs={{0,4},{1,5},{2,6},{3,7},{4,0},{5,1},{6,2},{7,3},{8,12},{9,13},{10,... | collective-permute-start | bytes 1572872 | tf_op jit(solution)/shard_map/ppermute | solution.py:240
  497.6 36.0 %collective-permute-start.24 = (bf16[2,2,2,64,512]{4,3,0,1,2:T(8,128)(2,1)}, bf16[2,2,2,64,512]{4,3,0,1,2:T(8,128)(2,1)}, u32[]{:S(2)}, u32[]{:S(2)}) collective-permute-start(bf16[2,2,2,64,512]{4,3,0,1,2:T(8,128)(2,1)} %bitcast.243), channel_id=1, source_target_pairs={{0,8},{1,9},{2,10},{3,11},{4,12},{5,13},{6,14},{7,15},{8,0},{9,1},... | collective-permute-start | bytes 1572872 | tf_op jit(solution)/shard_map/ppermute | solution.py:240
  503.1 25.6 %copy-start.23 = (f32[1024,1024]{1,0:T(8,128)}, f32[1024,1024]{1,0:T(8,128)S(1)}, u32[]{:S(2)}) copy-start(f32[1024,1024]{1,0:T(8,128)S(1)} %fusion.6) | copy-start | bytes 12582916
  504.5 16.6 %collective-permute-start.32 = (bf16[2,32,1024]{2,1,0:T(8,128)(2,1)S(1)}, bf16[2,32,1024]{2,1,0:T(8,128)(2,1)S(1)}, u32[]{:S(2)}, u32[]{:S(2)}) collective-permute-start(bf16[2,32,1024]{2,1,0:T(8,128)(2,1)S(1)} %dynamic-slice_bitcast_fusion.5), channel_id=1, source_target_pairs={{0,4},{1,5},{2,6},{3,7},{4,0},{5,1},{6,2},{7,3},{8,12},{9,13},{10,... | collective-permute-start | bytes 393224 | tf_op jit(solution)/shard_map/ppermute | solution.py:240
  521.2 8.3 %collective-permute-start.33 = (bf16[32,1024]{1,0:T(8,128)(2,1)S(1)}, bf16[32,1024]{1,0:T(8,128)(2,1)S(1)}, u32[]{:S(2)}, u32[]{:S(2)}) collective-permute-start(bf16[32,1024]{1,0:T(8,128)(2,1)S(1)} %dynamic-slice_bitcast_fusion.9), channel_id=1, source_target_pairs={{0,16},{1,17},{2,18},{3,19},{4,20},{5,21},{6,22},{7,23},{8,24},{9,... | collective-permute-start | bytes 196616 | tf_op jit(solution)/shard_map/ppermute | solution.py:240
  528.7 34.3 %collective-permute-start.10 = (f32[512,1024]{1,0:T(8,128)}, f32[512,1024]{1,0:T(8,128)S(1)}, u32[]{:S(2)}, u32[]{:S(2)}) collective-permute-start(f32[512,1024]{1,0:T(8,128)} %constant_dynamic-slice_fusion.16), channel_id=1, source_target_pairs={{0,1},{1,0},{2,3},{3,2},{4,5},{5,4},{6,7},{7,6},{8,9},{9,8},{10,11... | collective-permute-start | bytes 6291464 | tf_op jit(solution)/shard_map/ppermute | solution.py:240
  531.5 13.8 %collective-permute-start.17 = (bf16[2,2,64,512]{3,2,0,1:T(8,128)(2,1)S(1)}, bf16[2,2,64,512]{3,2,0,1:T(8,128)(2,1)S(1)}, u32[]{:S(2)}, u32[]{:S(2)}) collective-permute-start(bf16[2,2,64,512]{3,2,0,1:T(8,128)(2,1)S(1)} %dynamic-slice_bitcast_fusion.4), channel_id=1, source_target_pairs={{0,4},{1,5},{2,6},{3,7},{4,0},{5,1},{6,2},{7,3},{8,12},{9,13},{10,... | collective-permute-start | bytes 786440 | tf_op jit(solution)/shard_map/ppermute | solution.py:240
  533.6 11.9 %collective-permute-start.21 = (bf16[2,2,64,512]{3,2,0,1:T(8,128)(2,1)S(1)}, bf16[2,2,64,512]{3,2,0,1:T(8,128)(2,1)S(1)}, u32[]{:S(2)}, u32[]{:S(2)}) collective-permute-start(bf16[2,2,64,512]{3,2,0,1:T(8,128)(2,1)S(1)} %dynamic-slice_bitcast_fusion.3), channel_id=1, source_target_pairs={{0,8},{1,9},{2,10},{3,11},{4,12},{5,13},{6,14},{7,15},{8,0},{9,1},... | collective-permute-start | bytes 786440 | tf_op jit(solution)/shard_map/ppermute | solution.py:240
  534.9 13.2 %collective-permute-start.25 = (bf16[2,2,64,512]{3,2,0,1:T(8,128)(2,1)S(1)}, bf16[2,2,64,512]{3,2,0,1:T(8,128)(2,1)S(1)}, u32[]{:S(2)}, u32[]{:S(2)}) collective-permute-start(bf16[2,2,64,512]{3,2,0,1:T(8,128)(2,1)S(1)} %dynamic-slice_bitcast_fusion.2), channel_id=1, source_target_pairs={{0,2},{1,3},{2,0},{3,1},{4,6},{5,7},{6,4},{7,5},{8,10},{9,11},{10,... | collective-permute-start | bytes 786440 | tf_op jit(solution)/shard_map/ppermute | solution.py:240
  545.3 17.6 %copy-start.24 = (f32[1024,1024]{1,0:T(8,128)S(1)}, f32[1024,1024]{1,0:T(8,128)}, u32[]{:S(2)}) copy-start(f32[1024,1024]{1,0:T(8,128)} %copy-done.23) | copy-start | bytes 12582916
  545.4 5.3 collective-permute-start.18
  545.6 17.4 %copy-start.13 = (bf16[512,1024]{1,0:T(8,128)(2,1)S(1)}, bf16[512,1024]{1,0:T(8,128)(2,1)}, u32[]{:S(2)}) copy-start(bf16[512,1024]{1,0:T(8,128)(2,1)} %param.21) | copy-start | bytes 3145732
  545.6 17.4 %copy-start.41 = (f32[1,1024]{1,0:T(1,128)S(1)}, f32[1,1024]{1,0:T(1,128)}, u32[]{:S(2)}) copy-start(f32[1,1024]{1,0:T(1,128)} %copy-done.40) | copy-start | bytes 12292
  545.6 17.4 %copy-start.50 = (f32[512]{0:T(512)S(1)}, f32[512]{0:T(512)}, u32[]{:S(2)}) copy-start(f32[512]{0:T(512)} %broadcast_multiply_fusion.1) | copy-start | bytes 6148
  545.6 8.3 %collective-permute-start.22 = (bf16[2,64,512]{2,1,0:T(8,128)(2,1)S(1)}, bf16[2,64,512]{2,1,0:T(8,128)(2,1)S(1)}, u32[]{:S(2)}, u32[]{:S(2)}) collective-permute-start(bf16[2,64,512]{2,1,0:T(8,128)(2,1)S(1)} %dynamic-slice_bitcast_fusion.7), channel_id=1, source_target_pairs={{0,2},{1,3},{2,0},{3,1},{4,6},{5,7},{6,4},{7,5},{8,10},{9,11},{10,... | collective-permute-start | bytes 393224 | tf_op jit(solution)/shard_map/ppermute | solution.py:240
  548.2 5.9 collective-permute-start.26
  550.8 8.8 %collective-permute-start.19 = (bf16[64,512]{1,0:T(8,128)(2,1)S(1)}, bf16[64,512]{1,0:T(8,128)(2,1)S(1)}, u32[]{:S(2)}, u32[]{:S(2)}) collective-permute-start(bf16[64,512]{1,0:T(8,128)(2,1)S(1)} %dynamic-slice_bitcast_fusion.12), channel_id=1, source_target_pairs={{0,16},{1,17},{2,18},{3,19},{4,20},{5,21},{6,22},{7,23},{8,24},{9,... | collective-permute-start | bytes 196616 | tf_op jit(solution)/shard_map/ppermute | solution.py:240
  554.0 8.0 %collective-permute-start.23 = (bf16[64,512]{1,0:T(8,128)(2,1)S(1)}, bf16[64,512]{1,0:T(8,128)(2,1)S(1)}, u32[]{:S(2)}, u32[]{:S(2)}) collective-permute-start(bf16[64,512]{1,0:T(8,128)(2,1)S(1)} %dynamic-slice_bitcast_fusion.11), channel_id=1, source_target_pairs={{0,16},{1,17},{2,18},{3,19},{4,20},{5,21},{6,22},{7,23},{8,24},{9,... | collective-permute-start | bytes 196616 | tf_op jit(solution)/shard_map/ppermute | solution.py:240
  554.2 8.6 %collective-permute-start.27 = (bf16[64,512]{1,0:T(8,128)(2,1)S(1)}, bf16[64,512]{1,0:T(8,128)(2,1)S(1)}, u32[]{:S(2)}, u32[]{:S(2)}) collective-permute-start(bf16[64,512]{1,0:T(8,128)(2,1)S(1)} %dynamic-slice_bitcast_fusion.10), channel_id=1, source_target_pairs={{0,16},{1,17},{2,18},{3,19},{4,20},{5,21},{6,22},{7,23},{8,24},{9,... | collective-permute-start | bytes 196616 | tf_op jit(solution)/shard_map/ppermute | solution.py:240
  562.8 12.7 %collective-permute-start.28 = (bf16[32,1536]{1,0:T(8,128)(2,1)S(1)}, bf16[32,1536]{1,0:T(8,128)(2,1)S(1)}, u32[]{:S(2)}, u32[]{:S(2)}) collective-permute-start(bf16[32,1536]{1,0:T(8,128)(2,1)S(1)} %constant_dynamic-slice_fusion.3), channel_id=1, source_target_pairs={{0,1},{1,0},{2,3},{3,2},{4,5},{5,4},{6,7},{7,6},{8,9},{9,8},{10,11... | collective-permute-start | bytes 294920 | tf_op jit(solution)/shard_map/ppermute | solution.py:240
  570.4 5.0 collective-permute-start.11
  575.5 3.8 collective-permute-start.12
  579.3 3.7 collective-permute-start.13
  583.1 3.7 collective-permute-start.14
  586.7 1.2 collective-permute-start.15
  (49 other events, 161.4 us)
Sparse Core Ops, SparseCore 0:
  15.8 118.7 all-gather.2
  137.6 112.9 all-gather.4
  290.6 261.7 reduce-scatter.1

commit v3 on v2

v3 whole, which is shorter than its diff:
```python
from functools import partial
import jax
import jax.numpy as jnp
from jax import lax
from jax.experimental import pallas as pl
from jax.experimental.pallas import tpu as pltpu
from jax.sharding import PartitionSpec as P

HEAD_DIM = 64
PAIR = 2 * HEAD_DIM
IMG = 1370
BLK = 256
STEP = 512
norm_eps = 1e-06
bf16 = jnp.bfloat16
f32 = jnp.float32
NEG = -1e30


def layer_norm(row_values, gain_row, bias_row):
    center = row_values - jnp.mean(row_values, axis=-1, keepdims=True)
    spread = jnp.mean(center * center, axis=-1, keepdims=True)
    return center * lax.rsqrt(spread + norm_eps) * gain_row + bias_row


def product(a, b):
    return jnp.dot(a, b, preferred_element_type=f32)


def inner_rows(a, b):
    return lax.dot_general(a, b, (((0,), (0,)), ((), ())), preferred_element_type=f32)


def against(a, b):
    return lax.dot_general(a, b, (((1,), (1,)), ((), ())), preferred_element_type=f32)


def column_sums(rows):
    return jnp.sum(rows.astype(f32), axis=0)


def head_lanes(h):
    lane = lax.broadcasted_iota(jnp.int32, (1, PAIR), 1)
    return (lane >= h * HEAD_DIM) & (lane < (h + 1) * HEAD_DIM)


def own_head(block, h):
    return jnp.where(head_lanes(h), block, jnp.zeros_like(block))


def over_range(body, lo, hi, block):
    per = STEP // BLK
    start, count = lo[block], hi[block] - lo[block]
    steps = count // per

    def take(step, carried):
        body(start + per * step, step, STEP)
        return carried

    lax.fori_loop(0, steps, take, 0)

    @pl.when(count % per > 0)
    def _():
        body(start + per * steps, steps, BLK)


def apart_of():
    shape = (BLK, STEP)
    return lax.broadcasted_iota(jnp.int32, shape, 1) - lax.broadcasted_iota(jnp.int32, shape, 0)


def block_rows(block, size):
    return pl.ds(pl.multiple_of(block * BLK, BLK), size)


def heads_of(ref):
    return [
        (slice(p, p + PAIR), h) for p in range(0, ref.shape[1], PAIR) for h in range(2)
    ]


def folded(combine, block):
    parts = [block[:, i : i + 128] for i in range(0, block.shape[1], 128)]
    while len(parts) > 1:
        parts = [combine(parts[i], parts[i + 1]) for i in range(0, len(parts), 2)]
    return parts[0]


def attend_kernel(first, lo, hi, q_ref, k_ref, v_ref, ql_ref, kl_ref, o_ref, lse_ref, s_ref, m_ref, l_ref, a_ref):
    block = pl.program_id(1)
    apart = apart_of()
    ql = ql_ref[...]
    heads = heads_of(q_ref)
    q = [own_head(q_ref[:, cols], h) for cols, h in heads]
    m_ref[...] = jnp.full(m_ref.shape, NEG, f32)
    l_ref[...] = jnp.zeros(l_ref.shape, f32)
    a_ref[...] = jnp.zeros(a_ref.shape, f32)

    def scores(kb, step, size):
        rows = block_rows(kb, size)
        seen = (ql == kl_ref[:, rows]) | (apart[:, :size] == (first + block - kb) * BLK)
        for i, (cols, _) in enumerate(heads):
            s = jnp.where(seen, against(q[i], k_ref[rows, cols]), NEG)
            s_ref[i, step, :, :size] = s
            m_ref[i] = jnp.maximum(m_ref[i], folded(jnp.maximum, s))

    over_range(scores, lo, hi, block)
    peaks = [jnp.max(m_ref[i], axis=1, keepdims=True) for i in range(len(heads))]

    def values(kb, step, size):
        rows = block_rows(kb, size)
        for i, (cols, _) in enumerate(heads):
            p = jnp.exp(s_ref[i, step, :, :size] - peaks[i])
            l_ref[i] = l_ref[i] + folded(jnp.add, p)
            a_ref[i] = a_ref[i] + product(p.astype(bf16), v_ref[rows, cols])

    over_range(values, lo, hi, block)
    totals = [jnp.sum(l_ref[i], axis=1, keepdims=True) for i in range(len(heads))]
    first_head = head_lanes(0)
    for i in range(0, len(heads), 2):
        cols = heads[i][0]
        o_ref[:, cols] = jnp.where(first_head, a_ref[i] / totals[i], a_ref[i + 1] / totals[i + 1])
        lse_ref[:, cols] = jnp.where(
            first_head, peaks[i] + jnp.log(totals[i]), peaks[i + 1] + jnp.log(totals[i + 1])
        )


def query_kernel(first, lo, hi, q_ref, k_ref, v_ref, ql_ref, kl_ref, do_ref, lse_ref, o_ref, dq_ref, a_ref):
    block = pl.program_id(1)
    apart = apart_of()
    ql = ql_ref[...]
    heads = heads_of(q_ref)
    q = [own_head(q_ref[:, cols], h) for cols, h in heads]
    do = [own_head(do_ref[:, cols], h) for cols, h in heads]
    lse = [lse_ref[:, i * HEAD_DIM : i * HEAD_DIM + 1] for i in range(len(heads))]
    delta = [
        jnp.sum(own_head(do_ref[:, cols].astype(f32) * o_ref[:, cols], h), axis=1, keepdims=True)
        for cols, h in heads
    ]
    a_ref[...] = jnp.zeros(a_ref.shape, f32)

    def take(kb, step, size):
        rows = block_rows(kb, size)
        seen = (ql == kl_ref[:, rows]) | (apart[:, :size] == (first + block - kb) * BLK)
        for i, (cols, _) in enumerate(heads):
            k = k_ref[rows, cols]
            p = jnp.exp(jnp.where(seen, against(q[i], k), NEG) - lse[i])
            ds = (p * (against(do[i], v_ref[rows, cols]) - delta[i])).astype(bf16)
            a_ref[i] = a_ref[i] + product(ds, k)

    over_range(take, lo, hi, block)
    for i in range(0, len(heads), 2):
        both = jnp.where(head_lanes(0), a_ref[i], a_ref[i + 1])
        dq_ref[:, heads[i][0]] = (both * (HEAD_DIM**-0.5)).astype(bf16)


def key_kernel(
    first, count, lo, hi, q_ref, k_ref, v_ref, ql_ref, kl_ref, g0, g1, g2, g3, g4, st_ref, dk_ref, dv_ref, a_ref, b_ref, do_ref
):
    block = pl.program_id(1)

    @pl.when(block == 0)
    def _():
        rows = q_ref.shape[0] // 8
        at = 0
        for ref in (g0, g1, g2, g3, g4):
            for c in range(ref.shape[0] // (rows + count)):
                do_ref[at : at + rows, :] = ref[c * (rows + count) : c * (rows + count) + rows, :]
                at += rows

    apart = apart_of()
    kl = kl_ref[...]
    heads = heads_of(k_ref)
    k = [own_head(k_ref[:, cols], h) for cols, h in heads]
    v = [own_head(v_ref[:, cols], h) for cols, h in heads]
    a_ref[...] = jnp.zeros(a_ref.shape, f32)
    b_ref[...] = jnp.zeros(b_ref.shape, f32)

    def take(qb, step, size):
        rows = block_rows(qb, size)
        seen = (kl == ql_ref[:, rows]) | (apart[:, :size] == (first + block - qb) * BLK)
        for i, (cols, h) in enumerate(heads):
            q = q_ref[rows, cols]
            do = do_ref[rows, cols]
            at = 2 * (i - h) + h
            p = jnp.exp(jnp.where(seen, against(k[i], q), NEG) - st_ref[at : at + 1, rows])
            ds = (p * (against(v[i], do) - st_ref[at + 2 : at + 3, rows])).astype(bf16)
            a_ref[i] = a_ref[i] + product(ds, q)
            b_ref[i] = b_ref[i] + product(p.astype(bf16), do)

    over_range(take, lo, hi, block)
    for i in range(0, len(heads), 2):
        cols = heads[i][0]
        dk_ref[:, cols] = jnp.where(head_lanes(0), a_ref[i], a_ref[i + 1]).astype(bf16)
        dv_ref[:, cols] = jnp.where(head_lanes(0), b_ref[i], b_ref[i + 1]).astype(bf16)


def dense_kernel(n_ref, gd_ref, wh_ref, wp_ref, bh_ref, act_ref, gh_ref, dw_ref, dbh_ref):
    n = n_ref[...]
    gd = gd_ref[...]
    for u in range(0, wh_ref.shape[2], BLK):
        units = slice(u, u + BLK)
        hidden = product(n, wh_ref[0, :, units]) + bh_ref[0, :, units]
        grad = against(gd, wp_ref[0, units, :])
        below = 0.5 + 0.5 * lax.erf(hidden * 0.7071067811865476)
        act = (hidden * below).astype(bf16)
        gh = grad * (below + hidden * (jnp.exp(-0.5 * hidden * hidden) * 0.3989422804014327))
        gh_low = gh.astype(bf16)
        act_ref[:, units] = act
        gh_ref[:, units] = gh_low
        dbh_ref[0, :, units] = jnp.sum(gh_low.astype(f32), axis=0, keepdims=True)
        dw_ref[1, 0, units, :] = inner_rows(act, gd).astype(bf16)
        dw_ref[0, 0, :, units] = inner_rows(n, gh_low).astype(bf16)


def dense_sum_kernel(act_ref, gh_ref, wh_ref, wp_ref, out_ref, gn_ref):
    @pl.when(pl.program_id(0) == 0)
    def _():
        out_ref[...] = jnp.zeros(out_ref.shape, f32)
        gn_ref[...] = jnp.zeros(gn_ref.shape, f32)

    out_ref[...] += product(act_ref[...], wp_ref[0])
    gn_ref[...] += against(gh_ref[...], wh_ref[0])


def dense_call(n, gd, weights, bias):
    rows, width = n.shape
    parts = weights.shape[0] // 2
    whole = pl.BlockSpec((rows, width), lambda j: (0, 0))
    columns = pl.BlockSpec((rows, width), lambda j: (0, j))
    chunk = pl.BlockSpec((1, width, width), lambda j: (j, 0, 0))
    second = pl.BlockSpec((1, width, width), lambda j: (parts + j, 0, 0))
    row = pl.BlockSpec((1, 1, width), lambda j: (j, 0, 0))
    params = pltpu.CompilerParams(vmem_limit_bytes=56 * 1024 * 1024)
    act, gh, dw, dbh = pl.pallas_call(
        dense_kernel,
        grid=(parts,),
        in_specs=[whole, whole, chunk, second, row],
        out_specs=[columns, columns, pl.BlockSpec((2, 1, width, width), lambda j: (0, j, 0, 0)), row],
        out_shape=[
            jax.ShapeDtypeStruct((rows, parts * width), bf16),
            jax.ShapeDtypeStruct((rows, parts * width), bf16),
            jax.ShapeDtypeStruct((2, parts, width, width), bf16),
            jax.ShapeDtypeStruct((parts, 1, width), f32),
        ],
        compiler_params=params,
        cost_estimate=pl.CostEstimate(flops=35_000_000_000, bytes_accessed=40_000_000, transcendentals=0),
    )(n, gd, weights, weights, bias)
    out, gn = pl.pallas_call(
        dense_sum_kernel,
        grid=(parts,),
        in_specs=[columns, columns, chunk, second],
        out_specs=[whole, whole],
        out_shape=[jax.ShapeDtypeStruct((rows, width), f32)] * 2,
        compiler_params=params,
        cost_estimate=pl.CostEstimate(flops=15_000_000_000, bytes_accessed=25_000_000, transcendentals=0),
    )(act, gh, weights, weights)
    return out, gn, dw.reshape(2 * parts, width, width), dbh


def attention_call(kernel, grid, in_specs, out_specs, out_shape, scratch, flops):
    return pl.pallas_call(
        kernel,
        grid_spec=pltpu.PrefetchScalarGridSpec(
            num_scalar_prefetch=2,
            grid=grid,
            in_specs=in_specs,
            out_specs=out_specs,
            scratch_shapes=scratch,
        ),
        out_shape=out_shape,
        compiler_params=pltpu.CompilerParams(vmem_limit_bytes=48 * 1024 * 1024),
        cost_estimate=pl.CostEstimate(flops=flops, bytes_accessed=8_000_000, transcendentals=0),
    )


def own_bit(bit):
    return (lax.axis_index("dev") >> bit) & 1


def swap(block, bit):
    count = lax.axis_size("dev")
    return lax.ppermute(block, "dev", [(i, i ^ (1 << bit)) for i in range(count)])


def shifted(block, distance):
    count = lax.axis_size("dev")
    return lax.ppermute(block, "dev", [(i, i + distance) for i in range(count) if 0 <= i + distance < count])


def pick(block, axis, index):
    return lax.dynamic_index_in_dim(block, index, axis, keepdims=False)


def halves(blocks, bits, bit, kind=bf16):
    axis = bits.index(bit)
    mine = own_bit(bit)
    sent = jnp.concatenate([pick(b, axis, 1 - mine) for b in blocks], axis=-2).astype(kind)
    kept = jnp.concatenate([pick(b, axis, mine) for b in blocks], axis=-2)
    return kept, swap(sent, bit)


def added(kept, arrived):
    return (kept.astype(f32) + arrived.astype(f32)).astype(arrived.dtype)


class Travelling:
    def __init__(self, block, bits, order, kind=bf16):
        self.block, self.bits, self.order, self.kind = block, list(bits), list(order), kind

    def send(self):
        bit = self.order.pop(0)
        self.kept, self.arriving = halves([self.block], self.bits, bit, self.kind)
        self.bits.remove(bit)

    def receive(self, *beside):
        return received([self], *beside)


def received(travellers, *beside):
    tied = lax.optimization_barrier((*[t.arriving for t in travellers], *beside))
    for part, arrived in zip(travellers, tied):
        part.block = added(part.kept, arrived)
    return tied[len(travellers) :]


def on_device(
    tokens,
    cotangent,
    segment_ids,
    validity,
    first_gain,
    first_bias,
    query_weight,
    query_bias,
    key_weight,
    value_weight,
    value_bias,
    output_weight,
    output_bias,
    attention_scale,
    second_gain,
    second_bias,
    hidden_weight,
    hidden_bias,
    project_weight,
    project_bias,
    dense_scale,
):
    count = lax.axis_size("dev")
    depth = count.bit_length() - 1
    rows, width = tokens.shape
    half = width // 2
    window = 8 * rows
    assert 1 << depth == count and 2 * rows + rows >= IMG - 1 and rows % BLK == 0
    core = own_bit(0)
    shard = query_weight.shape[0]
    ff = hidden_weight.shape[1]
    parts = ff // width

    vectors = jnp.concatenate(
        [
            v.reshape(-1, shard).T
            for v in (
                first_gain,
                first_bias,
                query_bias,
                value_bias,
                output_bias,
                attention_scale,
                second_gain,
                second_bias,
                project_bias,
                dense_scale,
                hidden_bias,
            )
        ],
        axis=1,
    )
    vectors = jnp.pad(vectors, ((0, 0), (0, 128 - vectors.shape[1])))
    attention_pack = jnp.concatenate(
        [w[:, c * half : (c + 1) * half] for c in range(2) for w in (query_weight, key_weight, value_weight)]
        + [output_weight, vectors],
        axis=1,
    )
    hidden_local = hidden_weight.reshape(shard, count, parts, shard).transpose(2, 0, 1, 3).reshape(parts, shard, width)
    dense_pack = jnp.concatenate([hidden_local, project_weight.reshape(parts, shard, width)])
    attention_full = lax.all_gather(attention_pack, "dev", axis=0, tiled=True)
    dense_full = lax.all_gather(dense_pack, "dev", axis=1, tiled=True)

    labels = segment_ids + 1
    tag_rows = jnp.stack(
        [jnp.concatenate([labels % 256, labels // 256]), jnp.concatenate([validity, jnp.zeros_like(validity)])]
    ).astype(bf16)
    tag_rows = jnp.pad(tag_rows, ((0, 14), (0, 0)))
    own = jnp.concatenate([tokens, tag_rows])
    below = shifted(own, 2)
    above = shifted(own, -2)
    far = lax.ppermute(
        own,
        "dev",
        [(i, i - 4) for i in range(4, count, 2)] + [(i, i + 4) for i in range(1, count - 4, 2)],
    )
    mine = jnp.stack([below, own, above, far])
    theirs = swap(mine, 0)
    zero, one = jnp.where(core == 0, mine, theirs), jnp.where(core == 0, theirs, mine)
    blocks = [one[3], zero[0], one[0], zero[1], one[1], zero[2], one[2], zero[3]]
    window_tokens = jnp.concatenate([b[:rows] for b in blocks])
    tags = jnp.stack([b[rows : rows + 2] for b in blocks]).astype(jnp.int32)
    window_labels = (tags[:, 0, :rows] + 256 * tags[:, 0, rows:]).reshape(window)
    window_valid = tags[:, 1, :rows].reshape(window)
    key_label = jnp.where(window_valid == 1, window_labels, 0)
    query_label = jnp.where(window_labels == 0, -1, window_labels)
    first_row, last_row = 3 * rows, 5 * rows
    own_blocks = 2 * rows // BLK
    index = lax.broadcasted_iota(jnp.int32, (own_blocks, window), 1)
    block_labels = window_labels[first_row:last_row].reshape(own_blocks, BLK)
    lo = jnp.min(jnp.where(window_labels[None] == block_labels[:, :1], index, window), axis=1) // BLK
    hi = jnp.max(jnp.where(window_labels[None] == block_labels[:, -1:], index, -1), axis=1) // BLK + 1

    columns = attention_full[:, 4 * width :].T.astype(f32)
    (
        gain_first,
        bias_first,
        bias_query,
        bias_value,
        bias_output,
        scale_first,
        gain_second,
        bias_second,
        bias_project,
        scale_second,
    ) = [columns[i] for i in range(10)]
    bias_hidden = columns[10 : 10 + parts].reshape(parts, 1, width)
    weight_qkv = lax.dynamic_slice_in_dim(attention_full, core * 3 * half, 3 * half, 1)
    weight_output = attention_full[:, 3 * width : 4 * width]

    normed_window = layer_norm(window_tokens.astype(f32), gain_first, bias_first).astype(bf16)
    start = core * half
    bias_qkv = jnp.concatenate(
        [
            lax.dynamic_slice_in_dim(bias_query, start, half),
            jnp.zeros((half,), f32),
            lax.dynamic_slice_in_dim(bias_value, start, half),
        ]
    )
    scale_qkv = jnp.concatenate([jnp.full((half,), HEAD_DIM**-0.5, f32), jnp.ones((2 * half,), f32)])
    projected = ((product(normed_window, weight_qkv) + bias_qkv) * scale_qkv).astype(bf16)

    pairs = half // PAIR
    first = first_row // BLK

    def own_rows(group, lanes=half):
        return pl.BlockSpec((BLK, lanes), lambda h, b, lo, hi: (first + b, group * (half // lanes) + h))

    def all_rows(group, lanes=half):
        return pl.BlockSpec((window, lanes), lambda h, b, lo, hi: (0, group * (half // lanes) + h))

    row_block = pl.BlockSpec((BLK, half), lambda h, b, lo, hi: (b, 0))
    label_rows = pl.BlockSpec((BLK, 1), lambda h, b, lo, hi: (first + b, 0))
    label_all = pl.BlockSpec((1, window), lambda h, b, lo, hi: (0, 0))
    lanes = half // 2
    heads = lanes // HEAD_DIM
    half_block = pl.BlockSpec((BLK, lanes), lambda h, b, lo, hi: (b, h))
    attended_f, lse = attention_call(
        partial(attend_kernel, first),
        (half // lanes, own_blocks),
        [own_rows(0, lanes), all_rows(1, lanes), all_rows(2, lanes), label_rows, label_all],
        [half_block, half_block],
        [jax.ShapeDtypeStruct((2 * rows, half), f32)] * 2,
        [pltpu.VMEM((heads, window // STEP, BLK, STEP), f32)] + [pltpu.VMEM((heads, BLK, PAIR), f32)] * 3,
        50_000_000_000,
    )(lo, hi, projected, projected, projected, query_label[:, None], key_label[None])

    def columns_of(c, mine, theirs):
        return jnp.where(c == 0, jnp.concatenate([mine, theirs], 1), jnp.concatenate([theirs, mine], 1))

    attended_half = attended_f.astype(bf16)
    one_column = (jnp.arange(2 * pairs)[:, None] * HEAD_DIM == jnp.arange(half)[None]).astype(f32)
    lse_rows = lax.dot_general(one_column, lse, (((1,), (1,)), ((), ())), precision=lax.Precision.HIGHEST)
    attended_low = columns_of(
        core,
        lax.dynamic_slice_in_dim(attended_half, core * rows, rows, 0),
        swap(lax.dynamic_slice_in_dim(attended_half, (1 - core) * rows, rows, 0), 0),
    )
    inputs = tokens.astype(f32)
    branch = product(attended_low, weight_output) + bias_output
    middle = inputs + scale_first * branch

    normed_two, second_norm_back = jax.vjp(layer_norm, middle, gain_second, bias_second)
    upstream = cotangent.astype(f32)
    grad_dense = (upstream * scale_second).astype(bf16)
    chip_tokens = window_tokens[first_row:last_row].astype(f32)
    chip_center = chip_tokens - jnp.mean(chip_tokens, axis=-1, keepdims=True)
    chip_inverse = lax.rsqrt(jnp.mean(chip_center * chip_center, axis=-1, keepdims=True) + norm_eps)
    chip_unit = chip_center * chip_inverse
    normed_two_low, lse_rows, chip_unit, chip_inverse = lax.optimization_barrier(
        (normed_two.astype(bf16), lse_rows, chip_unit, chip_inverse)
    )
    dense_sum, grad_normed_two, dense_weight_grads, hidden_bias_grad = dense_call(
        normed_two_low, grad_dense, dense_full, bias_hidden
    )
    project_bias_grad = column_sums(grad_dense)
    grad_middle_norm, second_gain_grad, second_bias_grad = second_norm_back(grad_normed_two)
    grad_middle = upstream + grad_middle_norm
    grad_branch = (grad_middle * scale_first).astype(bf16)
    grad_attended = against(grad_branch, weight_output).astype(bf16)

    dense_sums = lax.psum_scatter(dense_weight_grads, "dev", scatter_dimension=1, tiled=True)
    bits = list(range(depth - 1, -1, -1))
    chips = bits[:-1][::-1]
    axes, far_bits = chips[:3], chips[3:]

    output_weight_grad = inner_rows(attended_low, grad_branch).astype(bf16)
    output_kept, output_other = halves([output_weight_grad.reshape((2,) * depth + (shard, width))], bits, 0)

    grad_half = jnp.where(core == 0, grad_attended[:, :half], grad_attended[:, half:])
    grad_other = swap(jnp.where(core == 0, grad_attended[:, half:], grad_attended[:, :half]), 0)
    grad_pair = jnp.where(
        core == 0, jnp.concatenate([grad_half, grad_other]), jnp.concatenate([grad_other, grad_half])
    )
    member = (jnp.arange(2 * pairs)[:, None] == jnp.arange(half)[None] // HEAD_DIM).astype(f32)
    delta = lax.dot_general(
        member, grad_pair.astype(f32) * attended_f, (((1,), (1,)), ((), ())), precision=lax.Precision.HIGHEST
    )
    stats = jnp.stack([lse_rows.reshape(pairs, 2, -1), delta.reshape(pairs, 2, -1)], axis=1).reshape(4 * pairs, -1)
    top = lax.reduce_precision(stats, 8, 7)
    mid = lax.reduce_precision(stats - top, 8, 7)
    pieces = jnp.concatenate([top, mid, stats - top - mid]).astype(bf16)
    stat_count = pieces.shape[0]
    packed = [jnp.concatenate([grad_pair[c * rows : (c + 1) * rows], pieces[:, c * rows : (c + 1) * rows]]) for c in range(2)]
    both = jnp.concatenate(packed)
    from_below = shifted(both, 2)
    from_above = shifted(both, -2)
    far_below = shifted(packed[1], 4)
    far_above = shifted(packed[0], -4)
    (grad_queries,) = attention_call(
        partial(query_kernel, first),
        (1, own_blocks),
        [own_rows(0), all_rows(1), all_rows(2), label_rows, label_all, row_block, row_block, row_block],
        [row_block],
        [jax.ShapeDtypeStruct((2 * rows, half), bf16)],
        [pltpu.VMEM((2 * pairs, BLK, PAIR), f32)],
        60_000_000_000,
    )(lo, hi, projected, projected, projected, query_label[:, None], key_label[None], grad_pair, lse, attended_f)
    from_below, from_above, far_below, far_above, output_other, grad_queries = lax.optimization_barrier(
        (from_below, from_above, far_below, far_above, output_other, grad_queries)
    )
    normed_pair = normed_window[first_row:last_row]
    chip_view = (2,) * (depth - 1) + (2 * shard, half)

    def weight_sum(grad):
        return inner_rows(normed_pair, grad).astype(bf16).reshape(chip_view)

    output_chip = added(output_kept, output_other)
    output_chip = jnp.concatenate([output_chip[..., :half], output_chip[..., half:]], axis=-2)
    first_part = Travelling(
        jnp.concatenate([weight_sum(grad_queries), output_chip], axis=-1),
        bits[:-1],
        [axes[2]] + far_bits + [axes[0], axes[1]],
    )
    first_part.send()
    unit = rows + stat_count
    own_unit = both
    stat_parts = [far_below[rows:]]
    for piece in (from_below, own_unit, from_above):
        stat_parts += [piece[rows:unit], piece[unit + rows :]]
    stat_parts.append(far_above[rows:])
    stat_window = jnp.concatenate(stat_parts, axis=1).astype(f32)
    third = 4 * pairs
    stat_window = stat_window[:third] + stat_window[third : 2 * third] + stat_window[2 * third :]
    one_unit = pl.BlockSpec((unit, half), lambda h, b, lo, hi: (0, 0))
    two_units = pl.BlockSpec((2 * unit, half), lambda h, b, lo, hi: (0, 0))
    grad_keys, grad_values = attention_call(
        partial(key_kernel, first, stat_count),
        (1, own_blocks),
        [
            all_rows(0),
            own_rows(1),
            own_rows(2),
            label_all,
            label_rows,
            one_unit,
            two_units,
            two_units,
            two_units,
            one_unit,
            pl.BlockSpec((4 * pairs, window), lambda h, b, lo, hi: (0, 0)),
        ],
        [row_block, row_block],
        [jax.ShapeDtypeStruct((2 * rows, half), bf16)] * 2,
        [pltpu.VMEM((2 * pairs, BLK, PAIR), f32)] * 2 + [pltpu.VMEM((window, half), bf16)],
        70_000_000_000,
    )(lo, hi, projected, projected, projected, query_label[None], key_label[:, None], far_below, from_below, own_unit, from_above, far_above, stat_window)

    grad_keys, grad_values, grad_branch, grad_middle, dense_sum = first_part.receive(
        grad_keys, grad_values, grad_branch, grad_middle, dense_sum
    )
    key_part = Travelling(weight_sum(grad_keys), bits[:-1], [axes[0], axes[1], axes[2]] + far_bits)
    value_part = Travelling(weight_sum(grad_values), bits[:-1], [axes[1], axes[2], axes[0]] + far_bits)
    for part in (key_part, value_part, first_part):
        part.send()
    grad_all = jnp.concatenate([grad_queries, grad_keys, grad_values], axis=1)
    grad_normed_pair = against(grad_all, weight_qkv)
    grad_normed_own = lax.dynamic_slice_in_dim(grad_normed_pair, core * rows, rows, 0)
    grad_normed_other = swap(lax.dynamic_slice_in_dim(grad_normed_pair, (1 - core) * rows, rows, 0), 0)
    first_gain_grad = jnp.sum(grad_normed_pair * chip_unit, axis=0)
    first_bias_grad = jnp.sum(grad_normed_pair, axis=0)
    output_bias_grad = column_sums(grad_branch)
    attention_scale_grad = jnp.sum(grad_middle * branch, axis=0)
    dense_out = dense_sum + bias_project
    layer_output = (middle + scale_second * dense_out).astype(bf16)
    dense_scale_grad = jnp.sum(upstream * dense_out, axis=0)

    def placed_half(values):
        spread = jnp.zeros((width,), f32)
        return lax.dynamic_update_slice_in_dim(spread, values, core * half, 0)

    grads = [
        first_gain_grad,
        first_bias_grad,
        placed_half(column_sums(grad_queries)),
        placed_half(column_sums(grad_values)),
        output_bias_grad,
        attention_scale_grad,
        second_gain_grad,
        second_bias_grad,
        project_bias_grad,
        dense_scale_grad,
        hidden_bias_grad.reshape(parts, count, shard).transpose(1, 0, 2),
    ]
    vector_rows = jnp.concatenate([g.reshape(count, -1) for g in grads], axis=1)
    vector_rows = jnp.pad(vector_rows, ((0, 0), (0, -vector_rows.shape[1] % 128)))
    vector_part = Travelling(vector_rows.reshape((2,) * depth + (1, -1)), bits, bits[::-1], f32)
    vector_part.send()
    grad_normed_own, grad_normed_other, layer_output = received(
        (key_part, value_part, first_part, vector_part), grad_normed_own, grad_normed_other, layer_output
    )
    for part in (key_part, value_part, first_part, vector_part):
        part.send()

    grad_normed = grad_normed_own + grad_normed_other
    unit_rows = lax.dynamic_slice_in_dim(chip_unit, core * rows, rows, 0)
    inverse = lax.dynamic_slice_in_dim(chip_inverse, core * rows, rows, 0)
    gained = grad_normed * gain_first
    along = jnp.mean(gained * unit_rows, axis=-1, keepdims=True)
    gained = gained - jnp.mean(gained, axis=-1, keepdims=True) - unit_rows * along
    input_gradient = grad_middle + gained * inverse

    moving = [key_part, value_part, first_part, vector_part]
    swapped = {}

    def to_core(name, part):
        kept = lax.dynamic_slice_in_dim(part.block, core * shard, shard, 0)
        sent = lax.dynamic_slice_in_dim(part.block, (1 - core) * shard, shard, 0)
        if name == "first":
            swapped["output"] = part.block[:, half:]
            kept, sent = kept[:, :half], sent[:, :half]
        swapped[name] = (kept, swap(sent, 0))

    names = {id(key_part): "key", id(value_part): "value", id(first_part): "first"}
    turn = 0
    while moving:
        if turn == 0:
            input_gradient, dense_sums = received(moving, input_gradient, dense_sums)
            project_out = dense_sums[parts:].reshape(parts * shard, width).astype(f32)
            hidden_out = dense_sums[:parts].reshape(parts, shard, count, shard)
            hidden_out = hidden_out.transpose(1, 2, 0, 3).reshape(shard, ff).astype(f32)
        elif turn == 1:
            project_out, hidden_out = received(moving, project_out, hidden_out)
        else:
            received(moving)
        still = []
        for part in moving:
            if part.order:
                part.send()
                still.append(part)
            elif id(part) in names:
                to_core(names[id(part)], part)
        moving = still
        turn += 1
    query_out, key_out, value_out = [columns_of(core, *swapped[n]).astype(f32) for n in ("first", "key", "value")]
    output_out = jnp.concatenate([swapped["output"][:shard], swapped["output"][shard:]], axis=1).astype(f32)
    vector_sum = vector_part.block[0]
    out = [vector_sum[i * shard : (i + 1) * shard] for i in range(10)]
    hidden_bias_out = vector_sum[10 * shard : (10 + parts) * shard]
    return (
        layer_output,
        input_gradient,
        out[0],
        out[1],
        query_out,
        out[2],
        key_out,
        value_out,
        out[3],
        output_out,
        out[4],
        out[5],
        out[6],
        out[7],
        hidden_out,
        hidden_bias_out,
        project_out,
        out[8],
        out[9],
    )


def solution(mesh):
    placed = (
        P("dev", None),
        P("dev", None),
        P("dev"),
        P("dev"),
        P("dev"),
        P("dev"),
        P("dev", None),
        P("dev"),
        P("dev", None),
        P("dev", None),
        P("dev"),
        P("dev", None),
        P("dev"),
        P("dev"),
        P("dev"),
        P("dev"),
        P("dev", None),
        P("dev"),
        P("dev", None),
        P("dev"),
        P("dev"),
    )
    return jax.shard_map(
        on_device,
        mesh=mesh,
        in_specs=placed,
        out_specs=(
            P("dev", None),
            P("dev", None),
            P("dev"),
            P("dev"),
            P("dev", None),
            P("dev"),
            P("dev", None),
            P("dev", None),
            P("dev"),
            P("dev", None),
            P("dev"),
            P("dev"),
            P("dev"),
            P("dev"),
            P("dev", None),
            P("dev"),
            P("dev", None),
            P("dev"),
            P("dev"),
        ),
        check_vma=False,
    )
```

time: 611 us -> 595 us (0.974)
  Pallas kernels: 164 us -> 144 us
  local copies, waits for them, and re-layouts: 81.8 us -> 62.7 us
  starting transfers between devices: 67 us -> 81 us
  waiting for transfers between devices: 179 us -> 187 us
    ppermute x27 -> x25, waiting for transfers between devices: 77 us -> 36 us  [swap(): return lax.ppermute(block, 'dev', [(i, i ^ 1 << bit) for i in range(count)])]
    ppermute x6, waiting for transfers between devices: 47.9 us -> 82.7 us  [shifted(): lax.ppermute(block, 'dev', [(i, i + distance) for i in range(count) if 0...]
    all_gather x1, waiting for transfers between devices: 31.3 us -> 48.2 us  [on_device(): dense_full = lax.all_gather(dense_pack, 'dev', axis=1, tiled=True)]
    ppermute x27 -> x25, starting transfers between devices: 46.9 us -> 61 us  [swap(): return lax.ppermute(block, 'dev', [(i, i ^ 1 << bit) for i in range(count)])]
    pallas_call x1, Pallas kernels: 37.5 us -> 25.5 us  [dense_call(): pl.pallas_call(dense_kernel, grid=(parts,), in_specs=[whole, whole, chunk...]
    unnamed x157 -> x144, local copies, waits for them, and re-layouts: 35.8 us -> 24.3 us
    reshape x5 -> x1, local copies, waits for them, and re-layouts: 10.3 us -> 0.05 us  [on_device(): jnp.stack([lse_rows.reshape(pairs, 2, -1), delta.reshape(pairs, 2, -1)],...]
    convert_element_type x0 -> x3, local copies, waits for them, and re-layouts: none -> 8.22 us  [on_device(): hidden_out = hidden_out.transpose(1, 2, 0, 3).reshape(shard, ff).astype(f32)]
  transfers between devices with their start and end apart: 37 -> 35, of which waited for: 19 -> 17; matrix products, arithmetic and copies ran while one was open for 24% -> 24% of each run, Pallas kernels for 21% -> 20%
where the time goes in v3:
time: 595 us; the launch traced here: 592 us
  waiting for transfers between devices  187 us (31%)
  Pallas kernels  144 us (24%)
  starting transfers between devices  81 us (14%)
  local copies, waits for them, and re-layouts  62.7 us (11%)
  other arithmetic  56.1 us (9%)
  matrix products  46.4 us (8%)
  between operations  15.5 us (3%)
    ppermute x6, waiting for transfers between devices, shifted(): lax.ppermute(block, 'dev', [(i, i + distance) for i in range(count) if 0...  82.7 us
    ppermute x25, starting transfers between devices, swap(): return lax.ppermute(block, 'dev', [(i, i ^ 1 << bit) for i in range(count)])  61 us
    all_gather x1, waiting for transfers between devices, on_device(): dense_full = lax.all_gather(dense_pack, 'dev', axis=1, tiled=True)  48.2 us
    pallas_call x1, Pallas kernels, on_device(): attention_call(partial(key_kernel, first, stat_count), (1, own_blocks), [...  38.6 us
    ppermute x25, waiting for transfers between devices, swap(): return lax.ppermute(block, 'dev', [(i, i ^ 1 << bit) for i in range(count)])  36 us
    pallas_call x1, Pallas kernels, on_device(): attention_call(partial(query_kernel, first), (1, own_blocks), [own_rows(0...  34.7 us
    pallas_call x1, Pallas kernels, on_device(): attention_call(partial(attend_kernel, first), (half // lanes, own_blocks)...  29.8 us
    pallas_call x1, Pallas kernels, dense_call(): pl.pallas_call(dense_kernel, grid=(parts,), in_specs=[whole, whole, chunk...  25.5 us
  transfers between devices with their start and end apart: 35, of which 17 were waited for; matrix products, arithmetic and copies ran while one was open for 24% of the time, Pallas kernels for 20%

profile of v3, /device:TPU:0, one launch (start us, length us, event | category | flops | bytes accessed | tf_op | source)
XLA Modules:
  0.0 592.2 jit_solution(16285168245916011253)
XLA Ops:
  20.1 4.9 collective-permute-start
  27.8 45.4 %collective-permute-done = bf16[528,1024]{1,0:T(8,128)(2,1)S(1)} collective-permute-done((bf16[528,1024]{1,0:T(8,128)(2,1)S(1)}, bf16[528,1024]{1,0:T(8,128)(2,1)S(1)}, u32[]{:S(2)}, u32[]{:S(2)}) %collective-permute-start) | collective-permute-done | bytes 1081376 | tf_op jit(solution)/shard_map/ppermute | solution.py:288
  73.1 1.9 collective-permute-done.1
  75.1 2.4 pad_maximum_fusion
  77.5 7.7 %collective-permute-done.3 = bf16[4,528,1024]{2,1,0:T(8,128)(2,1)} collective-permute-done((bf16[4,528,1024]{2,1,0:T(8,128)(2,1)}, bf16[4,528,1024]{2,1,0:T(8,128)(2,1)}, u32[]{:S(2)}, u32[]{:S(2)}) %collective-permute-start.3) | collective-permute-done | bytes 4325408 | tf_op jit(solution)/shard_map/ppermute | solution.py:283
  85.2 2.9 broadcast_select_fusion
  88.3 1.9 copy-done.7
  104.7 2.5 copy-done.3
  107.2 2.8 fusion.2
  110.0 2.5 fusion.6
  112.6 2.3 broadcast_select_fusion.2
  114.9 19.7 %all-gather.3.cloned.1.call-done = bf16[1024,4224]{1,0:T(8,128)(2,1)} async-done(((bf16[32,4224]{1,0:T(8,128)(2,1)}), bf16[1024,4224]{1,0:T(8,128)(2,1)}) %all-gather.3.cloned.1.call-update) | async-done | bytes 8650768 | tf_op jit(solution)/shard_map/all_gather | solution.py:388
  136.5 5.8 fusion.5
  142.4 19.9 %multiply_convert_fusion.q_ref.k_ref.v_ref = bf16[4096,1536]{1,0:T(8,128)(2,1)} fusion(bf16[4096,1024]{1,0:T(8,128)(2,1)S(1)} %fusion.5, f32[1536]{0:T(1024)S(1)} %copy-done.54, f32[1536]{0:T(1024)S(1)} %pad_maximum_fusion.9, bf16[1024,4224]{1,0:T(8,128)(2,1)} %all-gather.3.cloned.1.call-done, s32[]{:T(128)S(6)} %select_n.244), kind=kOutput, calls=%fused_computation | convolution fusion | flops 12903776256 | bytes 24129540 | tf_op jit(solution)/shard_map/dot_general | solution.py:27
  162.2 29.8 %shard_map.348 = (f32[1024,512]{1,0:T(8,128)S(1)}, f32[1024,512]{1,0:T(8,128)S(1)}) custom-call(s32[4]{0:T(128)S(1)} %get-tuple-element.200.lo, s32[4]{0:T(128)S(1)} %get-tuple-element.201.hi, bf16[4096,1536]{1,0:T(8,128)(2,1)} %multiply_convert_fusion.q_ref.k_ref.v_ref, bf16[4096,1536]{1,0:T(8,128)(2,1)} %multiply_convert_fusion.q_ref.k_ref.v_ref, ...), custom_call_target="tpu_custom_call" | custom-call | flops 49999998976 | bytes 8000000 | tf_op jit(solution)/shard_map/pallas_call | solution.py:465
  196.4 4.7 fusion.101
  202.9 48.2 %all-gather.5.cloned.1.call-done.wh_ref.wp_ref = bf16[8,1024,1024]{2,1,0:T(8,128)(2,1)} async-done(((bf16[8,32,1024]{2,1,0:T(8,128)(2,1)}), bf16[8,1024,1024]{2,1,0:T(8,128)(2,1)}) %all-gather.5.cloned.1.call-update) | async-done | bytes 16777232 | tf_op jit(solution)/shard_map/all_gather | solution.py:389
  251.1 25.5 %shard_map.349 = (bf16[512,4096]{1,0:T(8,128)(2,1)}, bf16[512,4096]{1,0:T(8,128)(2,1)}, bf16[2,4,1024,1024]{3,2,1,0:T(8,128)(2,1)}, f32[4,1,1024]{2,1,0:T(1,128)}) custom-call(bf16[512,1024]{1,0:T(8,128)(2,1)} %add_convert_fusion.1.n_ref, bf16[512,1024]{1,0:T(8,128)(2,1)} %get-tuple-element.126.gd_ref, ...), custom_call_target="tpu_custom_call" | custom-call | flops 35000000512 | bytes 40000000 | tf_op jit(solution)/shard_map/pallas_call | solution.py:235
  277.4 15.1 %shard_map.350 = (f32[512,1024]{1,0:T(8,128)}, f32[512,1024]{1,0:T(8,128)}) custom-call(bf16[512,4096]{1,0:T(8,128)(2,1)} %get-tuple-element.70.act_ref, bf16[512,4096]{1,0:T(8,128)(2,1)} %get-tuple-element.71.gh_ref, bf16[8,1024,1024]{2,1,0:T(8,128)(2,1)} %all-gather.5.cloned.1.call-done.wh_ref.wp_ref, ...), custom_call_target="tpu_custom_call" | custom-call | flops 15000000512 | bytes 25000000 | tf_op jit(solution)/shard_map/pallas_call | solution.py:249
  292.5 2.5 multiply_reduce_fusion.2
  297.6 3.3 fusion.43
  312.5 3.6 collective-permute-start.6
  318.8 6.0 %collective-permute-start.8 = (bf16[560,512]{1,0:T(8,128)(2,1)S(1)}, bf16[560,512]{1,0:T(8,128)(2,1)S(1)}, u32[]{:S(2)}, u32[]{:S(2)}) collective-permute-start(bf16[560,512]{1,0:T(8,128)(2,1)S(1)} %pad_maximum_fusion.4), channel_id=1, source_target_pairs={{0,4},{1,5},{2,6},{3,7},{4,8},{5,9},{6,10},{7,11},{8,12},{9,13},{1... | collective-permute-start | bytes 1720328 | tf_op jit(solution)/shard_map/ppermute | solution.py:288
  324.9 34.7 %shard_map.351 = bf16[1024,512]{1,0:T(8,128)(2,1)S(1)} custom-call(s32[4]{0:T(128)S(1)} %get-tuple-element.200.lo, s32[4]{0:T(128)S(1)} %get-tuple-element.201.hi, bf16[4096,1536]{1,0:T(8,128)(2,1)} %multiply_convert_fusion.q_ref.k_ref.v_ref, bf16[4096,1536]{1,0:T(8,128)(2,1)} %multiply_convert_fusion.q_ref.k_ref.v_ref, ...), custom_call_target="tpu_custom_call" | custom-call | flops 60000002048 | bytes 8000000 | tf_op jit(solution)/shard_map/pallas_call | solution.py:537
  359.6 18.9 %collective-permute-done.8.g0 = bf16[560,512]{1,0:T(8,128)(2,1)S(1)} collective-permute-done((bf16[560,512]{1,0:T(8,128)(2,1)S(1)}, bf16[560,512]{1,0:T(8,128)(2,1)S(1)}, u32[]{:S(2)}, u32[]{:S(2)}) %collective-permute-start.8) | collective-permute-done | bytes 573472 | tf_op jit(solution)/shard_map/ppermute | solution.py:288
  378.4 12.9 %collective-permute-done.6.g1 = bf16[1120,512]{1,0:T(8,128)(2,1)S(1)} collective-permute-done((bf16[1120,512]{1,0:T(8,128)(2,1)S(1)}, bf16[1120,512]{1,0:T(8,128)(2,1)S(1)}, u32[]{:S(2)}, u32[]{:S(2)}) %collective-permute-start.6) | collective-permute-done | bytes 1146912 | tf_op jit(solution)/shard_map/ppermute | solution.py:288
  391.3 3.7 collective-permute-done.7.g3
  395.1 1.9 fusion.20
  397.2 2.9 fusion.34
  402.1 38.6 %shard_map.352 = (bf16[1024,512]{1,0:T(8,128)(2,1)S(1)}, bf16[1024,512]{1,0:T(8,128)(2,1)S(1)}) custom-call(s32[4]{0:T(128)S(1)} %get-tuple-element.200.lo, s32[4]{0:T(128)S(1)} %get-tuple-element.201.hi, bf16[4096,1536]{1,0:T(8,128)(2,1)} %multiply_convert_fusion.q_ref.k_ref.v_ref, bf16[4096,1536]{1,0:T(8,128)(2,1)} %multiply_convert_fusion.q_ref.k_ref.v_ref, ...), custom_call_target="tpu_custom_call" | custom-call | flops 70000001024 | bytes 8000000 | tf_op jit(solution)/shard_map/pallas_call | solution.py:574
  441.5 6.3 %fusion.97 = (f32[1024]{0:T(1024)S(1)}, f32[1024]{0:T(1024)S(1)}, f32[1024,1024]{1,0:T(8,128)S(1)}) fusion(f32[1024,1024]{1,0:T(8,128)} %fusion.6, bf16[1024,4224]{1,0:T(8,128)(2,1)} %all-gather.3.cloned.1.call-done, s32[]{:T(128)S(6)} %select_n.244, bf16[1024,512]{1,0:T(8,128)(2,1)S(1)} %get-tuple-element.84, ...), kind=kOutput, calls=%fused_computation.294 | convolution fusion | flops 3233806336 | bytes 14688260 | tf_op jit(solution)/shard_map/dot_general | solution.py:35
  447.9 2.5 constant_dynamic-slice_fusion.15
  455.3 2.0 fusion.19
  458.2 17.1 %collective-permute-start.14 = (bf16[2,2,64,1024]{3,2,0,1:T(8,128)(2,1)}, bf16[2,2,64,1024]{3,2,0,1:T(8,128)(2,1)}, u32[]{:S(2)}, u32[]{:S(2)}) collective-permute-start(bf16[2,2,64,1024]{3,2,0,1:T(8,128)(2,1)} %dynamic-slice_bitcast_fusion.1), channel_id=1, source_target_pairs={{0,16},{1,17},{2,18},{3,19},{4,20},{5,21},{6,22},{7,23},{8,24},{9,... | collective-permute-start | bytes 1572872 | tf_op jit(solution)/shard_map/ppermute | solution.py:283
  475.3 2.9 fusion.40
  479.9 13.8 %collective-permute-start.13 = (bf16[2,2,2,64,512]{4,3,0,2,1:T(8,128)(2,1)}, bf16[2,2,2,64,512]{4,3,0,2,1:T(8,128)(2,1)}, u32[]{:S(2)}, u32[]{:S(2)}) collective-permute-start(bf16[2,2,2,64,512]{4,3,0,2,1:T(8,128)(2,1)} %bitcast.217), channel_id=1, source_target_pairs={{0,4},{1,5},{2,6},{3,7},{4,0},{5,1},{6,2},{7,3},{8,12},{9,13},{10,... | collective-permute-start | bytes 1572872 | tf_op jit(solution)/shard_map/ppermute | solution.py:283
  493.8 2.9 fusion.37
  503.9 13.4 %collective-permute-done.13 = bf16[2,2,2,64,512]{4,3,0,2,1:T(8,128)(2,1)} collective-permute-done((bf16[2,2,2,64,512]{4,3,0,2,1:T(8,128)(2,1)}, bf16[2,2,2,64,512]{4,3,0,2,1:T(8,128)(2,1)}, u32[]{:S(2)}, u32[]{:S(2)}) %collective-permute-start.13) | collective-permute-done | bytes 524320 | tf_op jit(solution)/shard_map/ppermute | solution.py:283
  517.2 7.2 %collective-permute-done.12 = bf16[2,2,2,64,512]{4,3,0,1,2:T(8,128)(2,1)} collective-permute-done((bf16[2,2,2,64,512]{4,3,0,1,2:T(8,128)(2,1)}, bf16[2,2,2,64,512]{4,3,0,1,2:T(8,128)(2,1)}, u32[]{:S(2)}, u32[]{:S(2)}) %collective-permute-start.12) | collective-permute-done | bytes 524320 | tf_op jit(solution)/shard_map/ppermute | solution.py:283
  529.5 13.2 %collective-permute-start.18 = (bf16[2,2,64,512]{3,2,0,1:T(8,128)(2,1)S(1)}, bf16[2,2,64,512]{3,2,0,1:T(8,128)(2,1)S(1)}, u32[]{:S(2)}, u32[]{:S(2)}) collective-permute-start(bf16[2,2,64,512]{3,2,0,1:T(8,128)(2,1)S(1)} %dynamic-slice_bitcast_fusion.3), channel_id=1, source_target_pairs={{0,8},{1,9},{2,10},{3,11},{4,12},{5,13},{6,14},{7,15},{8,0},{9,1},... | collective-permute-start | bytes 786440 | tf_op jit(solution)/shard_map/ppermute | solution.py:283
  544.0 2.2 fusion.98
  548.0 2.3 collective-permute-done.17
  555.6 2.0 collective-permute-start.22
  559.9 3.1 copy.149
  563.1 4.4 reshape.462
  569.2 2.1 collective-permute-start.27
  572.4 3.0 collective-permute-start.25
  578.3 2.5 collective-permute-start.28
  (353 shorter events, 98.9 us)
Async XLA Ops:
  7.2 127.5 %all-gather.3.cloned.1.call-start = ((), (), s32[]{:S(2)}) async-start(), calls=%async_computation.1 | async-start | bytes 8921088 | tf_op jit(solution)/shard_map/all_gather | solution.py:388
  15.7 235.4 %all-gather.5.cloned.1.call-start = ((), (), s32[]{:S(2)}) async-start(), calls=%async_computation.2 | async-start | bytes 17301504 | tf_op jit(solution)/shard_map/all_gather | solution.py:389
  19.7 530.6 %reduce-scatter.2.cloned.1.call-start = ((), (), s32[]{:S(2)}) async-start(), calls=%async_computation.3 | async-start | bytes 17301504 | tf_op jit(solution)/shard_map/reduce_scatter | solution.py:509
  20.1 53.1 %collective-permute-start = (bf16[528,1024]{1,0:T(8,128)(2,1)S(1)}, bf16[528,1024]{1,0:T(8,128)(2,1)S(1)}, u32[]{:S(2)}, u32[]{:S(2)}) collective-permute-start(bf16[528,1024]{1,0:T(8,128)(2,1)S(1)} %get-tuple-element.144), channel_id=1, source_target_pairs={{0,2},{1,3},{2,4},{3,5},{4,6},{5,7},{6,8},{7,9},{8,10},{9,11},{10,... | collective-permute-start | bytes 3244040 | tf_op jit(solution)/shard_map/ppermute | solution.py:288
  25.0 50.1 %collective-permute-start.1 = (bf16[528,1024]{1,0:T(8,128)(2,1)S(1)}, bf16[528,1024]{1,0:T(8,128)(2,1)S(1)}, u32[]{:S(2)}, u32[]{:S(2)}) collective-permute-start(bf16[528,1024]{1,0:T(8,128)(2,1)S(1)} %get-tuple-element.144), channel_id=1, source_target_pairs={{2,0},{3,1},{4,2},{5,3},{6,4},{7,5},{8,6},{9,7},{10,8},{11,9},{12,... | collective-permute-start | bytes 3244040 | tf_op jit(solution)/shard_map/ppermute | solution.py:288
  26.3 48.8 %collective-permute-start.2 = (bf16[528,1024]{1,0:T(8,128)(2,1)S(1)}, bf16[528,1024]{1,0:T(8,128)(2,1)S(1)}, u32[]{:S(2)}, u32[]{:S(2)}) collective-permute-start(bf16[528,1024]{1,0:T(8,128)(2,1)S(1)} %get-tuple-element.144), channel_id=1, source_target_pairs={{4,0},{6,2},{8,4},{10,6},{12,8},{14,10},{16,12},{18,14},{20,16},{2... | collective-permute-start | bytes 3244040 | tf_op jit(solution)/shard_map/ppermute | solution.py:399
  77.5 7.7 %collective-permute-start.3 = (bf16[4,528,1024]{2,1,0:T(8,128)(2,1)}, bf16[4,528,1024]{2,1,0:T(8,128)(2,1)}, u32[]{:S(2)}, u32[]{:S(2)}) collective-permute-start(bf16[4,528,1024]{2,1,0:T(8,128)(2,1)} %pad_maximum_fusion), channel_id=1, source_target_pairs={{0,1},{1,0},{2,3},{3,2},{4,5},{5,4},{6,7},{7,6},{8,9},{9,8},{10,11... | collective-permute-start | bytes 12976136 | tf_op jit(solution)/shard_map/ppermute | solution.py:283
  136.4 56.8 %copy-start.39 = (f32[1,1024]{1,0:T(1,128)}, f32[1,1024]{1,0:T(1,128)S(1)}, u32[]{:S(2)}) copy-start(f32[1,1024]{1,0:T(1,128)S(1)} %get-tuple-element.160) | copy-start | bytes 12292
  136.4 60.0 %copy-start.46 = (f32[1,1024]{1,0:T(1,128)}, f32[1,1024]{1,0:T(1,128)S(1)}, u32[]{:S(2)}) copy-start(f32[1,1024]{1,0:T(1,128)S(1)} %get-tuple-element.163) | copy-start | bytes 12292
  142.4 19.9 %copy-start.17 = (bf16[4096,1024]{1,0:T(8,128)(2,1)}, bf16[4096,1024]{1,0:T(8,128)(2,1)S(1)}, u32[]{:S(2)}) copy-start(bf16[4096,1024]{1,0:T(8,128)(2,1)S(1)} %fusion.5) | copy-start | bytes 25165828
  192.0 119.0 %copy-start = (f32[1024,512]{1,0:T(8,128)}, f32[1024,512]{1,0:T(8,128)S(1)}, u32[]{:S(2)}) copy-start(f32[1024,512]{1,0:T(8,128)S(1)} %get-tuple-element.67.o_ref) | copy-start | bytes 6291460
  192.3 4.1 collective-permute-start.4
  277.4 15.1 %copy-start.5 = (f32[512,1024]{1,0:T(8,128)S(1)}, f32[512,1024]{1,0:T(8,128)}, u32[]{:S(2)}) copy-start(f32[512,1024]{1,0:T(8,128)} %copy-done.4) | copy-start | bytes 6291460
  301.8 6.5 %collective-permute-start.5 = (bf16[512,512]{1,0:T(8,128)(2,1)S(1)}, bf16[512,512]{1,0:T(8,128)(2,1)S(1)}, u32[]{:S(2)}, u32[]{:S(2)}) collective-permute-start(bf16[512,512]{1,0:T(8,128)(2,1)S(1)} %get-tuple-element.154), channel_id=1, source_target_pairs={{0,1},{1,0},{2,3},{3,2},{4,5},{5,4},{6,7},{7,6},{8,9},{9,8},{10,11... | collective-permute-start | bytes 1572872 | tf_op jit(solution)/shard_map/ppermute | solution.py:283
  305.9 53.7 %collective-permute-start.10 = (bf16[2,2,2,2,32,1024]{5,4,2,3,0,1:T(8,128)(2,1)}, bf16[2,2,2,2,32,1024]{5,4,2,3,0,1:T(8,128)(2,1)}, u32[]{:S(2)}, u32[]{:S(2)}) collective-permute-start(bf16[2,2,2,2,32,1024]{5,4,2,3,0,1:T(8,128)(2,1)} %bitcast.215), channel_id=1, source_target_pairs={{0,1},{1,0},{2,3},{3,2},{4,5},{5,4},{6,7},{7,6},{8,9},{9,8},{10,11... | collective-permute-start | bytes 3145736 | tf_op jit(solution)/shard_map/ppermute | solution.py:283
  312.5 78.8 %collective-permute-start.6 = (bf16[1120,512]{1,0:T(8,128)(2,1)S(1)}, bf16[1120,512]{1,0:T(8,128)(2,1)S(1)}, u32[]{:S(2)}, u32[]{:S(2)}) collective-permute-start(bf16[1120,512]{1,0:T(8,128)(2,1)S(1)} %pad_maximum_fusion.2.g2), channel_id=1, source_target_pairs={{0,2},{1,3},{2,4},{3,5},{4,6},{5,7},{6,8},{7,9},{8,10},{9,11},{10,... | collective-permute-start | bytes 3440648 | tf_op jit(solution)/shard_map/ppermute | solution.py:288
  316.1 78.8 %collective-permute-start.7 = (bf16[1120,512]{1,0:T(8,128)(2,1)S(1)}, bf16[1120,512]{1,0:T(8,128)(2,1)S(1)}, u32[]{:S(2)}, u32[]{:S(2)}) collective-permute-start(bf16[1120,512]{1,0:T(8,128)(2,1)S(1)} %pad_maximum_fusion.2.g2), channel_id=1, source_target_pairs={{2,0},{3,1},{4,2},{5,3},{6,4},{7,5},{8,6},{9,7},{10,8},{11,9},{12,... | collective-permute-start | bytes 3440648 | tf_op jit(solution)/shard_map/ppermute | solution.py:288
  317.5 42.1 %collective-permute-start.9 = (bf16[560,512]{1,0:T(8,128)(2,1)S(1)}, bf16[560,512]{1,0:T(8,128)(2,1)S(1)}, u32[]{:S(2)}, u32[]{:S(2)}) collective-permute-start(bf16[560,512]{1,0:T(8,128)(2,1)S(1)} %pad_maximum_fusion.5), channel_id=1, source_target_pairs={{4,0},{5,1},{6,2},{7,3},{8,4},{9,5},{10,6},{11,7},{12,8},{13,9},{1... | collective-permute-start | bytes 1720328 | tf_op jit(solution)/shard_map/ppermute | solution.py:288
  318.8 59.6 %collective-permute-start.8 = (bf16[560,512]{1,0:T(8,128)(2,1)S(1)}, bf16[560,512]{1,0:T(8,128)(2,1)S(1)}, u32[]{:S(2)}, u32[]{:S(2)}) collective-permute-start(bf16[560,512]{1,0:T(8,128)(2,1)S(1)} %pad_maximum_fusion.4), channel_id=1, source_target_pairs={{0,4},{1,5},{2,6},{3,7},{4,8},{5,9},{6,10},{7,11},{8,12},{9,13},{1... | collective-permute-start | bytes 1720328 | tf_op jit(solution)/shard_map/ppermute | solution.py:288
  359.5 35.6 %copy-start.19 = (bf16[2,2,2,2,1,32,1024]{6,5,4,3,2,1,0:T(8,128)(2,1)S(1)}, bf16[2,2,2,2,1,32,1024]{6,5,4,3,2,1,0:T(8,128)(2,1)}, u32[]{:S(2)}) copy-start(bf16[2,2,2,2,1,32,1024]{6,5,4,3,2,1,0:T(8,128)(2,1)} %get-tuple-element.141) | copy-start | bytes 3145732
  402.1 39.4 %collective-permute-start.11 = (bf16[2,2,2,64,1024]{4,3,1,2,0:T(8,128)(2,1)}, bf16[2,2,2,64,1024]{4,3,1,2,0:T(8,128)(2,1)}, u32[]{:S(2)}, u32[]{:S(2)}) collective-permute-start(bf16[2,2,2,64,1024]{4,3,1,2,0:T(8,128)(2,1)} %dynamic-slice_bitcast_fusion), channel_id=1, source_target_pairs={{0,8},{1,9},{2,10},{3,11},{4,12},{5,13},{6,14},{7,15},{8,0},{9,1},... | collective-permute-start | bytes 3145736 | tf_op jit(solution)/shard_map/ppermute | solution.py:283
  450.3 74.1 %collective-permute-start.16 = (f32[512,1024]{1,0:T(8,128)}, f32[512,1024]{1,0:T(8,128)}, u32[]{:S(2)}, u32[]{:S(2)}) collective-permute-start(f32[512,1024]{1,0:T(8,128)} %get-tuple-element.135), channel_id=1, source_target_pairs={{0,1},{1,0},{2,3},{3,2},{4,5},{5,4},{6,7},{7,6},{8,9},{9,8},{10,11... | collective-permute-start | bytes 6291464 | tf_op jit(solution)/shard_map/ppermute | solution.py:283
  457.3 20.9 %copy-start.22 = (bf16[2,2,2,64,1024]{4,3,1,2,0:T(8,128)(2,1)}, bf16[2,2,2,64,1024]{4,3,1,2,0:T(8,128)(2,1)S(1)}, u32[]{:S(2)}) copy-start(bf16[2,2,2,64,1024]{4,3,1,2,0:T(8,128)(2,1)S(1)} %fusion.19) | copy-start | bytes 3145732
  458.2 45.7 %collective-permute-start.14 = (bf16[2,2,64,1024]{3,2,0,1:T(8,128)(2,1)}, bf16[2,2,64,1024]{3,2,0,1:T(8,128)(2,1)}, u32[]{:S(2)}, u32[]{:S(2)}) collective-permute-start(bf16[2,2,64,1024]{3,2,0,1:T(8,128)(2,1)} %dynamic-slice_bitcast_fusion.1), channel_id=1, source_target_pairs={{0,16},{1,17},{2,18},{3,19},{4,20},{5,21},{6,22},{7,23},{8,24},{9,... | collective-permute-start | bytes 1572872 | tf_op jit(solution)/shard_map/ppermute | solution.py:283
  479.9 37.3 %collective-permute-start.13 = (bf16[2,2,2,64,512]{4,3,0,2,1:T(8,128)(2,1)}, bf16[2,2,2,64,512]{4,3,0,2,1:T(8,128)(2,1)}, u32[]{:S(2)}, u32[]{:S(2)}) collective-permute-start(bf16[2,2,2,64,512]{4,3,0,2,1:T(8,128)(2,1)} %bitcast.217), channel_id=1, source_target_pairs={{0,4},{1,5},{2,6},{3,7},{4,0},{5,1},{6,2},{7,3},{8,12},{9,13},{10,... | collective-permute-start | bytes 1572872 | tf_op jit(solution)/shard_map/ppermute | solution.py:283
  497.6 28.7 %copy-start.23 = (bf16[2,2,2,64,1024]{4,3,1,2,0:T(8,128)(2,1)S(1)}, bf16[2,2,2,64,1024]{4,3,1,2,0:T(8,128)(2,1)}, u32[]{:S(2)}) copy-start(bf16[2,2,2,64,1024]{4,3,1,2,0:T(8,128)(2,1)} %copy-done.22) | copy-start | bytes 3145732
  498.5 26.0 %collective-permute-start.12 = (bf16[2,2,2,64,512]{4,3,0,1,2:T(8,128)(2,1)}, bf16[2,2,2,64,512]{4,3,0,1,2:T(8,128)(2,1)}, u32[]{:S(2)}, u32[]{:S(2)}) collective-permute-start(bf16[2,2,2,64,512]{4,3,0,1,2:T(8,128)(2,1)} %bitcast.218), channel_id=1, source_target_pairs={{0,2},{1,3},{2,0},{3,1},{4,6},{5,7},{6,4},{7,5},{8,10},{9,11},{10,... | collective-permute-start | bytes 1572872 | tf_op jit(solution)/shard_map/ppermute | solution.py:283
  500.5 27.6 %copy-start.26 = (bf16[2,2,1,2,64,512]{5,4,3,2,1,0:T(8,128)(2,1)S(1)}, bf16[2,2,1,2,64,512]{5,4,3,2,1,0:T(8,128)(2,1)}, u32[]{:S(2)}) copy-start(bf16[2,2,1,2,64,512]{5,4,3,2,1,0:T(8,128)(2,1)} %get-tuple-element.145) | copy-start | bytes 1572868
  501.3 41.3 %copy-start.27 = (bf16[2,2,2,1,64,512]{5,4,3,2,1,0:T(8,128)(2,1)S(1)}, bf16[2,2,2,1,64,512]{5,4,3,2,1,0:T(8,128)(2,1)}, u32[]{:S(2)}) copy-start(bf16[2,2,2,1,64,512]{5,4,3,2,1,0:T(8,128)(2,1)} %get-tuple-element.147) | copy-start | bytes 1572868
  501.6 1.3 collective-permute-start.15
  524.5 23.5 %collective-permute-start.20 = (f32[2,2,2,1,512]{4,3,2,1,0:T(1,128)S(1)}, f32[2,2,2,1,512]{4,3,2,1,0:T(1,128)S(1)}, u32[]{:S(2)}, u32[]{:S(2)}) collective-permute-start(f32[2,2,2,1,512]{4,3,2,1,0:T(1,128)S(1)} %dynamic-slice_bitcast_fusion.11), channel_id=1, source_target_pairs={{0,2},{1,3},{2,0},{3,1},{4,6},{5,7},{6,4},{7,5},{8,10},{9,11},{10,... | collective-permute-start | bytes 49160 | tf_op jit(solution)/shard_map/ppermute | solution.py:283
  526.2 17.8 %copy-start.14 = (f32[512,1024]{1,0:T(8,128)S(1)}, f32[512,1024]{1,0:T(8,128)}, u32[]{:S(2)}) copy-start(f32[512,1024]{1,0:T(8,128)} %get-tuple-element.96) | copy-start | bytes 6291460
  527.7 20.4 %collective-permute-start.19 = (bf16[2,64,1024]{2,1,0:T(8,128)(2,1)S(1)}, bf16[2,64,1024]{2,1,0:T(8,128)(2,1)S(1)}, u32[]{:S(2)}, u32[]{:S(2)}) collective-permute-start(bf16[2,64,1024]{2,1,0:T(8,128)(2,1)S(1)} %dynamic-slice_bitcast_fusion.2), channel_id=1, source_target_pairs={{0,2},{1,3},{2,0},{3,1},{4,6},{5,7},{6,4},{7,5},{8,10},{9,11},{10,... | collective-permute-start | bytes 786440 | tf_op jit(solution)/shard_map/ppermute | solution.py:283
  528.1 15.9 %copy-start.42 = (f32[1,1024]{1,0:T(1,128)S(1)}, f32[1,1024]{1,0:T(1,128)}, u32[]{:S(2)}) copy-start(f32[1,1024]{1,0:T(1,128)} %copy-done.41) | copy-start | bytes 12292
  528.1 15.9 %copy-start.11 = (f32[1024,1024]{1,0:T(8,128)S(1)}, f32[1024,1024]{1,0:T(8,128)}, u32[]{:S(2)}) copy-start(f32[1024,1024]{1,0:T(8,128)} %fusion.6) | copy-start | bytes 12582916
  529.5 18.6 %collective-permute-start.18 = (bf16[2,2,64,512]{3,2,0,1:T(8,128)(2,1)S(1)}, bf16[2,2,64,512]{3,2,0,1:T(8,128)(2,1)S(1)}, u32[]{:S(2)}, u32[]{:S(2)}) collective-permute-start(bf16[2,2,64,512]{3,2,0,1:T(8,128)(2,1)S(1)} %dynamic-slice_bitcast_fusion.3), channel_id=1, source_target_pairs={{0,8},{1,9},{2,10},{3,11},{4,12},{5,13},{6,14},{7,15},{8,0},{9,1},... | collective-permute-start | bytes 786440 | tf_op jit(solution)/shard_map/ppermute | solution.py:283
  543.9 6.4 %collective-permute-start.17 = (bf16[2,2,64,512]{3,2,0,1:T(8,128)(2,1)S(1)}, bf16[2,2,64,512]{3,2,0,1:T(8,128)(2,1)S(1)}, u32[]{:S(2)}, u32[]{:S(2)}) collective-permute-start(bf16[2,2,64,512]{3,2,0,1:T(8,128)(2,1)S(1)} %dynamic-slice_bitcast_fusion.4), channel_id=1, source_target_pairs={{0,4},{1,5},{2,6},{3,7},{4,0},{5,1},{6,2},{7,3},{8,12},{9,13},{10,... | collective-permute-start | bytes 786440 | tf_op jit(solution)/shard_map/ppermute | solution.py:283
  552.1 15.4 %collective-permute-start.24 = (f32[2,2,1,512]{3,2,1,0:T(1,128)}, f32[2,2,1,512]{3,2,1,0:T(1,128)}, u32[]{:S(2)}, u32[]{:S(2)}) collective-permute-start(f32[2,2,1,512]{3,2,1,0:T(1,128)} %fusion.76), channel_id=1, source_target_pairs={{0,4},{1,5},{2,6},{3,7},{4,0},{5,1},{6,2},{7,3},{8,12},{9,13},{10,... | collective-permute-start | bytes 24584 | tf_op jit(solution)/shard_map/ppermute | solution.py:283
  553.1 14.4 %collective-permute-start.23 = (bf16[64,1024]{1,0:T(8,128)(2,1)}, bf16[64,1024]{1,0:T(8,128)(2,1)}, u32[]{:S(2)}, u32[]{:S(2)}) collective-permute-start(bf16[64,1024]{1,0:T(8,128)(2,1)} %dynamic-slice_bitcast_fusion.5), channel_id=1, source_target_pairs={{0,4},{1,5},{2,6},{3,7},{4,0},{5,1},{6,2},{7,3},{8,12},{9,13},{10,... | collective-permute-start | bytes 393224 | tf_op jit(solution)/shard_map/ppermute | solution.py:283
  555.6 11.9 %collective-permute-start.22 = (bf16[2,64,512]{2,1,0:T(8,128)(2,1)}, bf16[2,64,512]{2,1,0:T(8,128)(2,1)S(1)}, u32[]{:S(2)}, u32[]{:S(2)}) collective-permute-start(bf16[2,64,512]{2,1,0:T(8,128)(2,1)} %dynamic-slice_bitcast_fusion.6), channel_id=1, source_target_pairs={{0,2},{1,3},{2,0},{3,1},{4,6},{5,7},{6,4},{7,5},{8,10},{9,11},{10,... | collective-permute-start | bytes 393224 | tf_op jit(solution)/shard_map/ppermute | solution.py:283
  558.4 9.1 %collective-permute-start.21 = (bf16[2,64,512]{2,1,0:T(8,128)(2,1)}, bf16[2,64,512]{2,1,0:T(8,128)(2,1)}, u32[]{:S(2)}, u32[]{:S(2)}) collective-permute-start(bf16[2,64,512]{2,1,0:T(8,128)(2,1)} %dynamic-slice_bitcast_fusion.7), channel_id=1, source_target_pairs={{0,8},{1,9},{2,10},{3,11},{4,12},{5,13},{6,14},{7,15},{8,0},{9,1},... | collective-permute-start | bytes 393224 | tf_op jit(solution)/shard_map/ppermute | solution.py:283
  569.2 8.1 %collective-permute-start.27 = (f32[2,1,512]{2,1,0:T(1,128)S(1)}, f32[2,1,512]{2,1,0:T(1,128)S(1)}, u32[]{:S(2)}, u32[]{:S(2)}) collective-permute-start(f32[2,1,512]{2,1,0:T(1,128)S(1)} %fusion.81), channel_id=1, source_target_pairs={{0,8},{1,9},{2,10},{3,11},{4,12},{5,13},{6,14},{7,15},{8,0},{9,1},... | collective-permute-start | bytes 12296 | tf_op jit(solution)/shard_map/ppermute | solution.py:283
  571.3 6.1 %collective-permute-start.26 = (bf16[64,512]{1,0:T(8,128)(2,1)S(1)}, bf16[64,512]{1,0:T(8,128)(2,1)S(1)}, u32[]{:S(2)}, u32[]{:S(2)}) collective-permute-start(bf16[64,512]{1,0:T(8,128)(2,1)S(1)} %dynamic-slice_bitcast_fusion.8), channel_id=1, source_target_pairs={{0,16},{1,17},{2,18},{3,19},{4,20},{5,21},{6,22},{7,23},{8,24},{9,... | collective-permute-start | bytes 196616 | tf_op jit(solution)/shard_map/ppermute | solution.py:283
  572.4 5.7 collective-permute-start.25
  575.3 1.3 collective-permute-start.29
  578.1 5.9 collective-permute-start.31
  578.3 4.5 collective-permute-start.28
  580.8 4.0 collective-permute-start.30
  (44 other events, 157.9 us)
Sparse Core Ops, SparseCore 0:
  15.8 118.7 all-gather.2
  138.1 112.9 all-gather.4
  276.8 256.4 reduce-scatter.1

commit v4 on v3

--- a/solution.py
+++ b/solution.py
@@ -162,11 +162,17 @@
     @pl.when(block == 0)
     def _():
         rows = q_ref.shape[0] // 8
-        at = 0
-        for ref in (g0, g1, g2, g3, g4):
-            for c in range(ref.shape[0] // (rows + count)):
+        far = g0.shape[0] - count
+        left_out = jnp.zeros((rows - far, q_ref.shape[1]), bf16)
+        do_ref[: rows - far, :] = left_out
+        do_ref[rows - far : rows, :] = g0[:far, :]
+        at = rows
+        for ref in (g1, g2, g3):
+            for c in range(2):
                 do_ref[at : at + rows, :] = ref[c * (rows + count) : c * (rows + count) + rows, :]
                 at += rows
+        do_ref[at : at + far, :] = g4[:far, :]
+        do_ref[at + far :, :] = left_out
 
     apart = apart_of()
     kl = kl_ref[...]
@@ -198,8 +204,8 @@
 def dense_kernel(n_ref, gd_ref, wh_ref, wp_ref, bh_ref, act_ref, gh_ref, dw_ref, dbh_ref):
     n = n_ref[...]
     gd = gd_ref[...]
-    for u in range(0, wh_ref.shape[2], BLK):
-        units = slice(u, u + BLK)
+    for u in range(0, wh_ref.shape[2], STEP):
+        units = slice(u, u + STEP)
         hidden = product(n, wh_ref[0, :, units]) + bh_ref[0, :, units]
         grad = against(gd, wp_ref[0, units, :])
         below = 0.5 + 0.5 * lax.erf(hidden * 0.7071067811865476)
@@ -213,14 +219,36 @@
         dw_ref[0, 0, :, units] = inner_rows(n, gh_low).astype(bf16)
 
 
-def dense_sum_kernel(act_ref, gh_ref, wh_ref, wp_ref, out_ref, gn_ref):
+def forward_sum_kernel(act_ref, wp_ref, out_ref):
     @pl.when(pl.program_id(0) == 0)
     def _():
         out_ref[...] = jnp.zeros(out_ref.shape, f32)
+
+    out_ref[...] += product(act_ref[...], wp_ref[0])
+
+
+def backward_sum_kernel(gh_ref, wh_ref, gn_ref):
+    @pl.when(pl.program_id(0) == 0)
+    def _():
         gn_ref[...] = jnp.zeros(gn_ref.shape, f32)
 
-    out_ref[...] += product(act_ref[...], wp_ref[0])
     gn_ref[...] += against(gh_ref[...], wh_ref[0])
+
+
+def sum_call(kernel, units, weights, at):
+    rows, width = units.shape[0], weights.shape[2]
+    return pl.pallas_call(
+        kernel,
+        grid=(units.shape[1] // width,),
+        in_specs=[
+            pl.BlockSpec((rows, width), lambda j: (0, j)),
+            pl.BlockSpec((1, width, width), lambda j: (at + j, 0, 0)),
+        ],
+        out_specs=pl.BlockSpec((rows, width), lambda j: (0, 0)),
+        out_shape=jax.ShapeDtypeStruct((rows, width), f32),
+        compiler_params=pltpu.CompilerParams(vmem_limit_bytes=40 * 1024 * 1024),
+        cost_estimate=pl.CostEstimate(flops=8_000_000_000, bytes_accessed=12_000_000, transcendentals=0),
+    )(units, weights)
 
 
 def dense_call(n, gd, weights, bias):
@@ -246,16 +274,7 @@
         compiler_params=params,
         cost_estimate=pl.CostEstimate(flops=35_000_000_000, bytes_accessed=40_000_000, transcendentals=0),
     )(n, gd, weights, weights, bias)
-    out, gn = pl.pallas_call(
-        dense_sum_kernel,
-        grid=(parts,),
-        in_specs=[columns, columns, chunk, second],
-        out_specs=[whole, whole],
-        out_shape=[jax.ShapeDtypeStruct((rows, width), f32)] * 2,
-        compiler_params=params,
-        cost_estimate=pl.CostEstimate(flops=15_000_000_000, bytes_accessed=25_000_000, transcendentals=0),
-    )(act, gh, weights, weights)
-    return out, gn, dw.reshape(2 * parts, width, width), dbh
+    return act, sum_call(backward_sum_kernel, gh, weights, 0), dw.reshape(2 * parts, width, width), dbh
 
 
 def attention_call(kernel, grid, in_specs, out_specs, out_shape, scratch, flops):
@@ -396,10 +415,17 @@
     own = jnp.concatenate([tokens, tag_rows])
     below = shifted(own, 2)
     above = shifted(own, -2)
+    far_rows = -(-(IMG - 1 - 2 * rows) // 16) * 16
+    left_out = jnp.zeros((rows - far_rows, width), bf16)
     far = lax.ppermute(
-        own,
+        jnp.concatenate([jnp.where(core == 0, tokens[:far_rows], tokens[rows - far_rows :]), tag_rows]),
         "dev",
         [(i, i - 4) for i in range(4, count, 2)] + [(i, i + 4) for i in range(1, count - 4, 2)],
+    )
+    far = jnp.where(
+        core == 0,
+        jnp.concatenate([far[:far_rows], left_out, far[far_rows:]]),
+        jnp.concatenate([left_out, far]),
     )
     mine = jnp.stack([below, own, above, far])
     theirs = swap(mine, 0)
@@ -497,7 +523,7 @@
     normed_two_low, lse_rows, chip_unit, chip_inverse = lax.optimization_barrier(
         (normed_two.astype(bf16), lse_rows, chip_unit, chip_inverse)
     )
-    dense_sum, grad_normed_two, dense_weight_grads, hidden_bias_grad = dense_call(
+    active, grad_normed_two, dense_weight_grads, hidden_bias_grad = dense_call(
         normed_two_low, grad_dense, dense_full, bias_hidden
     )
     project_bias_grad = column_sums(grad_dense)
@@ -532,8 +558,8 @@
     both = jnp.concatenate(packed)
     from_below = shifted(both, 2)
     from_above = shifted(both, -2)
-    far_below = shifted(packed[1], 4)
-    far_above = shifted(packed[0], -4)
+    far_below = shifted(packed[1][rows - far_rows :], 4)
+    far_above = shifted(jnp.concatenate([packed[0][:far_rows], packed[0][rows:]]), -4)
     (grad_queries,) = attention_call(
         partial(query_kernel, first),
         (1, own_blocks),
@@ -562,14 +588,14 @@
     first_part.send()
     unit = rows + stat_count
     own_unit = both
-    stat_parts = [far_below[rows:]]
+    stat_parts = [far_below[far_rows:]]
     for piece in (from_below, own_unit, from_above):
         stat_parts += [piece[rows:unit], piece[unit + rows :]]
-    stat_parts.append(far_above[rows:])
+    stat_parts.append(far_above[far_rows:])
     stat_window = jnp.concatenate(stat_parts, axis=1).astype(f32)
     third = 4 * pairs
     stat_window = stat_window[:third] + stat_window[third : 2 * third] + stat_window[2 * third :]
-    one_unit = pl.BlockSpec((unit, half), lambda h, b, lo, hi: (0, 0))
+    one_unit = pl.BlockSpec((far_rows + stat_count, half), lambda h, b, lo, hi: (0, 0))
     two_units = pl.BlockSpec((2 * unit, half), lambda h, b, lo, hi: (0, 0))
     grad_keys, grad_values = attention_call(
         partial(key_kernel, first, stat_count),
@@ -593,8 +619,8 @@
         70_000_000_000,
     )(lo, hi, projected, projected, projected, query_label[None], key_label[:, None], far_below, from_below, own_unit, from_above, far_above, stat_window)
 
-    grad_keys, grad_values, grad_branch, grad_middle, dense_sum = first_part.receive(
-        grad_keys, grad_values, grad_branch, grad_middle, dense_sum
+    grad_keys, grad_values, grad_branch, grad_middle, active = first_part.receive(
+        grad_keys, grad_values, grad_branch, grad_middle, active
     )
     key_part = Travelling(weight_sum(grad_keys), bits[:-1], [axes[0], axes[1], axes[2]] + far_bits)
     value_part = Travelling(weight_sum(grad_values), bits[:-1], [axes[1], axes[2], axes[0]] + far_bits)
@@ -608,7 +634,7 @@
     first_bias_grad = jnp.sum(grad_normed_pair, axis=0)
     output_bias_grad = column_sums(grad_branch)
     attention_scale_grad = jnp.sum(grad_middle * branch, axis=0)
-    dense_out = dense_sum + bias_project
+    dense_out = sum_call(forward_sum_kernel, active, dense_full, parts) + bias_project
     layer_output = (middle + scale_second * dense_out).astype(bf16)
     dense_scale_grad = jnp.sum(upstream * dense_out, axis=0)
 

time: 595 us -> 590 us (level)
  starting transfers between devices: 81 us -> 68.5 us
  Pallas kernels: 144 us -> 155 us
  waiting for transfers between devices: 187 us -> 177 us
    ppermute x1, waiting for transfers between devices: 0.01 us -> 13.5 us  [on_device(): lax.ppermute(jnp.concatenate([jnp.where(core == 0, tokens[:far_rows], tok...]
    ppermute x25, starting transfers between devices: 61 us -> 48.6 us  [swap(): return lax.ppermute(block, 'dev', [(i, i ^ 1 << bit) for i in range(count)])]
    all_gather x1, waiting for transfers between devices: 19.7 us -> 7.77 us  [on_device(): attention_full = lax.all_gather(attention_pack, 'dev', axis=0, tiled=True)]
    ppermute x6, waiting for transfers between devices: 82.7 us -> 73.4 us  [shifted(): lax.ppermute(block, 'dev', [(i, i + distance) for i in range(count) if 0...]
    pallas_call x1 -> x2, Pallas kernels: 15.1 us -> 15.8 us  [sum_call(): pl.pallas_call(kernel, grid=(units.shape[1] // width,), in_specs=[pl.Bloc...]
    unnamed x144 -> x152, local copies, waits for them, and re-layouts: 24.3 us -> 24.1 us
  transfers between devices with their start and end apart: 35 -> 35, of which waited for: 17 -> 17; matrix products, arithmetic and copies ran while one was open for 24% -> 24% of each run, Pallas kernels for 20% -> 22%
where the time goes in v4:
time: 590 us; the launch traced here: 584 us
  waiting for transfers between devices  177 us (30%)
  Pallas kernels  155 us (26%)
  starting transfers between devices  68.5 us (12%)
  local copies, waits for them, and re-layouts  64.2 us (11%)
  other arithmetic  56.7 us (10%)
  matrix products  46.2 us (8%)
  between operations  15.7 us (3%)
    ppermute x6, waiting for transfers between devices, shifted(): lax.ppermute(block, 'dev', [(i, i + distance) for i in range(count) if 0...  73.4 us
    ppermute x25, starting transfers between devices, swap(): return lax.ppermute(block, 'dev', [(i, i ^ 1 << bit) for i in range(count)])  48.6 us
    all_gather x1, waiting for transfers between devices, on_device(): dense_full = lax.all_gather(dense_pack, 'dev', axis=1, tiled=True)  45.2 us
    pallas_call x1, Pallas kernels, on_device(): attention_call(partial(key_kernel, first, stat_count), (1, own_blocks), [...  43.5 us
    pallas_call x1, Pallas kernels, on_device(): attention_call(partial(query_kernel, first), (1, own_blocks), [own_rows(0...  38.1 us
    ppermute x25, waiting for transfers between devices, swap(): return lax.ppermute(block, 'dev', [(i, i ^ 1 << bit) for i in range(count)])  37.6 us
    pallas_call x1, Pallas kernels, on_device(): attention_call(partial(attend_kernel, first), (half // lanes, own_blocks)...  32.9 us
    pallas_call x1, Pallas kernels, dense_call(): pl.pallas_call(dense_kernel, grid=(parts,), in_specs=[whole, whole, chunk...  24.8 us
  transfers between devices with their start and end apart: 35, of which 17 were waited for; matrix products, arithmetic and copies ran while one was open for 24% of the time, Pallas kernels for 22%

profile of v4, /device:TPU:0, one launch (start us, length us, event | category | flops | bytes accessed | tf_op | source)
XLA Modules:
  0.0 584.0 jit_solution(11209453074171030826)
XLA Ops:
  21.2 4.9 collective-permute-start
  29.1 13.5 %collective-permute-done.2 = bf16[368,1024]{1,0:T(8,128)(2,1)S(1)} collective-permute-done((bf16[368,1024]{1,0:T(8,128)(2,1)S(1)}, bf16[368,1024]{1,0:T(8,128)(2,1)S(1)}, u32[]{:S(2)}, u32[]{:S(2)}) %collective-permute-start.2) | collective-permute-done | bytes 753696 | tf_op jit(solution)/shard_map/ppermute | solution.py:420
  42.9 39.3 %collective-permute-done = bf16[528,1024]{1,0:T(8,128)(2,1)S(1)} collective-permute-done((bf16[528,1024]{1,0:T(8,128)(2,1)}, bf16[528,1024]{1,0:T(8,128)(2,1)S(1)}, u32[]{:S(2)}, u32[]{:S(2)}) %collective-permute-start) | collective-permute-done | bytes 1081376 | tf_op jit(solution)/shard_map/ppermute | solution.py:307
  84.2 3.4 pad_maximum_fusion
  87.6 7.7 %collective-permute-done.3 = bf16[4,528,1024]{2,1,0:T(8,128)(2,1)} collective-permute-done((bf16[4,528,1024]{2,1,0:T(8,128)(2,1)}, bf16[4,528,1024]{2,1,0:T(8,128)(2,1)}, u32[]{:S(2)}, u32[]{:S(2)}) %collective-permute-start.3) | collective-permute-done | bytes 4325408 | tf_op jit(solution)/shard_map/ppermute | solution.py:302
  95.3 2.9 broadcast_select_fusion
  114.8 2.1 copy-done.7
  117.0 2.8 fusion.2
  119.8 2.5 fusion.6
  122.3 2.4 broadcast_select_fusion.2
  124.7 7.8 %all-gather.3.cloned.1.call-done = bf16[1024,4224]{1,0:T(8,128)(2,1)} async-done(((bf16[32,4224]{1,0:T(8,128)(2,1)}), bf16[1024,4224]{1,0:T(8,128)(2,1)}) %all-gather.3.cloned.1.call-update) | async-done | bytes 8650768 | tf_op jit(solution)/shard_map/all_gather | solution.py:407
  134.3 5.8 fusion.5
  140.1 19.8 %multiply_convert_fusion.q_ref.k_ref.v_ref = bf16[4096,1536]{1,0:T(8,128)(2,1)} fusion(bf16[4096,1024]{1,0:T(8,128)(2,1)S(1)} %fusion.5, f32[1536]{0:T(1024)S(1)} %copy-done.58, f32[1536]{0:T(1024)S(1)} %pad_maximum_fusion.10, bf16[1024,4224]{1,0:T(8,128)(2,1)} %all-gather.3.cloned.1.call-done, s32[]{:T(128)S(6)} %select_n.264), kind=kOutput, calls=%fused_computation | convolution fusion | flops 12903776256 | bytes 24129540 | tf_op jit(solution)/shard_map/dot_general | solution.py:27
  160.0 32.9 %shard_map.348 = (f32[1024,512]{1,0:T(8,128)S(1)}, f32[1024,512]{1,0:T(8,128)S(1)}) custom-call(s32[4]{0:T(128)S(1)} %get-tuple-element.196.lo, s32[4]{0:T(128)S(1)} %get-tuple-element.197.hi, bf16[4096,1536]{1,0:T(8,128)(2,1)} %multiply_convert_fusion.q_ref.k_ref.v_ref, bf16[4096,1536]{1,0:T(8,128)(2,1)} %multiply_convert_fusion.q_ref.k_ref.v_ref, ...), custom_call_target="tpu_custom_call" | custom-call | flops 49999998976 | bytes 8000000 | tf_op jit(solution)/shard_map/pallas_call | solution.py:491
  197.4 4.6 fusion.102
  203.7 45.2 %all-gather.5.cloned.1.call-done.wh_ref.wp_ref = bf16[8,1024,1024]{2,1,0:T(8,128)(2,1)} async-done(((bf16[8,32,1024]{2,1,0:T(8,128)(2,1)}), bf16[8,1024,1024]{2,1,0:T(8,128)(2,1)}) %all-gather.5.cloned.1.call-update) | async-done | bytes 16777232 | tf_op jit(solution)/shard_map/all_gather | solution.py:408
  248.9 24.8 %shard_map.349 = (bf16[512,4096]{1,0:T(8,128)(2,1)}, bf16[512,4096]{1,0:T(8,128)(2,1)}, bf16[2,4,1024,1024]{3,2,1,0:T(8,128)(2,1)}, f32[4,1,1024]{2,1,0:T(1,128)}) custom-call(bf16[512,1024]{1,0:T(8,128)(2,1)} %add_convert_fusion.1.n_ref, bf16[512,1024]{1,0:T(8,128)(2,1)} %get-tuple-element.122.gd_ref, ...), custom_call_target="tpu_custom_call" | custom-call | flops 35000000512 | bytes 40000000 | tf_op jit(solution)/shard_map/pallas_call | solution.py:263
  274.5 2.2 copy-done.6
  276.7 8.3 %shard_map.350 = f32[512,1024]{1,0:T(8,128)S(1)} custom-call(bf16[512,4096]{1,0:T(8,128)(2,1)S(1)} %copy-done.6, bf16[8,1024,1024]{2,1,0:T(8,128)(2,1)} %all-gather.5.cloned.1.call-done.wh_ref.wp_ref), custom_call_target="tpu_custom_call" | custom-call | flops 8000000000 | bytes 12000000 | tf_op jit(solution)/shard_map/pallas_call | solution.py:240
  288.2 3.3 fusion.43
  303.2 3.4 collective-permute-start.6
  309.3 6.1 %collective-permute-start.8 = (bf16[400,512]{1,0:T(8,128)(2,1)S(1)}, bf16[400,512]{1,0:T(8,128)(2,1)S(1)}, u32[]{:S(2)}, u32[]{:S(2)}) collective-permute-start(bf16[400,512]{1,0:T(8,128)(2,1)S(1)} %pad_maximum_fusion.6), channel_id=1, source_target_pairs={{0,4},{1,5},{2,6},{3,7},{4,8},{5,9},{6,10},{7,11},{8,12},{9,13},{1... | collective-permute-start | bytes 1228808 | tf_op jit(solution)/shard_map/ppermute | solution.py:307
  315.5 38.1 %shard_map.351 = bf16[1024,512]{1,0:T(8,128)(2,1)S(1)} custom-call(s32[4]{0:T(128)S(1)} %get-tuple-element.196.lo, s32[4]{0:T(128)S(1)} %get-tuple-element.197.hi, bf16[4096,1536]{1,0:T(8,128)(2,1)} %multiply_convert_fusion.q_ref.k_ref.v_ref, bf16[4096,1536]{1,0:T(8,128)(2,1)} %multiply_convert_fusion.q_ref.k_ref.v_ref, ...), custom_call_target="tpu_custom_call" | custom-call | flops 60000002048 | bytes 8000000 | tf_op jit(solution)/shard_map/pallas_call | solution.py:563
  353.6 6.6 %collective-permute-done.8.g0 = bf16[400,512]{1,0:T(8,128)(2,1)S(1)} collective-permute-done((bf16[400,512]{1,0:T(8,128)(2,1)S(1)}, bf16[400,512]{1,0:T(8,128)(2,1)S(1)}, u32[]{:S(2)}, u32[]{:S(2)}) %collective-permute-start.8) | collective-permute-done | bytes 409632 | tf_op jit(solution)/shard_map/ppermute | solution.py:307
  360.2 21.5 %collective-permute-done.6.g1 = bf16[1120,512]{1,0:T(8,128)(2,1)S(1)} collective-permute-done((bf16[1120,512]{1,0:T(8,128)(2,1)S(1)}, bf16[1120,512]{1,0:T(8,128)(2,1)S(1)}, u32[]{:S(2)}, u32[]{:S(2)}) %collective-permute-start.6) | collective-permute-done | bytes 1146912 | tf_op jit(solution)/shard_map/ppermute | solution.py:307
  381.7 4.1 collective-permute-done.7.g3
  387.9 2.9 fusion.34
  392.8 43.5 %shard_map.352 = (bf16[1024,512]{1,0:T(8,128)(2,1)S(1)}, bf16[1024,512]{1,0:T(8,128)(2,1)S(1)}) custom-call(s32[4]{0:T(128)S(1)} %get-tuple-element.196.lo, s32[4]{0:T(128)S(1)} %get-tuple-element.197.hi, bf16[4096,1536]{1,0:T(8,128)(2,1)} %multiply_convert_fusion.q_ref.k_ref.v_ref, bf16[4096,1536]{1,0:T(8,128)(2,1)} %multiply_convert_fusion.q_ref.k_ref.v_ref, ...), custom_call_target="tpu_custom_call" | custom-call | flops 70000001024 | bytes 8000000 | tf_op jit(solution)/shard_map/pallas_call | solution.py:600
  437.1 6.3 %fusion.98 = (f32[1024]{0:T(1024)S(1)}, f32[1024]{0:T(1024)S(1)}, f32[1024,1024]{1,0:T(8,128)S(1)}) fusion(f32[1024,1024]{1,0:T(8,128)} %fusion.6, bf16[1024,4224]{1,0:T(8,128)(2,1)} %all-gather.3.cloned.1.call-done, s32[]{:T(128)S(6)} %select_n.264, bf16[1024,512]{1,0:T(8,128)(2,1)S(1)} %get-tuple-element.80, ...), kind=kOutput, calls=%fused_computation.298 | convolution fusion | flops 3233806336 | bytes 14688260 | tf_op jit(solution)/shard_map/dot_general | solution.py:35
  443.4 2.7 constant_dynamic-slice_fusion.15
  447.2 7.5 %shard_map.353 = f32[512,1024]{1,0:T(8,128)S(1)} custom-call(bf16[512,4096]{1,0:T(8,128)(2,1)S(1)} %copy-done.5, bf16[8,1024,1024]{2,1,0:T(8,128)(2,1)} %all-gather.5.cloned.1.call-done.wh_ref.wp_ref), custom_call_target="tpu_custom_call" | custom-call | flops 8000000000 | bytes 12000000 | tf_op jit(solution)/shard_map/pallas_call | solution.py:240
  458.1 2.0 fusion.19
  461.0 14.4 %collective-permute-start.14 = (bf16[2,2,64,1024]{3,2,0,1:T(8,128)(2,1)}, bf16[2,2,64,1024]{3,2,0,1:T(8,128)(2,1)}, u32[]{:S(2)}, u32[]{:S(2)}) collective-permute-start(bf16[2,2,64,1024]{3,2,0,1:T(8,128)(2,1)} %dynamic-slice_bitcast_fusion.1), channel_id=1, source_target_pairs={{0,16},{1,17},{2,18},{3,19},{4,20},{5,21},{6,22},{7,23},{8,24},{9,... | collective-permute-start | bytes 1572872 | tf_op jit(solution)/shard_map/ppermute | solution.py:302
  475.4 2.9 fusion.40
  480.0 5.0 collective-permute-start.13
  485.0 2.9 fusion.37
  494.2 7.7 %collective-permute-done.14 = bf16[2,2,64,1024]{3,2,0,1:T(8,128)(2,1)} collective-permute-done((bf16[2,2,64,1024]{3,2,0,1:T(8,128)(2,1)}, bf16[2,2,64,1024]{3,2,0,1:T(8,128)(2,1)}, u32[]{:S(2)}, u32[]{:S(2)}) %collective-permute-start.14) | collective-permute-done | bytes 524320 | tf_op jit(solution)/shard_map/ppermute | solution.py:302
  501.9 5.9 %collective-permute-done.13 = bf16[2,2,2,64,512]{4,3,0,2,1:T(8,128)(2,1)} collective-permute-done((bf16[2,2,2,64,512]{4,3,0,2,1:T(8,128)(2,1)}, bf16[2,2,2,64,512]{4,3,0,2,1:T(8,128)(2,1)}, u32[]{:S(2)}, u32[]{:S(2)}) %collective-permute-start.13) | collective-permute-done | bytes 524320 | tf_op jit(solution)/shard_map/ppermute | solution.py:302
  507.8 8.7 %collective-permute-done.12 = bf16[2,2,2,64,512]{4,3,0,1,2:T(8,128)(2,1)} collective-permute-done((bf16[2,2,2,64,512]{4,3,0,1,2:T(8,128)(2,1)}, bf16[2,2,2,64,512]{4,3,0,1,2:T(8,128)(2,1)}, u32[]{:S(2)}, u32[]{:S(2)}) %collective-permute-start.12) | collective-permute-done | bytes 524320 | tf_op jit(solution)/shard_map/ppermute | solution.py:302
  516.6 2.5 collective-permute-start.20
  522.0 12.1 %collective-permute-start.18 = (bf16[2,2,64,512]{3,2,0,1:T(8,128)(2,1)S(1)}, bf16[2,2,64,512]{3,2,0,1:T(8,128)(2,1)S(1)}, u32[]{:S(2)}, u32[]{:S(2)}) collective-permute-start(bf16[2,2,64,512]{3,2,0,1:T(8,128)(2,1)S(1)} %dynamic-slice_bitcast_fusion.3), channel_id=1, source_target_pairs={{0,8},{1,9},{2,10},{3,11},{4,12},{5,13},{6,14},{7,15},{8,0},{9,1},... | collective-permute-start | bytes 786440 | tf_op jit(solution)/shard_map/ppermute | solution.py:302
  535.5 2.2 fusion.99
  539.6 2.6 collective-permute-done.17
  551.8 3.1 copy.153
  554.9 4.4 reshape.462
  563.9 3.0 collective-permute-start.25
  570.1 2.2 collective-permute-start.28
  572.5 2.2 collective-permute-done.28
  (371 shorter events, 105.6 us)
Async XLA Ops:
  7.2 125.2 %all-gather.3.cloned.1.call-start = ((), (), s32[]{:S(2)}) async-start(), calls=%async_computation.1 | async-start | bytes 8921088 | tf_op jit(solution)/shard_map/all_gather | solution.py:407
  15.7 233.2 %all-gather.5.cloned.1.call-start = ((), (), s32[]{:S(2)}) async-start(), calls=%async_computation.2 | async-start | bytes 17301504 | tf_op jit(solution)/shard_map/all_gather | solution.py:408
  19.7 522.5 %reduce-scatter.2.cloned.1.call-start = ((), (), s32[]{:S(2)}) async-start(), calls=%async_computation.3 | async-start | bytes 17301504 | tf_op jit(solution)/shard_map/reduce_scatter | solution.py:535
  21.2 61.1 %collective-permute-start = (bf16[528,1024]{1,0:T(8,128)(2,1)}, bf16[528,1024]{1,0:T(8,128)(2,1)S(1)}, u32[]{:S(2)}, u32[]{:S(2)}) collective-permute-start(bf16[528,1024]{1,0:T(8,128)(2,1)} %get-tuple-element.140), channel_id=1, source_target_pairs={{0,2},{1,3},{2,4},{3,5},{4,6},{5,7},{6,8},{7,9},{8,10},{9,11},{10,... | collective-permute-start | bytes 3244040 | tf_op jit(solution)/shard_map/ppermute | solution.py:307
  26.1 58.1 %collective-permute-start.1 = (bf16[528,1024]{1,0:T(8,128)(2,1)}, bf16[528,1024]{1,0:T(8,128)(2,1)}, u32[]{:S(2)}, u32[]{:S(2)}) collective-permute-start(bf16[528,1024]{1,0:T(8,128)(2,1)} %get-tuple-element.140), channel_id=1, source_target_pairs={{2,0},{3,1},{4,2},{5,3},{6,4},{7,5},{8,6},{9,7},{10,8},{11,9},{12,... | collective-permute-start | bytes 3244040 | tf_op jit(solution)/shard_map/ppermute | solution.py:307
  27.5 15.0 %collective-permute-start.2 = (bf16[368,1024]{1,0:T(8,128)(2,1)S(1)}, bf16[368,1024]{1,0:T(8,128)(2,1)S(1)}, u32[]{:S(2)}, u32[]{:S(2)}) collective-permute-start(bf16[368,1024]{1,0:T(8,128)(2,1)S(1)} %pad_maximum_fusion.4), channel_id=1, source_target_pairs={{4,0},{6,2},{8,4},{10,6},{12,8},{14,10},{16,12},{18,14},{20,16},{2... | collective-permute-start | bytes 2261000 | tf_op jit(solution)/shard_map/ppermute | solution.py:420
  87.6 7.7 %collective-permute-start.3 = (bf16[4,528,1024]{2,1,0:T(8,128)(2,1)}, bf16[4,528,1024]{2,1,0:T(8,128)(2,1)}, u32[]{:S(2)}, u32[]{:S(2)}) collective-permute-start(bf16[4,528,1024]{2,1,0:T(8,128)(2,1)} %pad_maximum_fusion), channel_id=1, source_target_pairs={{0,1},{1,0},{2,3},{3,2},{4,5},{5,4},{6,7},{7,6},{8,9},{9,8},{10,11... | collective-permute-start | bytes 12976136 | tf_op jit(solution)/shard_map/ppermute | solution.py:302
  134.2 59.9 %copy-start.43 = (f32[1,1024]{1,0:T(1,128)}, f32[1,1024]{1,0:T(1,128)S(1)}, u32[]{:S(2)}) copy-start(f32[1,1024]{1,0:T(1,128)S(1)} %get-tuple-element.156) | copy-start | bytes 12292
  134.2 63.1 %copy-start.50 = (f32[1,1024]{1,0:T(1,128)}, f32[1,1024]{1,0:T(1,128)S(1)}, u32[]{:S(2)}) copy-start(f32[1,1024]{1,0:T(1,128)S(1)} %get-tuple-element.159) | copy-start | bytes 12292
  140.1 19.9 %copy-start.21 = (bf16[4096,1024]{1,0:T(8,128)(2,1)}, bf16[4096,1024]{1,0:T(8,128)(2,1)S(1)}, u32[]{:S(2)}) copy-start(bf16[4096,1024]{1,0:T(8,128)(2,1)S(1)} %fusion.5) | copy-start | bytes 25165828
  192.9 108.7 %copy-start.2 = (f32[1024,512]{1,0:T(8,128)}, f32[1024,512]{1,0:T(8,128)S(1)}, u32[]{:S(2)}) copy-start(f32[1024,512]{1,0:T(8,128)S(1)} %get-tuple-element.65.o_ref) | copy-start | bytes 6291460
  193.2 4.1 collective-permute-start.4
  292.4 6.6 %collective-permute-start.5 = (bf16[512,512]{1,0:T(8,128)(2,1)S(1)}, bf16[512,512]{1,0:T(8,128)(2,1)S(1)}, u32[]{:S(2)}, u32[]{:S(2)}) collective-permute-start(bf16[512,512]{1,0:T(8,128)(2,1)S(1)} %get-tuple-element.150), channel_id=1, source_target_pairs={{0,1},{1,0},{2,3},{3,2},{4,5},{5,4},{6,7},{7,6},{8,9},{9,8},{10,11... | collective-permute-start | bytes 1572872 | tf_op jit(solution)/shard_map/ppermute | solution.py:302
  296.5 63.8 %collective-permute-start.10 = (bf16[2,2,2,2,32,1024]{5,4,2,3,0,1:T(8,128)(2,1)}, bf16[2,2,2,2,32,1024]{5,4,2,3,0,1:T(8,128)(2,1)}, u32[]{:S(2)}, u32[]{:S(2)}) collective-permute-start(bf16[2,2,2,2,32,1024]{5,4,2,3,0,1:T(8,128)(2,1)} %bitcast.216), channel_id=1, source_target_pairs={{0,1},{1,0},{2,3},{3,2},{4,5},{5,4},{6,7},{7,6},{8,9},{9,8},{10,11... | collective-permute-start | bytes 3145736 | tf_op jit(solution)/shard_map/ppermute | solution.py:302
  303.2 78.5 %collective-permute-start.6 = (bf16[1120,512]{1,0:T(8,128)(2,1)S(1)}, bf16[1120,512]{1,0:T(8,128)(2,1)S(1)}, u32[]{:S(2)}, u32[]{:S(2)}) collective-permute-start(bf16[1120,512]{1,0:T(8,128)(2,1)S(1)} %pad_maximum_fusion.2.g2), channel_id=1, source_target_pairs={{0,2},{1,3},{2,4},{3,5},{4,6},{5,7},{6,8},{7,9},{8,10},{9,11},{10,... | collective-permute-start | bytes 3440648 | tf_op jit(solution)/shard_map/ppermute | solution.py:307
  306.7 79.1 %collective-permute-start.7 = (bf16[1120,512]{1,0:T(8,128)(2,1)S(1)}, bf16[1120,512]{1,0:T(8,128)(2,1)S(1)}, u32[]{:S(2)}, u32[]{:S(2)}) collective-permute-start(bf16[1120,512]{1,0:T(8,128)(2,1)S(1)} %pad_maximum_fusion.2.g2), channel_id=1, source_target_pairs={{2,0},{3,1},{4,2},{5,3},{6,4},{7,5},{8,6},{9,7},{10,8},{11,9},{12,... | collective-permute-start | bytes 3440648 | tf_op jit(solution)/shard_map/ppermute | solution.py:307
  308.0 45.6 %collective-permute-start.9 = (bf16[400,512]{1,0:T(8,128)(2,1)S(1)}, bf16[400,512]{1,0:T(8,128)(2,1)S(1)}, u32[]{:S(2)}, u32[]{:S(2)}) collective-permute-start(bf16[400,512]{1,0:T(8,128)(2,1)S(1)} %pad_maximum_fusion.7), channel_id=1, source_target_pairs={{4,0},{5,1},{6,2},{7,3},{8,4},{9,5},{10,6},{11,7},{12,8},{13,9},{1... | collective-permute-start | bytes 1228808 | tf_op jit(solution)/shard_map/ppermute | solution.py:307
  309.3 50.9 %collective-permute-start.8 = (bf16[400,512]{1,0:T(8,128)(2,1)S(1)}, bf16[400,512]{1,0:T(8,128)(2,1)S(1)}, u32[]{:S(2)}, u32[]{:S(2)}) collective-permute-start(bf16[400,512]{1,0:T(8,128)(2,1)S(1)} %pad_maximum_fusion.6), channel_id=1, source_target_pairs={{0,4},{1,5},{2,6},{3,7},{4,8},{5,9},{6,10},{7,11},{8,12},{9,13},{1... | collective-permute-start | bytes 1228808 | tf_op jit(solution)/shard_map/ppermute | solution.py:307
  353.6 32.3 %copy-start.24 = (bf16[2,2,2,2,1,32,1024]{6,5,4,3,2,1,0:T(8,128)(2,1)S(1)}, bf16[2,2,2,2,1,32,1024]{6,5,4,3,2,1,0:T(8,128)(2,1)}, u32[]{:S(2)}) copy-start(bf16[2,2,2,2,1,32,1024]{6,5,4,3,2,1,0:T(8,128)(2,1)} %get-tuple-element.137) | copy-start | bytes 3145732
  392.3 44.7 %collective-permute-start.11 = (bf16[2,2,2,64,1024]{4,3,1,2,0:T(8,128)(2,1)}, bf16[2,2,2,64,1024]{4,3,1,2,0:T(8,128)(2,1)}, u32[]{:S(2)}, u32[]{:S(2)}) collective-permute-start(bf16[2,2,2,64,1024]{4,3,1,2,0:T(8,128)(2,1)} %dynamic-slice_bitcast_fusion), channel_id=1, source_target_pairs={{0,8},{1,9},{2,10},{3,11},{4,12},{5,13},{6,14},{7,15},{8,0},{9,1},... | collective-permute-start | bytes 3145736 | tf_op jit(solution)/shard_map/ppermute | solution.py:302
  446.2 70.3 %collective-permute-start.16 = (f32[512,1024]{1,0:T(8,128)}, f32[512,1024]{1,0:T(8,128)}, u32[]{:S(2)}, u32[]{:S(2)}) collective-permute-start(f32[512,1024]{1,0:T(8,128)} %get-tuple-element.131), channel_id=1, source_target_pairs={{0,1},{1,0},{2,3},{3,2},{4,5},{5,4},{6,7},{7,6},{8,9},{9,8},{10,11... | collective-permute-start | bytes 6291464 | tf_op jit(solution)/shard_map/ppermute | solution.py:302
  460.1 18.2 %copy-start.27 = (bf16[2,2,2,64,1024]{4,3,1,2,0:T(8,128)(2,1)}, bf16[2,2,2,64,1024]{4,3,1,2,0:T(8,128)(2,1)S(1)}, u32[]{:S(2)}) copy-start(bf16[2,2,2,64,1024]{4,3,1,2,0:T(8,128)(2,1)S(1)} %fusion.19) | copy-start | bytes 3145732
  461.0 40.9 %collective-permute-start.14 = (bf16[2,2,64,1024]{3,2,0,1:T(8,128)(2,1)}, bf16[2,2,64,1024]{3,2,0,1:T(8,128)(2,1)}, u32[]{:S(2)}, u32[]{:S(2)}) collective-permute-start(bf16[2,2,64,1024]{3,2,0,1:T(8,128)(2,1)} %dynamic-slice_bitcast_fusion.1), channel_id=1, source_target_pairs={{0,16},{1,17},{2,18},{3,19},{4,20},{5,21},{6,22},{7,23},{8,24},{9,... | collective-permute-start | bytes 1572872 | tf_op jit(solution)/shard_map/ppermute | solution.py:302
  480.0 27.8 %collective-permute-start.13 = (bf16[2,2,2,64,512]{4,3,0,2,1:T(8,128)(2,1)}, bf16[2,2,2,64,512]{4,3,0,2,1:T(8,128)(2,1)}, u32[]{:S(2)}, u32[]{:S(2)}) collective-permute-start(bf16[2,2,2,64,512]{4,3,0,2,1:T(8,128)(2,1)} %bitcast.218), channel_id=1, source_target_pairs={{0,4},{1,5},{2,6},{3,7},{4,0},{5,1},{6,2},{7,3},{8,12},{9,13},{10,... | collective-permute-start | bytes 1572872 | tf_op jit(solution)/shard_map/ppermute | solution.py:302
  488.8 30.3 %copy-start.28 = (bf16[2,2,2,64,1024]{4,3,1,2,0:T(8,128)(2,1)S(1)}, bf16[2,2,2,64,1024]{4,3,1,2,0:T(8,128)(2,1)}, u32[]{:S(2)}) copy-start(bf16[2,2,2,64,1024]{4,3,1,2,0:T(8,128)(2,1)} %copy-done.27) | copy-start | bytes 3145732
  489.7 26.8 %collective-permute-start.12 = (bf16[2,2,2,64,512]{4,3,0,1,2:T(8,128)(2,1)}, bf16[2,2,2,64,512]{4,3,0,1,2:T(8,128)(2,1)}, u32[]{:S(2)}, u32[]{:S(2)}) collective-permute-start(bf16[2,2,2,64,512]{4,3,0,1,2:T(8,128)(2,1)} %bitcast.219), channel_id=1, source_target_pairs={{0,2},{1,3},{2,0},{3,1},{4,6},{5,7},{6,4},{7,5},{8,10},{9,11},{10,... | collective-permute-start | bytes 1572872 | tf_op jit(solution)/shard_map/ppermute | solution.py:302
  491.8 28.8 %copy-start.30 = (bf16[2,2,1,2,64,512]{5,4,3,2,1,0:T(8,128)(2,1)S(1)}, bf16[2,2,1,2,64,512]{5,4,3,2,1,0:T(8,128)(2,1)}, u32[]{:S(2)}) copy-start(bf16[2,2,1,2,64,512]{5,4,3,2,1,0:T(8,128)(2,1)} %get-tuple-element.141) | copy-start | bytes 1572868
  492.7 41.5 %copy-start.31 = (bf16[2,2,2,1,64,512]{5,4,3,2,1,0:T(8,128)(2,1)S(1)}, bf16[2,2,2,1,64,512]{5,4,3,2,1,0:T(8,128)(2,1)}, u32[]{:S(2)}) copy-start(bf16[2,2,2,1,64,512]{5,4,3,2,1,0:T(8,128)(2,1)} %get-tuple-element.143) | copy-start | bytes 1572868
  492.9 1.3 collective-permute-start.15
  516.6 23.0 %collective-permute-start.20 = (f32[2,2,2,1,512]{4,3,2,1,0:T(1,128)S(1)}, f32[2,2,2,1,512]{4,3,2,1,0:T(1,128)S(1)}, u32[]{:S(2)}, u32[]{:S(2)}) collective-permute-start(f32[2,2,2,1,512]{4,3,2,1,0:T(1,128)S(1)} %dynamic-slice_bitcast_fusion.11), channel_id=1, source_target_pairs={{0,2},{1,3},{2,0},{3,1},{4,6},{5,7},{6,4},{7,5},{8,10},{9,11},{10,... | collective-permute-start | bytes 49160 | tf_op jit(solution)/shard_map/ppermute | solution.py:302
  519.1 16.4 %copy-start.18 = (f32[512,1024]{1,0:T(8,128)S(1)}, f32[512,1024]{1,0:T(8,128)}, u32[]{:S(2)}) copy-start(f32[512,1024]{1,0:T(8,128)} %get-tuple-element.92) | copy-start | bytes 6291460
  520.5 14.9 %copy-start.32 = (bf16[2,2,64,1024]{3,2,0,1:T(8,128)(2,1)}, bf16[2,2,64,1024]{3,2,0,1:T(8,128)(2,1)S(1)}, u32[]{:S(2)}) copy-start(bf16[2,2,64,1024]{3,2,0,1:T(8,128)(2,1)S(1)} %fusion.53) | copy-start | bytes 1572868
  520.6 19.0 %collective-permute-start.19 = (bf16[2,64,1024]{2,1,0:T(8,128)(2,1)S(1)}, bf16[2,64,1024]{2,1,0:T(8,128)(2,1)S(1)}, u32[]{:S(2)}, u32[]{:S(2)}) collective-permute-start(bf16[2,64,1024]{2,1,0:T(8,128)(2,1)S(1)} %dynamic-slice_bitcast_fusion.2), channel_id=1, source_target_pairs={{0,2},{1,3},{2,0},{3,1},{4,6},{5,7},{6,4},{7,5},{8,10},{9,11},{10,... | collective-permute-start | bytes 786440 | tf_op jit(solution)/shard_map/ppermute | solution.py:302
  520.7 14.8 %copy-start.46 = (f32[1,1024]{1,0:T(1,128)S(1)}, f32[1,1024]{1,0:T(1,128)}, u32[]{:S(2)}) copy-start(f32[1,1024]{1,0:T(1,128)} %copy-done.45) | copy-start | bytes 12292
  520.7 14.8 %copy-start.15 = (f32[1024,1024]{1,0:T(8,128)S(1)}, f32[1024,1024]{1,0:T(8,128)}, u32[]{:S(2)}) copy-start(f32[1024,1024]{1,0:T(8,128)} %fusion.6) | copy-start | bytes 12582916
  522.0 17.5 %collective-permute-start.18 = (bf16[2,2,64,512]{3,2,0,1:T(8,128)(2,1)S(1)}, bf16[2,2,64,512]{3,2,0,1:T(8,128)(2,1)S(1)}, u32[]{:S(2)}, u32[]{:S(2)}) collective-permute-start(bf16[2,2,64,512]{3,2,0,1:T(8,128)(2,1)S(1)} %dynamic-slice_bitcast_fusion.3), channel_id=1, source_target_pairs={{0,8},{1,9},{2,10},{3,11},{4,12},{5,13},{6,14},{7,15},{8,0},{9,1},... | collective-permute-start | bytes 786440 | tf_op jit(solution)/shard_map/ppermute | solution.py:302
  535.4 6.8 %collective-permute-start.17 = (bf16[2,2,64,512]{3,2,0,1:T(8,128)(2,1)S(1)}, bf16[2,2,64,512]{3,2,0,1:T(8,128)(2,1)S(1)}, u32[]{:S(2)}, u32[]{:S(2)}) collective-permute-start(bf16[2,2,64,512]{3,2,0,1:T(8,128)(2,1)S(1)} %dynamic-slice_bitcast_fusion.4), channel_id=1, source_target_pairs={{0,4},{1,5},{2,6},{3,7},{4,0},{5,1},{6,2},{7,3},{8,12},{9,13},{10,... | collective-permute-start | bytes 786440 | tf_op jit(solution)/shard_map/ppermute | solution.py:302
  543.9 15.4 %collective-permute-start.24 = (f32[2,2,1,512]{3,2,1,0:T(1,128)}, f32[2,2,1,512]{3,2,1,0:T(1,128)}, u32[]{:S(2)}, u32[]{:S(2)}) collective-permute-start(f32[2,2,1,512]{3,2,1,0:T(1,128)} %fusion.77), channel_id=1, source_target_pairs={{0,4},{1,5},{2,6},{3,7},{4,0},{5,1},{6,2},{7,3},{8,12},{9,13},{10,... | collective-permute-start | bytes 24584 | tf_op jit(solution)/shard_map/ppermute | solution.py:302
  545.0 14.3 %collective-permute-start.23 = (bf16[64,1024]{1,0:T(8,128)(2,1)}, bf16[64,1024]{1,0:T(8,128)(2,1)}, u32[]{:S(2)}, u32[]{:S(2)}) collective-permute-start(bf16[64,1024]{1,0:T(8,128)(2,1)} %dynamic-slice_bitcast_fusion.5), channel_id=1, source_target_pairs={{0,4},{1,5},{2,6},{3,7},{4,0},{5,1},{6,2},{7,3},{8,12},{9,13},{10,... | collective-permute-start | bytes 393224 | tf_op jit(solution)/shard_map/ppermute | solution.py:302
  547.5 11.8 %collective-permute-start.22 = (bf16[2,64,512]{2,1,0:T(8,128)(2,1)}, bf16[2,64,512]{2,1,0:T(8,128)(2,1)S(1)}, u32[]{:S(2)}, u32[]{:S(2)}) collective-permute-start(bf16[2,64,512]{2,1,0:T(8,128)(2,1)} %dynamic-slice_bitcast_fusion.6), channel_id=1, source_target_pairs={{0,2},{1,3},{2,0},{3,1},{4,6},{5,7},{6,4},{7,5},{8,10},{9,11},{10,... | collective-permute-start | bytes 393224 | tf_op jit(solution)/shard_map/ppermute | solution.py:302
  549.9 9.4 %collective-permute-start.21 = (bf16[2,64,512]{2,1,0:T(8,128)(2,1)}, bf16[2,64,512]{2,1,0:T(8,128)(2,1)}, u32[]{:S(2)}, u32[]{:S(2)}) collective-permute-start(bf16[2,64,512]{2,1,0:T(8,128)(2,1)} %dynamic-slice_bitcast_fusion.7), channel_id=1, source_target_pairs={{0,8},{1,9},{2,10},{3,11},{4,12},{5,13},{6,14},{7,15},{8,0},{9,1},... | collective-permute-start | bytes 393224 | tf_op jit(solution)/shard_map/ppermute | solution.py:302
  561.0 7.8 %collective-permute-start.27 = (f32[2,1,512]{2,1,0:T(1,128)S(1)}, f32[2,1,512]{2,1,0:T(1,128)S(1)}, u32[]{:S(2)}, u32[]{:S(2)}) collective-permute-start(f32[2,1,512]{2,1,0:T(1,128)S(1)} %fusion.82), channel_id=1, source_target_pairs={{0,8},{1,9},{2,10},{3,11},{4,12},{5,13},{6,14},{7,15},{8,0},{9,1},... | collective-permute-start | bytes 12296 | tf_op jit(solution)/shard_map/ppermute | solution.py:302
  562.8 6.0 %collective-permute-start.26 = (bf16[64,512]{1,0:T(8,128)(2,1)S(1)}, bf16[64,512]{1,0:T(8,128)(2,1)S(1)}, u32[]{:S(2)}, u32[]{:S(2)}) collective-permute-start(bf16[64,512]{1,0:T(8,128)(2,1)S(1)} %dynamic-slice_bitcast_fusion.8), channel_id=1, source_target_pairs={{0,16},{1,17},{2,18},{3,19},{4,20},{5,21},{6,22},{7,23},{8,24},{9,... | collective-permute-start | bytes 196616 | tf_op jit(solution)/shard_map/ppermute | solution.py:302
  563.9 6.0 %collective-permute-start.25 = (bf16[64,512]{1,0:T(8,128)(2,1)S(1)}, bf16[64,512]{1,0:T(8,128)(2,1)S(1)}, u32[]{:S(2)}, u32[]{:S(2)}) collective-permute-start(bf16[64,512]{1,0:T(8,128)(2,1)S(1)} %dynamic-slice_bitcast_fusion.9), channel_id=1, source_target_pairs={{0,16},{1,17},{2,18},{3,19},{4,20},{5,21},{6,22},{7,23},{8,24},{9,... | collective-permute-start | bytes 196616 | tf_op jit(solution)/shard_map/ppermute | solution.py:302
  566.9 1.3 collective-permute-start.29
  570.0 5.9 %collective-permute-start.31 = (bf16[32,512]{1,0:T(8,128)(2,1)S(1)}, bf16[32,512]{1,0:T(8,128)(2,1)S(1)}, u32[]{:S(2)}, u32[]{:S(2)}) collective-permute-start(bf16[32,512]{1,0:T(8,128)(2,1)S(1)} %get-tuple-element.172), channel_id=1, source_target_pairs={{0,1},{1,0},{2,3},{3,2},{4,5},{5,4},{6,7},{7,6},{8,9},{9,8},{10,11... | collective-permute-start | bytes 98312 | tf_op jit(solution)/shard_map/ppermute | solution.py:302
  570.1 4.5 collective-permute-start.28
  572.3 4.3 collective-permute-start.30
  (49 other events, 209.3 us)
Sparse Core Ops, SparseCore 0:
  15.8 116.5 all-gather.2
  135.9 112.9 all-gather.4
  273.8 255.9 reduce-scatter.1

commit v5 on v4

--- a/solution.py
+++ b/solution.py
@@ -275,6 +275,22 @@
         cost_estimate=pl.CostEstimate(flops=35_000_000_000, bytes_accessed=40_000_000, transcendentals=0),
     )(n, gd, weights, weights, bias)
     return act, sum_call(backward_sum_kernel, gh, weights, 0), dw.reshape(2 * parts, width, width), dbh
+
+
+def ungroup_kernel(g_ref, out_ref):
+    groups, rows, width = g_ref.shape
+    share = 128 // groups
+    lane = lax.broadcasted_iota(jnp.int32, (rows, 128), 1)
+    for t in range(0, width, 128):
+        tiles = [g_ref[j, :, t : t + 128].astype(f32) for j in range(groups)]
+        for i in range(groups):
+            tile = tiles[i]
+            for j in range(groups):
+                if j != i:
+                    moved = pltpu.roll(tiles[j], (j - i) * share % 128, 1)
+                    tile = jnp.where(lane // share == j, moved, tile)
+            at = groups * t + 128 * i
+            out_ref[:, at : at + 128] = tile
 
 
 def attention_call(kernel, grid, in_specs, out_specs, out_shape, scratch, flops):
@@ -690,8 +706,13 @@
         if turn == 0:
             input_gradient, dense_sums = received(moving, input_gradient, dense_sums)
             project_out = dense_sums[parts:].reshape(parts * shard, width).astype(f32)
-            hidden_out = dense_sums[:parts].reshape(parts, shard, count, shard)
-            hidden_out = hidden_out.transpose(1, 2, 0, 3).reshape(shard, ff).astype(f32)
+            if parts * shard == 128:
+                hidden_out = pl.pallas_call(ungroup_kernel, out_shape=jax.ShapeDtypeStruct((shard, ff), f32))(
+                    dense_sums[:parts]
+                )
+            else:
+                hidden_out = dense_sums[:parts].reshape(parts, shard, count, shard)
+                hidden_out = hidden_out.transpose(1, 2, 0, 3).reshape(shard, ff).astype(f32)
         elif turn == 1:
             project_out, hidden_out = received(moving, project_out, hidden_out)
         else:

time: 590 us -> 580 us (0.983)
  local copies, waits for them, and re-layouts: 64.2 us -> 54.2 us
  Pallas kernels: 155 us -> 146 us
  starting transfers between devices: 68.5 us -> 76.6 us
  waiting for transfers between devices: 177 us -> 185 us
    convert_element_type x3 -> x0, local copies, waits for them, and re-layouts: 8.2 us -> none  [on_device(): hidden_out = hidden_out.transpose(1, 2, 0, 3).reshape(shard, ff).astype(f32)]
    ppermute x25, starting transfers between devices: 48.6 us -> 56.6 us  [swap(): return lax.ppermute(block, 'dev', [(i, i ^ 1 << bit) for i in range(count)])]
    unnamed x152 -> x154, local copies, waits for them, and re-layouts: 24.1 us -> 24.1 us
  transfers between devices with their start and end apart: 35 -> 35, of which waited for: 17 -> 19; matrix products, arithmetic and copies ran while one was open for 24% -> 23% of each run, Pallas kernels for 22% -> 21%
where the time goes in v5:
time: 580 us; the launch traced here: 577 us
  waiting for transfers between devices  185 us (32%)
  Pallas kernels  146 us (25%)
  starting transfers between devices  76.6 us (13%)
  local copies, waits for them, and re-layouts  54.2 us (9%)
  other arithmetic  53.3 us (9%)
  matrix products  46.4 us (8%)
  between operations  15.7 us (3%)
    ppermute x6, waiting for transfers between devices, shifted(): lax.ppermute(block, 'dev', [(i, i + distance) for i in range(count) if 0...  76.3 us
    ppermute x25, starting transfers between devices, swap(): return lax.ppermute(block, 'dev', [(i, i ^ 1 << bit) for i in range(count)])  56.6 us
    all_gather x1, waiting for transfers between devices, on_device(): dense_full = lax.all_gather(dense_pack, 'dev', axis=1, tiled=True)  48.1 us
    ppermute x25, waiting for transfers between devices, swap(): return lax.ppermute(block, 'dev', [(i, i ^ 1 << bit) for i in range(count)])  39.2 us
    pallas_call x1, Pallas kernels, on_device(): attention_call(partial(key_kernel, first, stat_count), (1, own_blocks), [...  38.8 us
    pallas_call x1, Pallas kernels, on_device(): attention_call(partial(query_kernel, first), (1, own_blocks), [own_rows(0...  34.8 us
    pallas_call x1, Pallas kernels, on_device(): attention_call(partial(attend_kernel, first), (half // lanes, own_blocks)...  29.8 us
    pallas_call x1, Pallas kernels, dense_call(): pl.pallas_call(dense_kernel, grid=(parts,), in_specs=[whole, whole, chunk...  24.8 us
  transfers between devices with their start and end apart: 35, of which 19 were waited for; matrix products, arithmetic and copies ran while one was open for 23% of the time, Pallas kernels for 21%

profile of v5, /device:TPU:0, one launch (start us, length us, event | category | flops | bytes accessed | tf_op | source)
XLA Modules:
  0.0 577.0 jit_solution(5036525053637640809)
XLA Ops:
  21.2 4.9 collective-permute-start
  29.1 13.5 %collective-permute-done.2 = bf16[368,1024]{1,0:T(8,128)(2,1)S(1)} collective-permute-done((bf16[368,1024]{1,0:T(8,128)(2,1)S(1)}, bf16[368,1024]{1,0:T(8,128)(2,1)S(1)}, u32[]{:S(2)}, u32[]{:S(2)}) %collective-permute-start.2) | collective-permute-done | bytes 753696 | tf_op jit(solution)/shard_map/ppermute | solution.py:436
  42.9 39.3 %collective-permute-done = bf16[528,1024]{1,0:T(8,128)(2,1)S(1)} collective-permute-done((bf16[528,1024]{1,0:T(8,128)(2,1)}, bf16[528,1024]{1,0:T(8,128)(2,1)S(1)}, u32[]{:S(2)}, u32[]{:S(2)}) %collective-permute-start) | collective-permute-done | bytes 1081376 | tf_op jit(solution)/shard_map/ppermute | solution.py:323
  84.2 3.4 pad_maximum_fusion
  87.6 7.7 %collective-permute-done.3 = bf16[4,528,1024]{2,1,0:T(8,128)(2,1)} collective-permute-done((bf16[4,528,1024]{2,1,0:T(8,128)(2,1)}, bf16[4,528,1024]{2,1,0:T(8,128)(2,1)}, u32[]{:S(2)}, u32[]{:S(2)}) %collective-permute-start.3) | collective-permute-done | bytes 4325408 | tf_op jit(solution)/shard_map/ppermute | solution.py:318
  95.3 2.9 broadcast_select_fusion
  101.6 2.0 copy.110
  114.8 2.1 copy-done.7
  116.9 2.8 fusion.2
  119.7 2.5 fusion.6
  122.3 2.4 broadcast_select_fusion.2
  124.6 7.8 %all-gather.3.cloned.1.call-done = bf16[1024,4224]{1,0:T(8,128)(2,1)} async-done(((bf16[32,4224]{1,0:T(8,128)(2,1)}), bf16[1024,4224]{1,0:T(8,128)(2,1)}) %all-gather.3.cloned.1.call-update) | async-done | bytes 8650768 | tf_op jit(solution)/shard_map/all_gather | solution.py:423
  134.3 5.8 %fusion.5 = bf16[4096,1024]{1,0:T(8,128)(2,1)S(1)} fusion(bf16[4096,1024]{1,0:T(8,128)(2,1)} %copy-done.7, f32[1024]{0:T(1024)S(1)} %bitcast.251, f32[1024]{0:T(1024)S(1)} %bitcast.242, f32[4096]{0:T(1024)S(1)} %add_rsqrt_fusion, f32[4096]{0:T(1024)S(1)} %broadcast_multiply_fusion), kind=kLoop, calls=%fused_computation.8 | loop fusion | flops 25165824 | bytes 16818176 | tf_op jit(solution)/shard_map/convert_element_type | solution.py:480
  140.1 19.9 %multiply_convert_fusion.q_ref.k_ref.v_ref = bf16[4096,1536]{1,0:T(8,128)(2,1)} fusion(bf16[4096,1024]{1,0:T(8,128)(2,1)S(1)} %fusion.5, f32[1536]{0:T(1024)S(1)} %copy-done.59, f32[1536]{0:T(1024)S(1)} %pad_maximum_fusion.10, bf16[1024,4224]{1,0:T(8,128)(2,1)} %all-gather.3.cloned.1.call-done, s32[]{:T(128)S(6)} %select_n.264), kind=kOutput, calls=%fused_computation | convolution fusion | flops 12903776256 | bytes 24129540 | tf_op jit(solution)/shard_map/dot_general | solution.py:27
  160.0 29.8 %shard_map.348 = (f32[1024,512]{1,0:T(8,128)S(1)}, f32[1024,512]{1,0:T(8,128)S(1)}) custom-call(s32[4]{0:T(128)S(1)} %get-tuple-element.196.lo, s32[4]{0:T(128)S(1)} %get-tuple-element.197.hi, bf16[4096,1536]{1,0:T(8,128)(2,1)} %multiply_convert_fusion.q_ref.k_ref.v_ref, bf16[4096,1536]{1,0:T(8,128)(2,1)} %multiply_convert_fusion.q_ref.k_ref.v_ref, ...), custom_call_target="tpu_custom_call" | custom-call | flops 49999998976 | bytes 8000000 | tf_op jit(solution)/shard_map/pallas_call | solution.py:507
  194.3 4.7 fusion.102
  200.8 48.1 %all-gather.5.cloned.1.call-done.wh_ref.wp_ref = bf16[8,1024,1024]{2,1,0:T(8,128)(2,1)} async-done(((bf16[8,32,1024]{2,1,0:T(8,128)(2,1)}), bf16[8,1024,1024]{2,1,0:T(8,128)(2,1)}) %all-gather.5.cloned.1.call-update) | async-done | bytes 16777232 | tf_op jit(solution)/shard_map/all_gather | solution.py:424
  248.9 24.8 %shard_map.349 = (bf16[512,4096]{1,0:T(8,128)(2,1)}, bf16[512,4096]{1,0:T(8,128)(2,1)}, bf16[2,4,1024,1024]{3,2,1,0:T(8,128)(2,1)}, f32[4,1,1024]{2,1,0:T(1,128)}) custom-call(bf16[512,1024]{1,0:T(8,128)(2,1)} %add_convert_fusion.1.n_ref, bf16[512,1024]{1,0:T(8,128)(2,1)} %get-tuple-element.122.gd_ref, ...), custom_call_target="tpu_custom_call" | custom-call | flops 35000000512 | bytes 40000000 | tf_op jit(solution)/shard_map/pallas_call | solution.py:263
  274.5 2.2 copy-done.6
  276.6 8.3 %shard_map.350 = f32[512,1024]{1,0:T(8,128)S(1)} custom-call(bf16[512,4096]{1,0:T(8,128)(2,1)S(1)} %copy-done.6, bf16[8,1024,1024]{2,1,0:T(8,128)(2,1)} %all-gather.5.cloned.1.call-done.wh_ref.wp_ref), custom_call_target="tpu_custom_call" | custom-call | flops 8000000000 | bytes 12000000 | tf_op jit(solution)/shard_map/pallas_call | solution.py:240
  288.2 3.3 fusion.43
  299.7 2.0 maximum_select_fusion.2.do_ref
  303.3 3.4 collective-permute-start.6
  309.4 6.1 %collective-permute-start.8 = (bf16[400,512]{1,0:T(8,128)(2,1)S(1)}, bf16[400,512]{1,0:T(8,128)(2,1)S(1)}, u32[]{:S(2)}, u32[]{:S(2)}) collective-permute-start(bf16[400,512]{1,0:T(8,128)(2,1)S(1)} %pad_maximum_fusion.6), channel_id=1, source_target_pairs={{0,4},{1,5},{2,6},{3,7},{4,8},{5,9},{6,10},{7,11},{8,12},{9,13},{1... | collective-permute-start | bytes 1228808 | tf_op jit(solution)/shard_map/ppermute | solution.py:323
  315.6 34.8 %shard_map.351 = bf16[1024,512]{1,0:T(8,128)(2,1)S(1)} custom-call(s32[4]{0:T(128)S(1)} %get-tuple-element.196.lo, s32[4]{0:T(128)S(1)} %get-tuple-element.197.hi, bf16[4096,1536]{1,0:T(8,128)(2,1)} %multiply_convert_fusion.q_ref.k_ref.v_ref, bf16[4096,1536]{1,0:T(8,128)(2,1)} %multiply_convert_fusion.q_ref.k_ref.v_ref, ...), custom_call_target="tpu_custom_call" | custom-call | flops 60000002048 | bytes 8000000 | tf_op jit(solution)/shard_map/pallas_call | solution.py:579
  350.4 9.7 %collective-permute-done.8.g0 = bf16[400,512]{1,0:T(8,128)(2,1)S(1)} collective-permute-done((bf16[400,512]{1,0:T(8,128)(2,1)S(1)}, bf16[400,512]{1,0:T(8,128)(2,1)S(1)}, u32[]{:S(2)}, u32[]{:S(2)}) %collective-permute-start.8) | collective-permute-done | bytes 409632 | tf_op jit(solution)/shard_map/ppermute | solution.py:323
  360.1 21.4 %collective-permute-done.6.g1 = bf16[1120,512]{1,0:T(8,128)(2,1)S(1)} collective-permute-done((bf16[1120,512]{1,0:T(8,128)(2,1)S(1)}, bf16[1120,512]{1,0:T(8,128)(2,1)S(1)}, u32[]{:S(2)}, u32[]{:S(2)}) %collective-permute-start.6) | collective-permute-done | bytes 1146912 | tf_op jit(solution)/shard_map/ppermute | solution.py:323
  381.5 3.9 collective-permute-done.7.g3
  387.7 2.9 fusion.34
  392.5 38.8 %shard_map.352 = (bf16[1024,512]{1,0:T(8,128)(2,1)S(1)}, bf16[1024,512]{1,0:T(8,128)(2,1)S(1)}) custom-call(s32[4]{0:T(128)S(1)} %get-tuple-element.196.lo, s32[4]{0:T(128)S(1)} %get-tuple-element.197.hi, bf16[4096,1536]{1,0:T(8,128)(2,1)} %multiply_convert_fusion.q_ref.k_ref.v_ref, bf16[4096,1536]{1,0:T(8,128)(2,1)} %multiply_convert_fusion.q_ref.k_ref.v_ref, ...), custom_call_target="tpu_custom_call" | custom-call | flops 70000001024 | bytes 8000000 | tf_op jit(solution)/shard_map/pallas_call | solution.py:616
  432.0 6.3 %fusion.98 = (f32[1024]{0:T(1024)S(1)}, f32[1024]{0:T(1024)S(1)}, f32[1024,1024]{1,0:T(8,128)S(1)}) fusion(f32[1024,1024]{1,0:T(8,128)} %fusion.6, bf16[1024,4224]{1,0:T(8,128)(2,1)} %all-gather.3.cloned.1.call-done, s32[]{:T(128)S(6)} %select_n.264, bf16[1024,512]{1,0:T(8,128)(2,1)S(1)} %get-tuple-element.80, ...), kind=kOutput, calls=%fused_computation.296 | convolution fusion | flops 3233806336 | bytes 14688260 | tf_op jit(solution)/shard_map/dot_general | solution.py:35
  438.3 2.7 constant_dynamic-slice_fusion.15
  442.1 7.5 %shard_map.353 = f32[512,1024]{1,0:T(8,128)S(1)} custom-call(bf16[512,4096]{1,0:T(8,128)(2,1)S(1)} %copy-done.5, bf16[8,1024,1024]{2,1,0:T(8,128)(2,1)} %all-gather.5.cloned.1.call-done.wh_ref.wp_ref), custom_call_target="tpu_custom_call" | custom-call | flops 8000000000 | bytes 12000000 | tf_op jit(solution)/shard_map/pallas_call | solution.py:240
  455.9 22.7 %collective-permute-start.14 = (bf16[2,2,64,1024]{3,2,0,1:T(8,128)(2,1)}, bf16[2,2,64,1024]{3,2,0,1:T(8,128)(2,1)}, u32[]{:S(2)}, u32[]{:S(2)}) collective-permute-start(bf16[2,2,64,1024]{3,2,0,1:T(8,128)(2,1)} %dynamic-slice_bitcast_fusion.1), channel_id=1, source_target_pairs={{0,16},{1,17},{2,18},{3,19},{4,20},{5,21},{6,22},{7,23},{8,24},{9,... | collective-permute-start | bytes 1572872 | tf_op jit(solution)/shard_map/ppermute | solution.py:318
  478.6 2.9 fusion.40
  483.2 4.1 collective-permute-start.13
  487.3 2.9 fusion.37
  496.3 7.4 %collective-permute-done.14 = bf16[2,2,64,1024]{3,2,0,1:T(8,128)(2,1)} collective-permute-done((bf16[2,2,64,1024]{3,2,0,1:T(8,128)(2,1)}, bf16[2,2,64,1024]{3,2,0,1:T(8,128)(2,1)}, u32[]{:S(2)}, u32[]{:S(2)}) %collective-permute-start.14) | collective-permute-done | bytes 524320 | tf_op jit(solution)/shard_map/ppermute | solution.py:318
  503.6 6.6 %collective-permute-done.13 = bf16[2,2,2,64,512]{4,3,0,2,1:T(8,128)(2,1)} collective-permute-done((bf16[2,2,2,64,512]{4,3,0,2,1:T(8,128)(2,1)}, bf16[2,2,2,64,512]{4,3,0,2,1:T(8,128)(2,1)}, u32[]{:S(2)}, u32[]{:S(2)}) %collective-permute-start.13) | collective-permute-done | bytes 524320 | tf_op jit(solution)/shard_map/ppermute | solution.py:318
  510.3 7.7 %collective-permute-done.12 = bf16[2,2,2,64,512]{4,3,0,1,2:T(8,128)(2,1)} collective-permute-done((bf16[2,2,2,64,512]{4,3,0,1,2:T(8,128)(2,1)}, bf16[2,2,2,64,512]{4,3,0,1,2:T(8,128)(2,1)}, u32[]{:S(2)}, u32[]{:S(2)}) %collective-permute-start.12) | collective-permute-done | bytes 524320 | tf_op jit(solution)/shard_map/ppermute | solution.py:318
  518.0 2.2 collective-permute-start.20
  523.2 14.5 %collective-permute-start.18 = (bf16[2,2,64,512]{3,2,0,1:T(8,128)(2,1)S(1)}, bf16[2,2,64,512]{3,2,0,1:T(8,128)(2,1)S(1)}, u32[]{:S(2)}, u32[]{:S(2)}) collective-permute-start(bf16[2,2,64,512]{3,2,0,1:T(8,128)(2,1)S(1)} %dynamic-slice_bitcast_fusion.3), channel_id=1, source_target_pairs={{0,8},{1,9},{2,10},{3,11},{4,12},{5,13},{6,14},{7,15},{8,0},{9,1},... | collective-permute-start | bytes 786440 | tf_op jit(solution)/shard_map/ppermute | solution.py:318
  539.0 2.2 fusion.99
  543.0 2.6 collective-permute-done.17
  551.9 2.0 shard_map.354
  553.9 2.8 collective-permute-done.21
  557.1 3.0 collective-permute-start.25
  563.1 2.4 collective-permute-start.28
  (371 shorter events, 97.9 us)
Async XLA Ops:
  7.2 125.2 %all-gather.3.cloned.1.call-start = ((), (), s32[]{:S(2)}) async-start(), calls=%async_computation.1 | async-start | bytes 8921088 | tf_op jit(solution)/shard_map/all_gather | solution.py:423
  15.7 233.2 %all-gather.5.cloned.1.call-start = ((), (), s32[]{:S(2)}) async-start(), calls=%async_computation.2 | async-start | bytes 17301504 | tf_op jit(solution)/shard_map/all_gather | solution.py:424
  19.7 525.9 %reduce-scatter.2.cloned.1.call-start = ((), (), s32[]{:S(2)}) async-start(), calls=%async_computation.3 | async-start | bytes 17301504 | tf_op jit(solution)/shard_map/reduce_scatter | solution.py:551
  21.2 61.1 %collective-permute-start = (bf16[528,1024]{1,0:T(8,128)(2,1)}, bf16[528,1024]{1,0:T(8,128)(2,1)S(1)}, u32[]{:S(2)}, u32[]{:S(2)}) collective-permute-start(bf16[528,1024]{1,0:T(8,128)(2,1)} %get-tuple-element.140), channel_id=1, source_target_pairs={{0,2},{1,3},{2,4},{3,5},{4,6},{5,7},{6,8},{7,9},{8,10},{9,11},{10,... | collective-permute-start | bytes 3244040 | tf_op jit(solution)/shard_map/ppermute | solution.py:323
  26.1 58.1 %collective-permute-start.1 = (bf16[528,1024]{1,0:T(8,128)(2,1)}, bf16[528,1024]{1,0:T(8,128)(2,1)}, u32[]{:S(2)}, u32[]{:S(2)}) collective-permute-start(bf16[528,1024]{1,0:T(8,128)(2,1)} %get-tuple-element.140), channel_id=1, source_target_pairs={{2,0},{3,1},{4,2},{5,3},{6,4},{7,5},{8,6},{9,7},{10,8},{11,9},{12,... | collective-permute-start | bytes 3244040 | tf_op jit(solution)/shard_map/ppermute | solution.py:323
  27.5 15.0 %collective-permute-start.2 = (bf16[368,1024]{1,0:T(8,128)(2,1)S(1)}, bf16[368,1024]{1,0:T(8,128)(2,1)S(1)}, u32[]{:S(2)}, u32[]{:S(2)}) collective-permute-start(bf16[368,1024]{1,0:T(8,128)(2,1)S(1)} %pad_maximum_fusion.4), channel_id=1, source_target_pairs={{4,0},{6,2},{8,4},{10,6},{12,8},{14,10},{16,12},{18,14},{20,16},{2... | collective-permute-start | bytes 2261000 | tf_op jit(solution)/shard_map/ppermute | solution.py:436
  87.6 7.7 %collective-permute-start.3 = (bf16[4,528,1024]{2,1,0:T(8,128)(2,1)}, bf16[4,528,1024]{2,1,0:T(8,128)(2,1)}, u32[]{:S(2)}, u32[]{:S(2)}) collective-permute-start(bf16[4,528,1024]{2,1,0:T(8,128)(2,1)} %pad_maximum_fusion), channel_id=1, source_target_pairs={{0,1},{1,0},{2,3},{3,2},{4,5},{5,4},{6,7},{7,6},{8,9},{9,8},{10,11... | collective-permute-start | bytes 12976136 | tf_op jit(solution)/shard_map/ppermute | solution.py:318
  134.2 56.8 %copy-start.44 = (f32[1,1024]{1,0:T(1,128)}, f32[1,1024]{1,0:T(1,128)S(1)}, u32[]{:S(2)}) copy-start(f32[1,1024]{1,0:T(1,128)S(1)} %get-tuple-element.156) | copy-start | bytes 12292
  134.2 60.0 %copy-start.51 = (f32[1,1024]{1,0:T(1,128)}, f32[1,1024]{1,0:T(1,128)S(1)}, u32[]{:S(2)}) copy-start(f32[1,1024]{1,0:T(1,128)S(1)} %get-tuple-element.159) | copy-start | bytes 12292
  140.1 19.9 %copy-start.21 = (bf16[4096,1024]{1,0:T(8,128)(2,1)}, bf16[4096,1024]{1,0:T(8,128)(2,1)S(1)}, u32[]{:S(2)}) copy-start(bf16[4096,1024]{1,0:T(8,128)(2,1)S(1)} %fusion.5) | copy-start | bytes 25165828
  189.8 111.9 %copy-start.2 = (f32[1024,512]{1,0:T(8,128)}, f32[1024,512]{1,0:T(8,128)S(1)}, u32[]{:S(2)}) copy-start(f32[1024,512]{1,0:T(8,128)S(1)} %get-tuple-element.65.o_ref) | copy-start | bytes 6291460
  190.1 4.1 collective-permute-start.4
  292.4 6.6 %collective-permute-start.5 = (bf16[512,512]{1,0:T(8,128)(2,1)S(1)}, bf16[512,512]{1,0:T(8,128)(2,1)S(1)}, u32[]{:S(2)}, u32[]{:S(2)}) collective-permute-start(bf16[512,512]{1,0:T(8,128)(2,1)S(1)} %get-tuple-element.150), channel_id=1, source_target_pairs={{0,1},{1,0},{2,3},{3,2},{4,5},{5,4},{6,7},{7,6},{8,9},{9,8},{10,11... | collective-permute-start | bytes 1572872 | tf_op jit(solution)/shard_map/ppermute | solution.py:318
  296.4 63.7 %collective-permute-start.10 = (bf16[2,2,2,2,32,1024]{5,4,2,3,0,1:T(8,128)(2,1)}, bf16[2,2,2,2,32,1024]{5,4,2,3,0,1:T(8,128)(2,1)}, u32[]{:S(2)}, u32[]{:S(2)}) collective-permute-start(bf16[2,2,2,2,32,1024]{5,4,2,3,0,1:T(8,128)(2,1)} %bitcast.213), channel_id=1, source_target_pairs={{0,1},{1,0},{2,3},{3,2},{4,5},{5,4},{6,7},{7,6},{8,9},{9,8},{10,11... | collective-permute-start | bytes 3145736 | tf_op jit(solution)/shard_map/ppermute | solution.py:318
  303.3 78.2 %collective-permute-start.6 = (bf16[1120,512]{1,0:T(8,128)(2,1)S(1)}, bf16[1120,512]{1,0:T(8,128)(2,1)S(1)}, u32[]{:S(2)}, u32[]{:S(2)}) collective-permute-start(bf16[1120,512]{1,0:T(8,128)(2,1)S(1)} %pad_maximum_fusion.2.g2), channel_id=1, source_target_pairs={{0,2},{1,3},{2,4},{3,5},{4,6},{5,7},{6,8},{7,9},{8,10},{9,11},{10,... | collective-permute-start | bytes 3440648 | tf_op jit(solution)/shard_map/ppermute | solution.py:323
  306.8 78.7 %collective-permute-start.7 = (bf16[1120,512]{1,0:T(8,128)(2,1)S(1)}, bf16[1120,512]{1,0:T(8,128)(2,1)S(1)}, u32[]{:S(2)}, u32[]{:S(2)}) collective-permute-start(bf16[1120,512]{1,0:T(8,128)(2,1)S(1)} %pad_maximum_fusion.2.g2), channel_id=1, source_target_pairs={{2,0},{3,1},{4,2},{5,3},{6,4},{7,5},{8,6},{9,7},{10,8},{11,9},{12,... | collective-permute-start | bytes 3440648 | tf_op jit(solution)/shard_map/ppermute | solution.py:323
  308.1 42.3 %collective-permute-start.9 = (bf16[400,512]{1,0:T(8,128)(2,1)S(1)}, bf16[400,512]{1,0:T(8,128)(2,1)S(1)}, u32[]{:S(2)}, u32[]{:S(2)}) collective-permute-start(bf16[400,512]{1,0:T(8,128)(2,1)S(1)} %pad_maximum_fusion.7), channel_id=1, source_target_pairs={{4,0},{5,1},{6,2},{7,3},{8,4},{9,5},{10,6},{11,7},{12,8},{13,9},{1... | collective-permute-start | bytes 1228808 | tf_op jit(solution)/shard_map/ppermute | solution.py:323
  309.4 50.7 %collective-permute-start.8 = (bf16[400,512]{1,0:T(8,128)(2,1)S(1)}, bf16[400,512]{1,0:T(8,128)(2,1)S(1)}, u32[]{:S(2)}, u32[]{:S(2)}) collective-permute-start(bf16[400,512]{1,0:T(8,128)(2,1)S(1)} %pad_maximum_fusion.6), channel_id=1, source_target_pairs={{0,4},{1,5},{2,6},{3,7},{4,8},{5,9},{6,10},{7,11},{8,12},{9,13},{1... | collective-permute-start | bytes 1228808 | tf_op jit(solution)/shard_map/ppermute | solution.py:323
  350.4 35.2 %copy-start.24 = (bf16[2,2,2,2,1,32,1024]{6,5,4,3,2,1,0:T(8,128)(2,1)S(1)}, bf16[2,2,2,2,1,32,1024]{6,5,4,3,2,1,0:T(8,128)(2,1)}, u32[]{:S(2)}) copy-start(bf16[2,2,2,2,1,32,1024]{6,5,4,3,2,1,0:T(8,128)(2,1)} %get-tuple-element.137) | copy-start | bytes 3145732
  392.1 40.0 %collective-permute-start.11 = (bf16[2,2,2,64,1024]{4,3,1,2,0:T(8,128)(2,1)}, bf16[2,2,2,64,1024]{4,3,1,2,0:T(8,128)(2,1)}, u32[]{:S(2)}, u32[]{:S(2)}) collective-permute-start(bf16[2,2,2,64,1024]{4,3,1,2,0:T(8,128)(2,1)} %dynamic-slice_bitcast_fusion), channel_id=1, source_target_pairs={{0,8},{1,9},{2,10},{3,11},{4,12},{5,13},{6,14},{7,15},{8,0},{9,1},... | collective-permute-start | bytes 3145736 | tf_op jit(solution)/shard_map/ppermute | solution.py:318
  441.1 76.8 %collective-permute-start.16 = (f32[512,1024]{1,0:T(8,128)}, f32[512,1024]{1,0:T(8,128)}, u32[]{:S(2)}, u32[]{:S(2)}) collective-permute-start(f32[512,1024]{1,0:T(8,128)} %get-tuple-element.131), channel_id=1, source_target_pairs={{0,1},{1,0},{2,3},{3,2},{4,5},{5,4},{6,7},{7,6},{8,9},{9,8},{10,11... | collective-permute-start | bytes 6291464 | tf_op jit(solution)/shard_map/ppermute | solution.py:318
  455.0 26.5 %copy-start.27 = (bf16[2,2,2,64,1024]{4,3,1,2,0:T(8,128)(2,1)}, bf16[2,2,2,64,1024]{4,3,1,2,0:T(8,128)(2,1)S(1)}, u32[]{:S(2)}) copy-start(bf16[2,2,2,64,1024]{4,3,1,2,0:T(8,128)(2,1)S(1)} %fusion.19) | copy-start | bytes 3145732
  455.9 47.8 %collective-permute-start.14 = (bf16[2,2,64,1024]{3,2,0,1:T(8,128)(2,1)}, bf16[2,2,64,1024]{3,2,0,1:T(8,128)(2,1)}, u32[]{:S(2)}, u32[]{:S(2)}) collective-permute-start(bf16[2,2,64,1024]{3,2,0,1:T(8,128)(2,1)} %dynamic-slice_bitcast_fusion.1), channel_id=1, source_target_pairs={{0,16},{1,17},{2,18},{3,19},{4,20},{5,21},{6,22},{7,23},{8,24},{9,... | collective-permute-start | bytes 1572872 | tf_op jit(solution)/shard_map/ppermute | solution.py:318
  483.2 27.1 %collective-permute-start.13 = (bf16[2,2,2,64,512]{4,3,0,2,1:T(8,128)(2,1)}, bf16[2,2,2,64,512]{4,3,0,2,1:T(8,128)(2,1)}, u32[]{:S(2)}, u32[]{:S(2)}) collective-permute-start(bf16[2,2,2,64,512]{4,3,0,2,1:T(8,128)(2,1)} %bitcast.215), channel_id=1, source_target_pairs={{0,4},{1,5},{2,6},{3,7},{4,0},{5,1},{6,2},{7,3},{8,12},{9,13},{10,... | collective-permute-start | bytes 1572872 | tf_op jit(solution)/shard_map/ppermute | solution.py:318
  491.0 29.2 %copy-start.28 = (bf16[2,2,2,64,1024]{4,3,1,2,0:T(8,128)(2,1)S(1)}, bf16[2,2,2,64,1024]{4,3,1,2,0:T(8,128)(2,1)}, u32[]{:S(2)}) copy-start(bf16[2,2,2,64,1024]{4,3,1,2,0:T(8,128)(2,1)} %copy-done.27) | copy-start | bytes 3145732
  491.9 26.0 %collective-permute-start.12 = (bf16[2,2,2,64,512]{4,3,0,1,2:T(8,128)(2,1)}, bf16[2,2,2,64,512]{4,3,0,1,2:T(8,128)(2,1)}, u32[]{:S(2)}, u32[]{:S(2)}) collective-permute-start(bf16[2,2,2,64,512]{4,3,0,1,2:T(8,128)(2,1)} %bitcast.216), channel_id=1, source_target_pairs={{0,2},{1,3},{2,0},{3,1},{4,6},{5,7},{6,4},{7,5},{8,10},{9,11},{10,... | collective-permute-start | bytes 1572872 | tf_op jit(solution)/shard_map/ppermute | solution.py:318
  493.9 27.9 %copy-start.30 = (bf16[2,2,1,2,64,512]{5,4,3,2,1,0:T(8,128)(2,1)S(1)}, bf16[2,2,1,2,64,512]{5,4,3,2,1,0:T(8,128)(2,1)}, u32[]{:S(2)}) copy-start(bf16[2,2,1,2,64,512]{5,4,3,2,1,0:T(8,128)(2,1)} %get-tuple-element.141) | copy-start | bytes 1572868
  494.8 42.9 %copy-start.31 = (bf16[2,2,2,1,64,512]{5,4,3,2,1,0:T(8,128)(2,1)S(1)}, bf16[2,2,2,1,64,512]{5,4,3,2,1,0:T(8,128)(2,1)}, u32[]{:S(2)}) copy-start(bf16[2,2,2,1,64,512]{5,4,3,2,1,0:T(8,128)(2,1)} %get-tuple-element.143) | copy-start | bytes 1572868
  495.0 1.3 collective-permute-start.15
  518.0 25.0 %collective-permute-start.20 = (f32[2,2,2,1,512]{4,3,2,1,0:T(1,128)S(1)}, f32[2,2,2,1,512]{4,3,2,1,0:T(1,128)S(1)}, u32[]{:S(2)}, u32[]{:S(2)}) collective-permute-start(f32[2,2,2,1,512]{4,3,2,1,0:T(1,128)S(1)} %dynamic-slice_bitcast_fusion.11), channel_id=1, source_target_pairs={{0,2},{1,3},{2,0},{3,1},{4,6},{5,7},{6,4},{7,5},{8,10},{9,11},{10,... | collective-permute-start | bytes 49160 | tf_op jit(solution)/shard_map/ppermute | solution.py:318
  520.2 18.7 %copy-start.18 = (f32[512,1024]{1,0:T(8,128)S(1)}, f32[512,1024]{1,0:T(8,128)}, u32[]{:S(2)}) copy-start(f32[512,1024]{1,0:T(8,128)} %get-tuple-element.92) | copy-start | bytes 6291460
  521.6 17.2 %copy-start.32 = (bf16[2,2,64,1024]{3,2,0,1:T(8,128)(2,1)}, bf16[2,2,64,1024]{3,2,0,1:T(8,128)(2,1)S(1)}, u32[]{:S(2)}) copy-start(bf16[2,2,64,1024]{3,2,0,1:T(8,128)(2,1)S(1)} %fusion.53) | copy-start | bytes 1572868
  521.7 21.3 %collective-permute-start.19 = (bf16[2,64,1024]{2,1,0:T(8,128)(2,1)S(1)}, bf16[2,64,1024]{2,1,0:T(8,128)(2,1)S(1)}, u32[]{:S(2)}, u32[]{:S(2)}) collective-permute-start(bf16[2,64,1024]{2,1,0:T(8,128)(2,1)S(1)} %dynamic-slice_bitcast_fusion.2), channel_id=1, source_target_pairs={{0,2},{1,3},{2,0},{3,1},{4,6},{5,7},{6,4},{7,5},{8,10},{9,11},{10,... | collective-permute-start | bytes 786440 | tf_op jit(solution)/shard_map/ppermute | solution.py:318
  521.8 17.2 %copy-start.47 = (f32[1,1024]{1,0:T(1,128)S(1)}, f32[1,1024]{1,0:T(1,128)}, u32[]{:S(2)}) copy-start(f32[1,1024]{1,0:T(1,128)} %copy-done.46) | copy-start | bytes 12292
  521.8 17.2 %copy-start.15 = (f32[1024,1024]{1,0:T(8,128)S(1)}, f32[1024,1024]{1,0:T(8,128)}, u32[]{:S(2)}) copy-start(f32[1024,1024]{1,0:T(8,128)} %fusion.6) | copy-start | bytes 12582916
  523.2 19.8 %collective-permute-start.18 = (bf16[2,2,64,512]{3,2,0,1:T(8,128)(2,1)S(1)}, bf16[2,2,64,512]{3,2,0,1:T(8,128)(2,1)S(1)}, u32[]{:S(2)}, u32[]{:S(2)}) collective-permute-start(bf16[2,2,64,512]{3,2,0,1:T(8,128)(2,1)S(1)} %dynamic-slice_bitcast_fusion.3), channel_id=1, source_target_pairs={{0,8},{1,9},{2,10},{3,11},{4,12},{5,13},{6,14},{7,15},{8,0},{9,1},... | collective-permute-start | bytes 786440 | tf_op jit(solution)/shard_map/ppermute | solution.py:318
  538.9 6.8 %collective-permute-start.17 = (bf16[2,2,64,512]{3,2,0,1:T(8,128)(2,1)S(1)}, bf16[2,2,64,512]{3,2,0,1:T(8,128)(2,1)S(1)}, u32[]{:S(2)}, u32[]{:S(2)}) collective-permute-start(bf16[2,2,64,512]{3,2,0,1:T(8,128)(2,1)S(1)} %dynamic-slice_bitcast_fusion.4), channel_id=1, source_target_pairs={{0,4},{1,5},{2,6},{3,7},{4,0},{5,1},{6,2},{7,3},{8,12},{9,13},{10,... | collective-permute-start | bytes 786440 | tf_op jit(solution)/shard_map/ppermute | solution.py:318
  545.7 8.2 %collective-permute-start.24 = (f32[2,2,1,512]{3,2,1,0:T(1,128)S(1)}, f32[2,2,1,512]{3,2,1,0:T(1,128)S(1)}, u32[]{:S(2)}, u32[]{:S(2)}) collective-permute-start(f32[2,2,1,512]{3,2,1,0:T(1,128)S(1)} %fusion.77), channel_id=1, source_target_pairs={{0,4},{1,5},{2,6},{3,7},{4,0},{5,1},{6,2},{7,3},{8,12},{9,13},{10,... | collective-permute-start | bytes 24584 | tf_op jit(solution)/shard_map/ppermute | solution.py:318
  546.1 7.8 %collective-permute-start.23 = (bf16[64,1024]{1,0:T(8,128)(2,1)S(1)}, bf16[64,1024]{1,0:T(8,128)(2,1)S(1)}, u32[]{:S(2)}, u32[]{:S(2)}) collective-permute-start(bf16[64,1024]{1,0:T(8,128)(2,1)S(1)} %dynamic-slice_bitcast_fusion.5), channel_id=1, source_target_pairs={{0,4},{1,5},{2,6},{3,7},{4,0},{5,1},{6,2},{7,3},{8,12},{9,13},{10,... | collective-permute-start | bytes 393224 | tf_op jit(solution)/shard_map/ppermute | solution.py:318
  548.1 5.9 %collective-permute-start.22 = (bf16[2,64,512]{2,1,0:T(8,128)(2,1)S(1)}, bf16[2,64,512]{2,1,0:T(8,128)(2,1)S(1)}, u32[]{:S(2)}, u32[]{:S(2)}) collective-permute-start(bf16[2,64,512]{2,1,0:T(8,128)(2,1)S(1)} %dynamic-slice_bitcast_fusion.6), channel_id=1, source_target_pairs={{0,2},{1,3},{2,0},{3,1},{4,6},{5,7},{6,4},{7,5},{8,10},{9,11},{10,... | collective-permute-start | bytes 393224 | tf_op jit(solution)/shard_map/ppermute | solution.py:318
  550.7 6.0 %collective-permute-start.21 = (bf16[2,64,512]{2,1,0:T(8,128)(2,1)S(1)}, bf16[2,64,512]{2,1,0:T(8,128)(2,1)S(1)}, u32[]{:S(2)}, u32[]{:S(2)}) collective-permute-start(bf16[2,64,512]{2,1,0:T(8,128)(2,1)S(1)} %dynamic-slice_bitcast_fusion.7), channel_id=1, source_target_pairs={{0,8},{1,9},{2,10},{3,11},{4,12},{5,13},{6,14},{7,15},{8,0},{9,1},... | collective-permute-start | bytes 393224 | tf_op jit(solution)/shard_map/ppermute | solution.py:318
  556.8 5.3 collective-permute-start.27
  557.0 5.2 collective-permute-start.26
  557.1 5.8 %collective-permute-start.25 = (bf16[64,512]{1,0:T(8,128)(2,1)S(1)}, bf16[64,512]{1,0:T(8,128)(2,1)S(1)}, u32[]{:S(2)}, u32[]{:S(2)}) collective-permute-start(bf16[64,512]{1,0:T(8,128)(2,1)S(1)} %dynamic-slice_bitcast_fusion.9), channel_id=1, source_target_pairs={{0,16},{1,17},{2,18},{3,19},{4,20},{5,21},{6,22},{7,23},{8,24},{9,... | collective-permute-start | bytes 196616 | tf_op jit(solution)/shard_map/ppermute | solution.py:318
  560.1 1.3 collective-permute-start.29
  562.9 5.9 %collective-permute-start.31 = (bf16[32,512]{1,0:T(8,128)(2,1)S(1)}, bf16[32,512]{1,0:T(8,128)(2,1)S(1)}, u32[]{:S(2)}, u32[]{:S(2)}) collective-permute-start(bf16[32,512]{1,0:T(8,128)(2,1)S(1)} %get-tuple-element.172), channel_id=1, source_target_pairs={{0,1},{1,0},{2,3},{3,2},{4,5},{5,4},{6,7},{7,6},{8,9},{9,8},{10,11... | collective-permute-start | bytes 98312 | tf_op jit(solution)/shard_map/ppermute | solution.py:318
  563.1 4.5 collective-permute-start.28
  565.5 4.0 collective-permute-start.30
  (50 other events, 211.5 us)
Sparse Core Ops, SparseCore 0:
  15.8 116.5 all-gather.2
  135.9 112.9 all-gather.4
  273.8 254.8 reduce-scatter.1
